TPU v7x, 32 devices: a whole 2x2x4 slice. The times are simulated.
32 devices in a mesh: tower: 8 (over z, x), dev: 4 (over y, core).
Axes of the slice: x: 2, y: 2, z: 4, core: 2. Of those that a mesh axis runs over, the one named last changes fastest.
Arguments:
- ids: int32 [8, 16, 512, 32], P('tower', 'dev'), may hold values from 0 to 511
- tables: bfloat16 [8, 16, 512, 128], P('tower', 'dev'), may hold values from -1 to 1
- order: int32 [512], replicated, may hold values from 0 to 511, each once
- w_first: bfloat16 [8, 2048, 1024], P('tower', 'dev'), may hold values from -0.125 to 0.125
- w_second: bfloat16 [8, 1024, 512], P('tower'), may hold values from -0.1875 to 0.1875
- w_head: bfloat16 [4096, 128], replicated, may hold values from -0.09375 to 0.09375
- w_interact: float32 [64, 128], replicated, may hold values from -0.375 to 0.375
Outputs:
- scores: float32 [4, 128, 128], P('dev', 'tower')
Inputs may be any that keep to these rules, and one draw needn't show every extreme that they name: order is a permutation of the batch rows 0 to 511.
All inputs are finite; a program needn't handle non-finite values.
Results may differ from a plain program's by a relative error of at most 0.0023.
Values may be sent and summed in bfloat16 or wider, within the bound.
No kernel may reach another device: no remote copies, remote signals or barrier semaphores. Data moves between devices by JAX's collectives and lax.ppermute only.
A program may use at most 64 MiB of HBM per device.

v0:
```python
import math

import jax
import jax.numpy as jnp
from jax import lax
from jax.sharding import PartitionSpec as P


def pool_feature(feature_ids, table):
    samples = feature_ids.shape[0]
    active = table.shape[0]
    block = math.gcd(samples, 512)
    blocked = feature_ids.reshape(samples // block, block, feature_ids.shape[1])
    positions = lax.broadcasted_iota(jnp.int32, (1, 1, active), 2)

    def pool_block(block_ids):
        tally = jnp.sum((block_ids[:, :, None] == positions).astype(jnp.int32), axis=1)
        return jnp.dot(
            tally.astype(jnp.bfloat16), table, preferred_element_type=jnp.float32
        ).astype(jnp.bfloat16)

    pooled = lax.map(pool_block, blocked)
    return pooled.reshape(samples, table.shape[1])


def on_device(ids, tables, order, w_first, w_second, w_head, w_interact):
    feature_local = tables.shape[1]
    towers = lax.axis_size("tower")
    devices = lax.axis_size("dev")
    samples = ids.shape[2]
    my_rows = samples // devices
    pieces = []
    for feature in range(feature_local):
        pieces.append(pool_feature(ids[0, feature], tables[0, feature]))
    features = jnp.take(jnp.concatenate(pieces, axis=1), order, axis=0)
    received = lax.all_to_all(features, "dev", split_axis=0, concat_axis=1, tiled=True)
    preact = jnp.dot(
        received,
        lax.all_gather(w_first[0], "dev", axis=0, tiled=True),
        preferred_element_type=jnp.float32,
    )
    hidden = jnp.maximum(preact, 0.0).astype(jnp.bfloat16)
    outputs = jnp.dot(hidden, w_second[0], preferred_element_type=jnp.float32).astype(jnp.bfloat16)
    width = outputs.shape[1]
    share = my_rows // towers
    gathered = lax.all_to_all(
        outputs.reshape(1, towers, share, width), "tower", split_axis=1, concat_axis=0, tiled=True
    )[:, 0]
    amount = gathered.shape[1]
    joined = jnp.transpose(gathered, (1, 0, 2)).reshape(amount, towers * width)
    head = jnp.dot(joined, w_head, preferred_element_type=jnp.float32)
    widened = gathered.astype(jnp.float32)
    products = jnp.einsum(
        "tmz,smz->mts", widened, widened, precision=lax.Precision.HIGHEST
    ) / math.sqrt(width)
    interact_term = jnp.dot(
        products.reshape(amount, towers * towers), w_interact, precision=lax.Precision.HIGHEST
    )
    scored = head + interact_term
    return scored[None]


def solution(mesh):
    return jax.shard_map(
        on_device,
        mesh=mesh,
        in_specs=(
            P("tower", "dev", None, None),
            P("tower", "dev", None, None),
            P(),
            P("tower", "dev", None),
            P("tower", None, None),
            P(),
            P(),
        ),
        out_specs=P("dev", "tower", None),
        check_vma=False,
    )
```

profile of v0, /device:TPU:0, one launch (start us, length us, event | category | flops | bytes accessed | tf_op | source)
XLA Modules:
  0.0 94.6 jit_solution(2863527872841962671)
XLA Ops:
  6.5 0.0 copy-start
  6.5 0.0 copy-start.2
  6.5 0.0 all-gather.3.cloned.1.call-start
  6.5 0.7 all-gather.3.cloned.1.call-update
  7.3 1.0 %slice_bitcast_fusion.3 = (s32[512,32]{0,1:T(8,128)S(1)}, s32[512,32]{0,1:T(8,128)S(1)}, s32[512,32]{0,1:T(8,128)S(1)}, s32[512,32]{0,1:T(8,128)S(1)}) fusion(s32[1,4,512,32]{2,3,1,0:T(8,128)} %param.7), kind=kLoop, calls=%fused_computation.42 | loop fusion | bytes 524288 | tf_op jit(solution)/shard_map/while/body/eval_jaxpr/eq | solution.py:17
  8.2 0.1 copy.34
  8.3 0.1 copy.33
  8.5 0.1 copy.32
  8.6 0.1 copy.31
  8.8 11.1 %convert_reduce_fusion = s32[512,512]{1,0:T(8,128)S(1)} fusion(s32[512,32]{1,0:T(8,128)S(1)} %copy.34), kind=kLoop, calls=%fused_computation.1 | loop fusion | flops 24903680 | bytes 1114112 | tf_op jit(solution)/shard_map/while/body/eval_jaxpr/reduce_sum | solution.py:17
  19.9 0.0 copy-done.2
  19.9 0.3 convolution_convert_fusion
  20.2 11.1 %convert_reduce_fusion.1 = s32[512,512]{1,0:T(8,128)S(1)} fusion(s32[512,32]{1,0:T(8,128)S(1)} %copy.33), kind=kLoop, calls=%fused_computation.3 | loop fusion | flops 24903680 | bytes 1114112 | tf_op jit(solution)/shard_map/while/body/eval_jaxpr/reduce_sum | solution.py:17
  31.4 0.0 copy-start.4
  31.4 0.3 convolution_convert_fusion.1
  31.7 11.1 %convert_reduce_fusion.2 = s32[512,512]{1,0:T(8,128)S(1)} fusion(s32[512,32]{1,0:T(8,128)S(1)} %copy.32), kind=kLoop, calls=%fused_computation.5 | loop fusion | flops 24903680 | bytes 1114112 | tf_op jit(solution)/shard_map/while/body/eval_jaxpr/reduce_sum | solution.py:17
  42.8 0.3 convolution_convert_fusion.2
  43.2 11.1 %convert_reduce_fusion.3 = s32[512,512]{1,0:T(8,128)S(1)} fusion(s32[512,32]{1,0:T(8,128)S(1)} %copy.31), kind=kLoop, calls=%fused_computation.7 | loop fusion | flops 24903680 | bytes 1114112 | tf_op jit(solution)/shard_map/while/body/eval_jaxpr/reduce_sum | solution.py:17
  54.3 0.3 convolution_convert_fusion.3
  54.7 0.2 copy.35
  54.9 0.0 copy-done.4
  54.9 2.0 %gather_fusion = bf16[512,512]{1,0:T(8,128)(2,1)S(1)} fusion(bf16[512,512]{1,0:T(8,128)(2,1)S(1)} %copy.35, s32[1024]{0:T(1024)S(1)} %pad_clamp_fusion), kind=kCustom, calls=%fused_computation | custom fusion | bytes 1050624 | tf_op jit(solution)/shard_map/jit(_take)/gather | solution.py:35
  56.9 0.3 copy.36
  57.2 0.0 copy-start.1
  57.2 0.1 broadcast_select_fusion
  57.3 13.0 %all_to_all.25 = bf16[4,128,512]{1,2,0:T(8,128)(2,1)S(1)} all-to-all(bf16[4,128,512]{1,2,0:T(8,128)(2,1)S(1)} %broadcast_select_fusion), channel_id=1, replica_groups=mesh['tower'=8,'dev'=4] {'dev'}, dimensions={0} | all-to-all | bytes 1048576 | tf_op jit(solution)/shard_map/all_to_all | solution.py:36
  70.3 0.0 copy-start.3
  70.3 0.0 all-gather.3.cloned.1.call-done
  70.3 0.0 copy-done
  70.3 3.1 %fusion.11 = bf16[128,512]{1,0:T(8,128)(2,1)S(1)} fusion(bf16[128,2048]{0,1:T(8,128)(2,1)S(1)} %bitcast.60, bf16[1,2048,1024]{2,1,0:T(8,128)(2,1)} %all-gather.3.cloned.1.call-done, bf16[1,1024,512]{2,1,0:T(8,128)(2,1)S(1)} %copy-done), kind=kOutput, calls=%fused_computation.18 | convolution fusion | flops 671416320 | bytes 5898240 | tf_op jit(solution)/shard_map/dot_general | solution.py:43
  73.4 12.9 %all_to_all.26 = bf16[1,8,16,512]{3,2,0,1:T(8,128)(2,1)S(1)} all-to-all(bf16[1,8,16,512]{3,2,0,1:T(8,128)(2,1)S(1)} %bitcast.63), channel_id=1, replica_groups=mesh['tower'=8,'dev'=4] {'tower'}, dimensions={1} | all-to-all | bytes 262144 | tf_op jit(solution)/shard_map/all_to_all | solution.py:46
  86.4 0.2 convolution_multiply_fusion
  86.6 0.1 copy.39
  86.7 0.0 copy-done.1
  86.7 0.2 fusion.33
  86.9 0.0 copy-done.3
  86.9 0.8 fusion.14
  (5 shorter events, 0.1 us)
Async XLA Ops:
  6.5 63.7 %copy-start = (bf16[1,1024,512]{2,1,0:T(8,128)(2,1)S(1)}, bf16[1,1024,512]{2,1,0:T(8,128)(2,1)}, u32[]{:S(2)}) copy-start(bf16[1,1024,512]{2,1,0:T(8,128)(2,1)} %param.11) | copy-start | bytes 3145732
  6.5 13.4 %copy-start.2 = (bf16[1,4,512,128]{3,2,1,0:T(8,128)(2,1)S(1)}, bf16[1,4,512,128]{3,2,1,0:T(8,128)(2,1)}, u32[]{:S(2)}) copy-start(bf16[1,4,512,128]{3,2,1,0:T(8,128)(2,1)} %param.8) | copy-start | bytes 1572868
  6.5 63.7 %all-gather.3.cloned.1.call-start = ((), (), s32[]{:S(2)}) async-start(), calls=%async_computation.2 | async-start | bytes 5242880 | tf_op jit(solution)/shard_map/all_gather | solution.py:39
  31.4 23.5 %copy-start.4 = (s32[512]{0:T(512)S(1)}, s32[512]{0:T(512)}, u32[]{:S(2)}) copy-start(s32[512]{0:T(512)} %param.9) | copy-start | bytes 6148
  57.2 29.5 %copy-start.1 = (bf16[4096,128]{1,0:T(8,128)(2,1)S(1)}, bf16[4096,128]{1,0:T(8,128)(2,1)}, u32[]{:S(2)}) copy-start(bf16[4096,128]{1,0:T(8,128)(2,1)} %param.12) | copy-start | bytes 3145732
  70.3 16.7 %copy-start.3 = (f32[64,128]{1,0:T(8,128)S(1)}, f32[64,128]{1,0:T(8,128)}, u32[]{:S(2)}) copy-start(f32[64,128]{1,0:T(8,128)} %param.13) | copy-start | bytes 98308
Sparse Core Ops, SparseCore 0:
  8.9 37.1 all-gather.2
where the time goes:
time: 94.9 us; the launch traced here: 94.6 us
  other arithmetic  44.6 us (47%)
  blocking collectives  26 us (27%)
  between operations  13.6 us (14%)
  matrix products  5.69 us (6%)
  local copies, waits for them, and re-layouts  4.03 us (4%)
    reduce_sum x4, other arithmetic, pool_block(): jnp.sum((block_ids[:, :, None] == positions).astype(jnp.int32), axis=1)  44.5 us
    all_to_all x1, blocking collectives, on_device(): lax.all_to_all(features, 'dev', split_axis=0, concat_axis=1, tiled=True)  13 us
    all_to_all x1, blocking collectives, on_device(): lax.all_to_all(outputs.reshape(1, towers, share, width), 'tower', split_a...  12.9 us
    dot_general x1, matrix products, on_device(): jnp.dot(hidden, w_second[0], preferred_element_type=jnp.float32)  3.14 us
    gather x2, local copies, waits for them, and re-layouts, on_device(): features = jnp.take(jnp.concatenate(pieces, axis=1), order, axis=0)  2.24 us
  transfers between devices with their start and end apart: 1, of which 0 were waited for; matrix products, arithmetic and copies ran while one was open for 53% of the time, Pallas kernels for 0%

commit v1 on v0

v1 whole, which is shorter than its diff:
```python
import math

import jax
import jax.numpy as jnp
from jax import lax
from jax.experimental import pallas as pl
from jax.experimental.pallas import tpu as pltpu
from jax.sharding import PartitionSpec as P

FIELDS = 8
FIELD_MAX = 15
EVEN_FIELDS = 0x0F0F0F0F


def select_ids(ids, order_row, residues):
    feats, bag, samples = ids.shape
    rows = order_row.shape[1]
    shift = residues.bit_length() - 1
    pick = lax.broadcasted_iota(jnp.int32, (samples, rows), 0) == order_row
    pick = jnp.where(pick, 1.0, 0.0).astype(jnp.bfloat16)
    flat = ids.reshape(feats * bag, samples)
    low = (flat & (residues - 1)).astype(jnp.float32).astype(jnp.bfloat16)
    high = (flat >> shift).astype(jnp.float32).astype(jnp.bfloat16)
    low = jnp.dot(low, pick, preferred_element_type=jnp.float32)
    high = jnp.dot(high, pick, preferred_element_type=jnp.float32)
    return low.astype(jnp.int32), jnp.left_shift(1, 4 * high.astype(jnp.int32))


def pool_feature(residue_ref, weight_ref, base, bag, table):
    residues = table.shape[0] // FIELDS
    spots = lax.broadcasted_iota(jnp.int32, (residues, residue_ref.shape[1]), 0)
    even, odd = None, None
    for first in range(0, bag, FIELD_MAX):
        tally = None
        for at in range(base + first, base + min(first + FIELD_MAX, bag)):
            hit = jnp.where(
                residue_ref[pl.ds(at, 1), :] == spots, weight_ref[pl.ds(at, 1), :], 0
            )
            tally = hit if tally is None else tally + hit
        low, high = tally & EVEN_FIELDS, (tally >> 4) & EVEN_FIELDS
        even, odd = (low, high) if even is None else (even + low, odd + high)
    words = jnp.concatenate([even, odd], axis=0).T
    counts = jnp.concatenate(
        [
            ((words >> (8 * place)) & 255).astype(jnp.float32).astype(jnp.bfloat16)
            for place in range(FIELDS // 2)
        ],
        axis=1,
    )
    return jnp.dot(counts, table, preferred_element_type=jnp.float32).astype(jnp.bfloat16)


def pool_kernel(offsets, ids_ref, tables_ref, order_ref, out_ref, residue_ref, weight_ref):
    feats, bag, samples = ids_ref.shape
    active, emb = tables_ref.shape[1:]
    rows = order_ref.shape[1]
    me = lax.axis_index("dev")
    devices = order_ref.shape[0]
    for block, offset in enumerate(offsets):
        target = lax.rem(me + 2 * offset, devices)
        residue_ref[...], weight_ref[...] = select_ids(
            ids_ref[...], order_ref[pl.ds(target, 1), :], active // FIELDS
        )
        for feature in range(feats):
            out_ref[block * rows : (block + 1) * rows, feature * emb : (feature + 1) * emb] = (
                pool_feature(residue_ref, weight_ref, feature * bag, bag, tables_ref[feature])
            )


def pool(offsets, ids, tables, order):
    feats, bag, samples = ids.shape
    rows = order.shape[1]
    emb = tables.shape[2]
    count = len(offsets) * rows
    return pl.pallas_call(
        lambda *refs: pool_kernel(offsets, *refs),
        out_shape=jax.ShapeDtypeStruct((count, feats * emb), jnp.bfloat16),
        in_specs=[pl.BlockSpec(memory_space=pltpu.VMEM)] * 3,
        out_specs=pl.BlockSpec(memory_space=pltpu.VMEM),
        scratch_shapes=[pltpu.VMEM((feats * bag, rows), jnp.int32)] * 2,
        compiler_params=pltpu.CompilerParams(vmem_limit_bytes=32 * 1024 * 1024),
        cost_estimate=pl.CostEstimate(
            flops=2 * count * feats * emb * tables.shape[1] * 4,
            bytes_accessed=4 * ids.size + 2 * tables.size,
            transcendentals=0,
        ),
    )(ids, tables, order)


def matmul(left, right):
    return jnp.dot(left, right, preferred_element_type=jnp.float32)


def on_device(ids, tables, order, w_first, w_second, w_head, w_interact):
    towers = lax.axis_size("tower")
    devices = lax.axis_size("dev")
    samples = ids.shape[2]
    my_rows = samples // devices
    chips = devices // 2
    order = order.reshape(devices, my_rows)
    ids = jnp.swapaxes(ids[0], 1, 2)
    tables, w_first = tables[0], w_first[0]

    core_swap = [(i, i ^ 1) for i in range(devices)]
    ids_other = lax.ppermute(ids, "dev", core_swap)
    tables_other = lax.ppermute(tables, "dev", core_swap)
    w_other = lax.ppermute(w_first, "dev", core_swap)

    away = tuple(range(1, chips))
    mine = pool(away, ids, tables, order)
    other = pool(away, ids_other, tables_other, order)
    partial = (matmul(mine, w_first) + matmul(other, w_other)).astype(jnp.bfloat16)
    received = []
    for k in away:
        received.append(
            lax.ppermute(
                partial[(k - 1) * my_rows : k * my_rows],
                "dev",
                [(i, (i + 2 * k) % devices) for i in range(devices)],
            )
        )
    mine = pool((0,), ids, tables, order)
    other = pool((0,), ids_other, tables_other, order)
    preact = matmul(mine, w_first) + matmul(other, w_other)
    for part in received:
        preact = preact + part.astype(jnp.float32)

    hidden = jnp.maximum(preact, 0.0).astype(jnp.bfloat16)
    outputs = jnp.dot(hidden, w_second[0], preferred_element_type=jnp.float32).astype(jnp.bfloat16)
    width = outputs.shape[1]
    share = my_rows // towers
    gathered = lax.all_to_all(
        outputs.reshape(1, towers, share, width), "tower", split_axis=1, concat_axis=0, tiled=True
    )[:, 0]
    amount = gathered.shape[1]
    joined = jnp.transpose(gathered, (1, 0, 2)).reshape(amount, towers * width)
    head = jnp.dot(joined, w_head, preferred_element_type=jnp.float32)
    widened = gathered.astype(jnp.float32)
    products = jnp.einsum(
        "tmz,smz->mts", widened, widened, precision=lax.Precision.HIGHEST
    ) / math.sqrt(width)
    interact_term = jnp.dot(
        products.reshape(amount, towers * towers), w_interact, precision=lax.Precision.HIGHEST
    )
    scored = head + interact_term
    return scored[None]


def solution(mesh):
    return jax.shard_map(
        on_device,
        mesh=mesh,
        in_specs=(
            P("tower", "dev", None, None),
            P("tower", "dev", None, None),
            P(),
            P("tower", "dev", None),
            P("tower", None, None),
            P(),
            P(),
        ),
        out_specs=P("dev", "tower", None),
        check_vma=False,
    )
```

time: 94.9 us -> 33.4 us (0.35)
  other arithmetic: 44.6 us -> 0 us
  between operations: 13.6 us -> 0.11 us
  blocking collectives: 26 us -> 13.2 us
  waiting for transfers between devices: 0.71 us -> 5.43 us
  Pallas kernels: 0 us -> 4.59 us
  starting transfers between devices: 0.01 us -> 3.64 us
  matrix products: 5.69 us -> 3.9 us
  local copies, waits for them, and re-layouts: 4.03 us -> 2.28 us
    reduce_sum x4 -> x0, other arithmetic: 44.5 us -> none  [pool_block(): jnp.sum((block_ids[:, :, None] == positions).astype(jnp.int32), axis=1)]
    all_to_all x1 -> x0, blocking collectives: 13 us -> none  [on_device(): lax.all_to_all(features, 'dev', split_axis=0, concat_axis=1, tiled=True)]
    ppermute x0 -> x4, waiting for transfers between devices: none -> 5.43 us  [the longest x1 5.43 us: on_device(): lax.ppermute(partial[(k - 1) * my_rows:k * my_rows], 'dev', [(i, (i + 2 *...]
    pallas_call x0 -> x4, Pallas kernels: none -> 4.59 us  [pool(): pl.pallas_call(lambda *refs: pool_kernel(offsets, *refs), out_shape=jax.S...]
    ppermute x0 -> x4, starting transfers between devices: none -> 3.64 us  [the longest x1 2.68 us: on_device(): lax.ppermute(partial[(k - 1) * my_rows:k * my_rows], 'dev', [(i, (i + 2 *...]
    dot_general x1, matrix products: 3.14 us -> 0.47 us  [on_device(): jnp.dot(hidden, w_second[0], preferred_element_type=jnp.float32)]
    gather x2 -> x0, local copies, waits for them, and re-layouts: 2.24 us -> none  [on_device(): features = jnp.take(jnp.concatenate(pieces, axis=1), order, axis=0)]
    unnamed x11 -> x13, local copies, waits for them, and re-layouts: 0.03 us -> 2.19 us
  transfers between devices with their start and end apart: 1 -> 4, of which waited for: 0 -> 1; matrix products, arithmetic and copies ran while one was open for 53% -> 2% of each run, Pallas kernels for 0% -> 14%
where the time goes in v1:
time: 33.4 us; the launch traced here: 33.1 us
  blocking collectives  13.2 us (40%)
  waiting for transfers between devices  5.43 us (16%)
  Pallas kernels  4.59 us (14%)
  matrix products  3.9 us (12%)
  starting transfers between devices  3.64 us (11%)
  local copies, waits for them, and re-layouts  2.28 us (7%)
    all_to_all x1, blocking collectives, on_device(): lax.all_to_all(outputs.reshape(1, towers, share, width), 'tower', split_a...  13.2 us
    ppermute x1, waiting for transfers between devices, on_device(): lax.ppermute(partial[(k - 1) * my_rows:k * my_rows], 'dev', [(i, (i + 2 *...  5.43 us
    pallas_call x4, Pallas kernels, pool(): pl.pallas_call(lambda *refs: pool_kernel(offsets, *refs), out_shape=jax.S...  4.59 us
    ppermute x1, starting transfers between devices, on_device(): lax.ppermute(partial[(k - 1) * my_rows:k * my_rows], 'dev', [(i, (i + 2 *...  2.68 us
    unnamed x13, local copies, waits for them, and re-layouts  2.19 us
    dot_general x1, matrix products, on_device(): head = jnp.dot(joined, w_head, preferred_element_type=jnp.float32)  1.47 us
    dot_general x3, matrix products, matmul(): return jnp.dot(left, right, preferred_element_type=jnp.float32)  0.93 us
    dot_general x1, matrix products, on_device(): jnp.dot(products.reshape(amount, towers * towers), w_interact, precision=...  0.83 us
  transfers between devices with their start and end apart: 4, of which 1 were waited for; matrix products, arithmetic and copies ran while one was open for 2% of the time, Pallas kernels for 14%

profile of v1, /device:TPU:0, one launch (start us, length us, event | category | flops | bytes accessed | tf_op | source)
XLA Modules:
  0.0 33.1 jit_solution(14237472396273866182)
XLA Ops:
  0.0 0.0 copy-start
  0.0 0.5 %collective-permute-start.2 = (bf16[512,1024]{1,0:T(8,128)(2,1)}, bf16[512,1024]{1,0:T(8,128)(2,1)S(1)}, u32[]{:S(2)}, u32[]{:S(2)}) collective-permute-start(bf16[512,1024]{1,0:T(8,128)(2,1)} %bitcast.48), channel_id=1, source_target_pairs={{0,1},{1,0},{2,3},{3,2},{4,5},{5,4},{6,7},{7,6},{8,9},{9,8},{10,11... | collective-permute-start | bytes 3145736 | tf_op jit(solution)/shard_map/ppermute | solution.py:107
  0.5 0.0 copy-start.3
  0.5 0.1 collective-permute-start.1
  0.5 0.4 %collective-permute-start = (s32[4,32,512]{2,1,0:T(8,128)}, s32[4,32,512]{2,1,0:T(8,128)S(1)}, u32[]{:S(2)}, u32[]{:S(2)}) collective-permute-start(s32[4,32,512]{2,1,0:T(8,128)} %bitcast.41), channel_id=1, source_target_pairs={{0,1},{1,0},{2,3},{3,2},{4,5},{5,4},{6,7},{7,6},{8,9},{9,8},{10,11... | collective-permute-start | bytes 786440 | tf_op jit(solution)/shard_map/ppermute | solution.py:105
  1.0 0.2 copy-done.3
  1.1 0.0 copy-start.1
  1.1 1.0 %copy-done.1 = bf16[1,4,512,128]{3,2,1,0:T(8,128)(2,1)S(1)} copy-done((bf16[1,4,512,128]{3,2,1,0:T(8,128)(2,1)S(1)}, bf16[1,4,512,128]{3,2,1,0:T(8,128)(2,1)}, u32[]{:S(2)}) %copy-start.1) | copy-done | bytes 524312
  2.2 0.0 copy-start.2
  2.2 0.9 %copy-done.2 = s32[1,4,512,32]{2,3,1,0:T(8,128)S(1)} copy-done((s32[1,4,512,32]{2,3,1,0:T(8,128)S(1)}, s32[1,4,512,32]{2,3,1,0:T(8,128)}, u32[]{:S(2)}) %copy-start.2) | copy-done | bytes 262168
  3.1 0.0 copy-start.4
  3.1 1.2 %shard_map.75 = bf16[128,512]{1,0:T(8,128)(2,1)S(1)} custom-call(s32[4,32,512]{2,1,0:T(8,128)S(1)} %bitcast.42, bf16[4,512,128]{2,1,0:T(8,128)(2,1)S(1)} %bitcast.39, s32[4,128]{1,0:T(4,128)S(1)} %bitcast.44), custom_call_target="tpu_custom_call" | custom-call | flops 268435456 | bytes 786432 | tf_op jit(solution)/shard_map/pallas_call | solution.py:75
  4.3 1.1 %shard_map.73 = bf16[128,512]{1,0:T(8,128)(2,1)S(1)} custom-call(s32[4,32,512]{2,1,0:T(8,128)S(1)} %bitcast.43, bf16[4,512,128]{2,1,0:T(8,128)(2,1)S(1)} %bitcast.40, s32[4,128]{1,0:T(4,128)S(1)} %bitcast.45), custom_call_target="tpu_custom_call" | custom-call | flops 268435456 | bytes 786432 | tf_op jit(solution)/shard_map/pallas_call | solution.py:75
  5.4 0.0 copy-done.4
  5.4 0.3 fusion.12
  5.8 0.0 collective-permute-done.refs_0_
  5.8 0.0 collective-permute-done.1.refs_1_
  5.8 1.2 %shard_map.76 = bf16[128,512]{1,0:T(8,128)(2,1)S(1)} custom-call(s32[4,32,512]{2,1,0:T(8,128)S(1)} %collective-permute-done.refs_0_, bf16[4,512,128]{2,1,0:T(8,128)(2,1)S(1)} %collective-permute-done.1.refs_1_, s32[4,128]{1,0:T(4,128)S(1)} %bitcast.46), custom_call_target="tpu_custom_call" | custom-call | flops 268435456 | bytes 786432 | tf_op jit(solution)/shard_map/pallas_call | solution.py:75
  6.9 0.0 collective-permute-done.2
  7.0 0.3 fusion.3
  7.3 2.7 %collective-permute-start.3 = (bf16[128,1024]{1,0:T(8,128)(2,1)S(1)}, bf16[128,1024]{1,0:T(8,128)(2,1)S(1)}, u32[]{:S(2)}, u32[]{:S(2)}) collective-permute-start(bf16[128,1024]{1,0:T(8,128)(2,1)S(1)} %fusion.3), channel_id=1, source_target_pairs={{0,2},{1,3},{2,0},{3,1},{4,6},{5,7},{6,4},{7,5},{8,10},{9,11},{10,... | collective-permute-start | bytes 786440 | tf_op jit(solution)/shard_map/ppermute | solution.py:116
  10.0 0.3 fusion.14
  10.3 1.1 %shard_map.74 = bf16[128,512]{1,0:T(8,128)(2,1)S(1)} custom-call(s32[4,32,512]{2,1,0:T(8,128)S(1)} %collective-permute-done.refs_0_, bf16[4,512,128]{2,1,0:T(8,128)(2,1)S(1)} %collective-permute-done.1.refs_1_, s32[4,128]{1,0:T(4,128)S(1)} %bitcast.47), custom_call_target="tpu_custom_call" | custom-call | flops 268435456 | bytes 786432 | tf_op jit(solution)/shard_map/pallas_call | solution.py:75
  11.4 5.4 %collective-permute-done.3 = bf16[128,1024]{1,0:T(8,128)(2,1)S(1)} collective-permute-done((bf16[128,1024]{1,0:T(8,128)(2,1)S(1)}, bf16[128,1024]{1,0:T(8,128)(2,1)S(1)}, u32[]{:S(2)}, u32[]{:S(2)}) %collective-permute-start.3) | collective-permute-done | bytes 262176 | tf_op jit(solution)/shard_map/ppermute | solution.py:116
  16.8 0.0 copy-done
  16.8 0.5 %fusion.5 = bf16[128,512]{1,0:T(8,128)(2,1)S(1)} fusion(f32[128,1024]{1,0:T(8,128)S(1)} %fusion.14, bf16[128,512]{1,0:T(8,128)(2,1)S(1)} %shard_map.74, bf16[512,1024]{1,0:T(8,128)(2,1)S(1)} %collective-permute-done.2, bf16[1,1024,512]{2,1,0:T(8,128)(2,1)S(1)} %copy-done, bf16[128,1024]{1,0:T(8,128)(2,1)S(1)} %collective-permute-done.3), kind=kOutput, calls=%fused_computation.7 | convolution fusion | flops 269156352 | bytes 3145728 | tf_op jit(solution)/shard_map/dot_general | solution.py:129
  17.3 13.2 %all_to_all.4 = bf16[1,8,16,512]{3,2,0,1:T(8,128)(2,1)S(1)} all-to-all(bf16[1,8,16,512]{3,2,0,1:T(8,128)(2,1)S(1)} %bitcast.49), channel_id=1, replica_groups=mesh['tower'=8,'dev'=4] {'tower'}, dimensions={1} | all-to-all | bytes 262144 | tf_op jit(solution)/shard_map/all_to_all | solution.py:132
  30.5 0.2 convolution_multiply_fusion
  30.7 0.1 copy.13
  30.8 0.0 copy-start.5
  30.8 1.5 %fusion.18 = f32[16,128]{1,0:T(8,128)S(1)} fusion(bf16[16,4096]{1,0:T(8,128)(2,1)S(1)} %bitcast.50, bf16[4096,128]{1,0:T(8,128)(2,1)} %param.12), kind=kOutput, calls=%fused_computation.22 | convolution fusion | flops 16777216 | bytes 1187840 | tf_op jit(solution)/shard_map/dot_general | solution.py:137
  32.3 0.0 copy-done.5
  32.3 0.8 %fusion.6 = f32[1,16,128]{2,1,0:T(8,128)} fusion(f32[16,128]{1,0:T(8,128)S(1)} %fusion.18, f32[64,128]{1,0:T(8,128)S(1)} %copy-done.5, f32[16,8,8]{0,2,1:T(8,128)S(1)} %copy.13), kind=kOutput, calls=%fused_computation.10 | convolution fusion | flops 1574912 | bytes 53248 | tf_op jit(solution)/shard_map/dot_general | solution.py:142
  (1 shorter events, 0.0 us)
Async XLA Ops:
  0.0 16.8 %copy-start = (bf16[1,1024,512]{2,1,0:T(8,128)(2,1)S(1)}, bf16[1,1024,512]{2,1,0:T(8,128)(2,1)}, u32[]{:S(2)}) copy-start(bf16[1,1024,512]{2,1,0:T(8,128)(2,1)} %param.11) | copy-start | bytes 3145732
  0.0 6.9 %collective-permute-start.2 = (bf16[512,1024]{1,0:T(8,128)(2,1)}, bf16[512,1024]{1,0:T(8,128)(2,1)S(1)}, u32[]{:S(2)}, u32[]{:S(2)}) collective-permute-start(bf16[512,1024]{1,0:T(8,128)(2,1)} %bitcast.48), channel_id=1, source_target_pairs={{0,1},{1,0},{2,3},{3,2},{4,5},{5,4},{6,7},{7,6},{8,9},{9,8},{10,11... | collective-permute-start | bytes 3145736 | tf_op jit(solution)/shard_map/ppermute | solution.py:107
  0.5 0.7 %copy-start.3 = (s32[512]{0:T(512)S(1)}, s32[512]{0:T(512)}, u32[]{:S(2)}) copy-start(s32[512]{0:T(512)} %param.9) | copy-start | bytes 6148
  0.5 5.3 %collective-permute-start.1 = (bf16[4,512,128]{2,1,0:T(8,128)(2,1)}, bf16[4,512,128]{2,1,0:T(8,128)(2,1)S(1)}, u32[]{:S(2)}, u32[]{:S(2)}) collective-permute-start(bf16[4,512,128]{2,1,0:T(8,128)(2,1)} %bitcast.38), channel_id=1, source_target_pairs={{0,1},{1,0},{2,3},{3,2},{4,5},{5,4},{6,7},{7,6},{8,9},{9,8},{10,11... | collective-permute-start | bytes 1572872 | tf_op jit(solution)/shard_map/ppermute | solution.py:106
  0.5 5.2 %collective-permute-start = (s32[4,32,512]{2,1,0:T(8,128)}, s32[4,32,512]{2,1,0:T(8,128)S(1)}, u32[]{:S(2)}, u32[]{:S(2)}) collective-permute-start(s32[4,32,512]{2,1,0:T(8,128)} %bitcast.41), channel_id=1, source_target_pairs={{0,1},{1,0},{2,3},{3,2},{4,5},{5,4},{6,7},{7,6},{8,9},{9,8},{10,11... | collective-permute-start | bytes 786440 | tf_op jit(solution)/shard_map/ppermute | solution.py:105
  1.1 1.0 %copy-start.1 = (bf16[1,4,512,128]{3,2,1,0:T(8,128)(2,1)S(1)}, bf16[1,4,512,128]{3,2,1,0:T(8,128)(2,1)}, u32[]{:S(2)}) copy-start(bf16[1,4,512,128]{3,2,1,0:T(8,128)(2,1)} %param.8) | copy-start | bytes 1572868
  2.2 0.9 %copy-start.2 = (s32[1,4,512,32]{2,3,1,0:T(8,128)S(1)}, s32[1,4,512,32]{2,3,1,0:T(8,128)}, u32[]{:S(2)}) copy-start(s32[1,4,512,32]{2,3,1,0:T(8,128)} %param.7) | copy-start | bytes 786436
  3.1 2.3 %copy-start.4 = (bf16[1,512,1024]{2,1,0:T(8,128)(2,1)S(1)}, bf16[1,512,1024]{2,1,0:T(8,128)(2,1)}, u32[]{:S(2)}) copy-start(bf16[1,512,1024]{2,1,0:T(8,128)(2,1)} %param.10) | copy-start | bytes 3145732
  7.3 9.6 %collective-permute-start.3 = (bf16[128,1024]{1,0:T(8,128)(2,1)S(1)}, bf16[128,1024]{1,0:T(8,128)(2,1)S(1)}, u32[]{:S(2)}, u32[]{:S(2)}) collective-permute-start(bf16[128,1024]{1,0:T(8,128)(2,1)S(1)} %fusion.3), channel_id=1, source_target_pairs={{0,2},{1,3},{2,0},{3,1},{4,6},{5,7},{6,4},{7,5},{8,10},{9,11},{10,... | collective-permute-start | bytes 786440 | tf_op jit(solution)/shard_map/ppermute | solution.py:116
  30.8 1.5 %copy-start.5 = (f32[64,128]{1,0:T(8,128)S(1)}, f32[64,128]{1,0:T(8,128)}, u32[]{:S(2)}) copy-start(f32[64,128]{1,0:T(8,128)} %param.13) | copy-start | bytes 98308

commit v2 on v1

v2 whole, which is shorter than its diff:
```python
import math

import jax
import jax.numpy as jnp
from jax import lax
from jax.experimental import pallas as pl
from jax.experimental.pallas import tpu as pltpu
from jax.sharding import PartitionSpec as P

FIELDS = 8
FIELD_MAX = 15
EVEN_FIELDS = 0x0F0F0F0F


def multiply(left, right):
    return jnp.dot(left, right, preferred_element_type=jnp.float32)


def select_ids(ids, order_row, residues):
    feats, bag, samples = ids.shape
    rows = order_row.shape[1]
    shift = residues.bit_length() - 1
    pick = lax.broadcasted_iota(jnp.int32, (samples, rows), 0) == order_row
    pick = jnp.where(pick, 1.0, 0.0).astype(jnp.bfloat16)
    flat = ids.reshape(feats * bag, samples)
    low = (flat & (residues - 1)).astype(jnp.float32).astype(jnp.bfloat16)
    high = (flat >> shift).astype(jnp.float32).astype(jnp.bfloat16)
    low = jnp.dot(low, pick, preferred_element_type=jnp.float32)
    high = jnp.dot(high, pick, preferred_element_type=jnp.float32)
    return low.astype(jnp.int32), jnp.left_shift(1, 4 * high.astype(jnp.int32))


def pool_feature(residue_ref, weight_ref, base, bag, table):
    residues = table.shape[0] // FIELDS
    spots = lax.broadcasted_iota(jnp.int32, (residues, residue_ref.shape[1]), 0)
    even, odd = None, None
    for first in range(0, bag, FIELD_MAX):
        tally = None
        for at in range(base + first, base + min(first + FIELD_MAX, bag)):
            hit = jnp.where(
                residue_ref[pl.ds(at, 1), :] == spots, weight_ref[pl.ds(at, 1), :], 0
            )
            tally = hit if tally is None else tally + hit
        low, high = tally & EVEN_FIELDS, (tally >> 4) & EVEN_FIELDS
        even, odd = (low, high) if even is None else (even + low, odd + high)
    words = jnp.concatenate([even, odd], axis=0).T
    counts = jnp.concatenate(
        [
            ((words >> (8 * place)) & 255).astype(jnp.float32).astype(jnp.bfloat16)
            for place in range(FIELDS // 2)
        ],
        axis=1,
    )
    return jnp.dot(counts, table, preferred_element_type=jnp.float32).astype(jnp.bfloat16)


def multiply(left, right):
    return jnp.dot(left, right, preferred_element_type=jnp.float32)


def pick_ids(target, ids, order_ref, active, residue_ref, weight_ref):
    residue_ref[...], weight_ref[...] = select_ids(
        ids, order_ref[pl.ds(target, 1), :], active // FIELDS
    )


def fetch(sources, targets, sems):
    copies = [
        pltpu.make_async_copy(source, target, sems.at[place])
        for place, (source, target) in enumerate(zip(sources, targets))
    ]
    for copy in copies:
        copy.start()
    return copies


def block_of(chips_on, core_flip, devices):
    return lax.rem((lax.axis_index("dev") ^ core_flip) + 2 * chips_on, devices)


def first_kernel(
    blocks, order_hbm, ids_hbm, tables_hbm, w_hbm, out_ref, order_ref, ids_ref, tables_ref, w_ref,
    residue_ref, weight_ref, sems,
):
    devices, rows = order_hbm.shape
    feats, bag, samples = ids_hbm.shape
    active, emb = tables_hbm.shape[1:]
    copies = fetch(
        (order_hbm, ids_hbm, tables_hbm, w_hbm), (order_ref, ids_ref, tables_ref, w_ref), sems
    )
    copies[0].wait()
    copies[1].wait()
    for block, chips_on in enumerate(blocks):
        pick_ids(
            block_of(chips_on, 1, devices), ids_ref[...], order_ref, active, residue_ref, weight_ref
        )
        if block == 0:
            copies[2].wait()
        for feature in range(feats):
            out_ref[block * rows : (block + 1) * rows, feature * emb : (feature + 1) * emb] = (
                pool_feature(residue_ref, weight_ref, feature * bag, bag, tables_ref[feature])
            )
    copies[3].wait()


def pool_kernel(
    blocks, order_ref, ids_ref, tables_ref, after_hbm, out_ref, residue_ref, weight_ref
):
    devices, rows = order_ref.shape
    feats, bag, samples = ids_ref.shape
    active, emb = tables_ref.shape[1:]
    for block, chips_on in enumerate(blocks):
        pick_ids(
            block_of(chips_on, 1, devices), ids_ref[...], order_ref, active, residue_ref, weight_ref
        )
        for feature in range(feats):
            out_ref[block * rows : (block + 1) * rows, feature * emb : (feature + 1) * emb] = (
                pool_feature(residue_ref, weight_ref, feature * bag, bag, tables_ref[feature])
            )


def layer_kernel(
    blocks, order_ref, ids_ref, tables_ref, w_ref, *refs
):
    if len(refs) == 3:
        out_ref, residue_ref, weight_ref = refs
        copy = None
    else:
        head_hbm, after_hbm, out_ref, head_ref, residue_ref, weight_ref, sem = refs
        copy = pltpu.make_async_copy(head_hbm, head_ref, sem)
        copy.start()
    devices, rows = order_ref.shape
    feats, bag, samples = ids_ref.shape
    active, emb = tables_ref.shape[1:]
    for block, chips_on in enumerate(blocks):
        pick_ids(
            block_of(chips_on, 0, devices), ids_ref[...], order_ref, active, residue_ref, weight_ref
        )
        total = None
        for first in range(0, feats, 2):
            some = range(first, min(first + 2, feats))
            pooled = [
                pool_feature(residue_ref, weight_ref, feature * bag, bag, tables_ref[feature])
                for feature in some
            ]
            part = multiply(
                jnp.concatenate(pooled, axis=1), w_ref[first * emb : (first + len(some)) * emb, :]
            )
            total = part if total is None else total + part
        out_ref[block * rows : (block + 1) * rows, :] = total
    if copy is not None:
        copy.wait()


IN_HBM = pl.BlockSpec(memory_space=pltpu.HBM)
ON_CHIP = pl.BlockSpec(memory_space=pltpu.VMEM)
VMEM_LIMIT = 32 * 1024 * 1024


def in_hbm(*arrays):
    return [pltpu.with_memory_space_constraint(array, pltpu.HBM) for array in arrays]


def like(array):
    return jax.ShapeDtypeStruct(array.shape, array.dtype)


def picked(ids, rows):
    return [pltpu.VMEM((ids.shape[0] * ids.shape[1], rows), jnp.int32)] * 2


def options():
    return {
        "compiler_params": pltpu.CompilerParams(vmem_limit_bytes=VMEM_LIMIT),
        "cost_estimate": pl.CostEstimate(flops=1, bytes_accessed=1, transcendentals=0),
    }


def first_pool(blocks, order, ids, tables, w):
    rows = order.shape[1]
    count = len(blocks) * rows
    width = ids.shape[0] * tables.shape[2]
    return pl.pallas_call(
        lambda *refs: first_kernel(blocks, *refs),
        out_shape=(
            jax.ShapeDtypeStruct((count, width), jnp.bfloat16),
            like(order), like(ids), like(tables), like(w),
        ),
        in_specs=[IN_HBM] * 4,
        out_specs=(ON_CHIP,) * 5,
        scratch_shapes=picked(ids, rows) + [pltpu.SemaphoreType.DMA((4,))],
        name="first_pool",
        **options(),
    )(*in_hbm(order, ids, tables, w))


def pool(blocks, order, ids, tables, after):
    rows = order.shape[1]
    count = len(blocks) * rows
    width = ids.shape[0] * tables.shape[2]
    return pl.pallas_call(
        lambda *refs: pool_kernel(blocks, *refs),
        out_shape=jax.ShapeDtypeStruct((count, width), jnp.bfloat16),
        in_specs=[ON_CHIP] * 3 + [pl.BlockSpec(memory_space=pl.ANY)],
        out_specs=ON_CHIP,
        scratch_shapes=picked(ids, rows),
        name="pool",
        **options(),
    )(order, ids, tables, after)


def layer(blocks, order, ids, tables, w, head=None, after=None):
    rows = order.shape[1]
    count = len(blocks) * rows
    out_shape = [jax.ShapeDtypeStruct((count, w.shape[1]), jnp.float32)]
    operands = [order, ids, tables, w]
    in_specs = [ON_CHIP] * 4
    scratch = picked(ids, rows)
    if head is not None:
        out_shape.append(like(head))
        operands += in_hbm(head) + [after]
        in_specs += [IN_HBM, pl.BlockSpec(memory_space=pl.ANY)]
        scratch.append(pltpu.SemaphoreType.DMA)
    return pl.pallas_call(
        lambda *refs: layer_kernel(blocks, *refs),
        out_shape=tuple(out_shape),
        in_specs=in_specs,
        out_specs=(ON_CHIP,) * len(out_shape),
        scratch_shapes=scratch,
        name="layer",
        **options(),
    )(*operands)


def join_kernel(partial_ref, pooled_ref, w_ref, out_ref):
    out_ref[...] = partial_ref[...] + multiply(pooled_ref[...], w_ref[...])


def join(partial, pooled, w):
    return pl.pallas_call(
        join_kernel,
        out_shape=like(partial),
        in_specs=[ON_CHIP] * 3,
        out_specs=ON_CHIP,
        compiler_params=pltpu.CompilerParams(vmem_limit_bytes=VMEM_LIMIT),
        cost_estimate=pl.CostEstimate(flops=1, bytes_accessed=1, transcendentals=0),
        name="join",
    )(partial, pooled, w)


def score_kernel(outputs_ref, head_ref, interact_ref, scores_ref):
    towers, rows, width = outputs_ref.shape
    wide = jnp.concatenate([outputs_ref[t] for t in range(towers)], axis=1)
    scores = multiply(wide, head_ref[...])
    interact = interact_ref[...] * (1.0 / math.sqrt(width))
    for t in range(towers):
        mine = outputs_ref[t].astype(jnp.float32)
        for s in range(t, towers):
            gram = jnp.sum(mine * outputs_ref[s].astype(jnp.float32), axis=1, keepdims=True)
            weights = interact[t * towers + s : t * towers + s + 1, :]
            if s != t:
                weights = weights + interact[s * towers + t : s * towers + t + 1, :]
            scores = scores + gram * weights
    scores_ref[...] = scores


def score(outputs, head, interact):
    towers, rows, width = outputs.shape
    return pl.pallas_call(
        score_kernel,
        out_shape=jax.ShapeDtypeStruct((rows, head.shape[1]), jnp.float32),
        in_specs=[ON_CHIP] * 3,
        out_specs=ON_CHIP,
        compiler_params=pltpu.CompilerParams(vmem_limit_bytes=VMEM_LIMIT),
        name="score",
    )(outputs, head, interact)


def on_device(ids, tables, order, w_first, w_second, w_head, w_interact):
    towers = lax.axis_size("tower")
    devices = lax.axis_size("dev")
    samples = ids.shape[2]
    my_rows = samples // devices
    order = order.reshape(devices, my_rows)
    ids, tables, w_first = jnp.swapaxes(ids[0], 1, 2), tables[0], w_first[0]

    def swap_cores(array):
        return lax.ppermute(array, "dev", [(i, i ^ 1) for i in range(devices)])

    w_other = swap_cores(w_first)
    away = tuple(range(1, devices // 2))
    pooled, order, ids, tables, w_first = first_pool(away, order, ids, tables, w_first)
    pooled = swap_cores(pooled)
    (partial,) = layer(away, order, ids, tables, w_first)
    partial = (partial + multiply(pooled, w_other)).astype(jnp.bfloat16)
    received = []
    for k in away:
        received.append(
            lax.ppermute(
                partial[(k - 1) * my_rows : k * my_rows],
                "dev",
                [(i, (i + 2 * k) % devices) for i in range(devices)],
            )
        )
    pooled = swap_cores(pool((0,), order, ids, tables, partial))
    preact, w_head = layer((0,), order, ids, tables, w_first, w_head, partial)
    preact = join(preact, pooled, w_other)
    for part in received:
        preact = preact + part.astype(jnp.float32)

    hidden = jnp.maximum(preact, 0.0).astype(jnp.bfloat16)
    outputs = multiply(hidden, w_second[0]).astype(jnp.bfloat16)
    width = outputs.shape[1]
    share = my_rows // towers
    gathered = lax.all_to_all(
        outputs.reshape(1, towers, share, width), "tower", split_axis=1, concat_axis=0, tiled=True
    )[:, 0]
    return score(gathered, w_head, w_interact)[None]


def solution(mesh):
    return jax.shard_map(
        on_device,
        mesh=mesh,
        in_specs=(
            P("tower", "dev", None, None),
            P("tower", "dev", None, None),
            P(),
            P("tower", "dev", None),
            P("tower", None, None),
            P(),
            P(),
        ),
        out_specs=P("dev", "tower", None),
        check_vma=False,
    )
```

time: 33.4 us -> 28.7 us (0.86)
  Pallas kernels: 4.59 us -> 8.11 us
  matrix products: 3.9 us -> 0.63 us
  waiting for transfers between devices: 5.43 us -> 2.79 us
  local copies, waits for them, and re-layouts: 2.28 us -> 0.01 us
    pallas_call x4 -> x6, Pallas kernels: 4.59 us -> 8.11 us  [the longest x2 3.6 us: layer(): pl.pallas_call(lambda *refs: layer_kernel(blocks, *refs), out_shape=tuple...]
    dot_general x7 -> x2, matrix products: 3.9 us -> 0.63 us  [multiply(): return jnp.dot(left, right, preferred_element_type=jnp.float32)]
    ppermute x1, waiting for transfers between devices: 5.43 us -> 2.78 us  [on_device(): lax.ppermute(partial[(k - 1) * my_rows:k * my_rows], 'dev', [(i, (i + 2 *...]
    unnamed x13 -> x4, local copies, waits for them, and re-layouts: 2.19 us -> 0.01 us
  transfers between devices with their start and end apart: 4 -> 4, of which waited for: 1 -> 1; matrix products, arithmetic and copies ran while one was open for 2% -> 0% of each run, Pallas kernels for 14% -> 25%
where the time goes in v2:
time: 28.7 us; the launch traced here: 28.5 us
  blocking collectives  13.2 us (46%)
  Pallas kernels  8.11 us (28%)
  starting transfers between devices  3.67 us (13%)
  waiting for transfers between devices  2.79 us (10%)
  matrix products  0.63 us (2%)
    all_to_all x1, blocking collectives, on_device(): lax.all_to_all(outputs.reshape(1, towers, share, width), 'tower', split_a...  13.2 us
    pallas_call x2, Pallas kernels, layer(): pl.pallas_call(lambda *refs: layer_kernel(blocks, *refs), out_shape=tuple...  3.6 us
    ppermute x1, starting transfers between devices, on_device(): lax.ppermute(partial[(k - 1) * my_rows:k * my_rows], 'dev', [(i, (i + 2 *...  2.95 us
    ppermute x1, waiting for transfers between devices, on_device(): lax.ppermute(partial[(k - 1) * my_rows:k * my_rows], 'dev', [(i, (i + 2 *...  2.78 us
    pallas_call x1, Pallas kernels, first_pool(): pl.pallas_call(lambda *refs: first_kernel(blocks, *refs), out_shape=(jax....  2.14 us
    pallas_call x1, Pallas kernels, pool(): pl.pallas_call(lambda *refs: pool_kernel(blocks, *refs), out_shape=jax.Sh...  1.15 us
    pallas_call x1, Pallas kernels, score(): pl.pallas_call(score_kernel, out_shape=jax.ShapeDtypeStruct((rows, head.s...  0.9 us
    ppermute x3, starting transfers between devices, swap_cores(): return lax.ppermute(array, 'dev', [(i, i ^ 1) for i in range(devices)])  0.72 us
  transfers between devices with their start and end apart: 4, of which 1 were waited for; matrix products, arithmetic and copies ran while one was open for 0% of the time, Pallas kernels for 25%

profile of v2, /device:TPU:0, one launch (start us, length us, event | category | flops | bytes accessed | tf_op | source)
XLA Modules:
  0.0 28.5 jit_solution(13250181988588298301)
XLA Ops:
  0.0 0.0 copy-start
  0.0 0.5 %collective-permute-start.1 = (bf16[512,1024]{1,0:T(8,128)(2,1)}, bf16[512,1024]{1,0:T(8,128)(2,1)S(1)}, u32[]{:S(2)}, u32[]{:S(2)}) collective-permute-start(bf16[512,1024]{1,0:T(8,128)(2,1)} %bitcast.17), channel_id=1, source_target_pairs={{0,1},{1,0},{2,3},{3,2},{4,5},{5,4},{6,7},{7,6},{8,9},{9,8},{10,11... | collective-permute-start | bytes 3145736 | tf_op jit(solution)/shard_map/ppermute | solution.py:288
  0.5 2.1 %first_pool.1 = (bf16[128,512]{1,0:T(8,128)(2,1)S(1)}, s32[4,128]{1,0:T(4,128)S(1)}, s32[4,32,512]{2,1,0:T(8,128)S(1)}, bf16[4,512,128]{2,1,0:T(8,128)(2,1)S(1)}, bf16[512,1024]{1,0:T(8,128)(2,1)S(1)}) custom-call(s32[4,128]{1,0:T(4,128)} %bitcast.22, s32[4,32,512]{2,1,0:T(8,128)} %bitcast.21, bf16[4,512,128]{2,1,0:T(8,128)(2,1)} %bitcast.19, ...), custom_call_target="tpu_custom_call" | custom-call | flops 1 | bytes 1 | tf_op jit(solution)/shard_map/first_pool/pallas_call | solution.py:183
  2.6 0.2 collective-permute-start
  2.8 1.4 %layer.2 = f32[128,1024]{1,0:T(8,128)S(1)} custom-call(s32[4,128]{1,0:T(4,128)S(1)} %get-tuple-element.12.refs_0_, s32[4,32,512]{2,1,0:T(8,128)S(1)} %get-tuple-element.13.refs_1_, bf16[4,512,128]{2,1,0:T(8,128)(2,1)S(1)} %get-tuple-element.14.refs_2_, bf16[512,1024]{1,0:T(8,128)(2,1)S(1)} %get-tuple-element.15.refs_3_), custom_call_target="tpu_custom_call" | custom-call | flops 1 | bytes 1 | tf_op jit(solution)/shard_map/layer/pallas_call | solution.py:224
  4.2 0.0 collective-permute-done
  4.2 0.0 collective-permute-done.1.w_ref
  4.2 0.3 %fusion.refs_5_.refs_3_ = bf16[128,1024]{1,0:T(8,128)(2,1)S(1)} fusion(f32[128,1024]{1,0:T(8,128)S(1)} %layer.2, bf16[128,512]{1,0:T(8,128)(2,1)S(1)} %collective-permute-done, bf16[512,1024]{1,0:T(8,128)(2,1)S(1)} %collective-permute-done.1.w_ref), kind=kOutput, calls=%fused_computation.1 | convolution fusion | flops 134479872 | bytes 1966080 | tf_op jit(solution)/shard_map/dot_general | solution.py:58
  4.6 3.0 %collective-permute-start.3 = (bf16[128,1024]{1,0:T(8,128)(2,1)S(1)}, bf16[128,1024]{1,0:T(8,128)(2,1)S(1)}, u32[]{:S(2)}, u32[]{:S(2)}) collective-permute-start(bf16[128,1024]{1,0:T(8,128)(2,1)S(1)} %fusion.refs_5_.refs_3_), channel_id=1, source_target_pairs={{0,2},{1,3},{2,0},{3,1},{4,6},{5,7},{6,4},{7,5},{8,10},{9,11},{10,... | collective-permute-start | bytes 786440 | tf_op jit(solution)/shard_map/ppermute | solution.py:299
  7.5 1.2 %pool.1 = bf16[128,512]{1,0:T(8,128)(2,1)S(1)} custom-call(s32[4,128]{1,0:T(4,128)S(1)} %get-tuple-element.12.refs_0_, s32[4,32,512]{2,1,0:T(8,128)S(1)} %get-tuple-element.13.refs_1_, bf16[4,512,128]{2,1,0:T(8,128)(2,1)S(1)} %get-tuple-element.14.refs_2_, bf16[128,1024]{1,0:T(8,128)(2,1)S(1)} %fusion.refs_5_.refs_3_), custom_call_target="tpu_custom_call" | custom-call | flops 1 | bytes 1 | tf_op jit(solution)/shard_map/pool/pallas_call | solution.py:201
  8.7 0.1 collective-permute-start.2
  8.7 2.2 %layer.3 = (f32[128,1024]{1,0:T(8,128)S(1)}, bf16[4096,128]{1,0:T(8,128)(2,1)S(1)}) custom-call(s32[4,128]{1,0:T(4,128)S(1)} %get-tuple-element.12.refs_0_, s32[4,32,512]{2,1,0:T(8,128)S(1)} %get-tuple-element.13.refs_1_, bf16[4,512,128]{2,1,0:T(8,128)(2,1)S(1)} %get-tuple-element.14.refs_2_, bf16[512,1024]{1,0:T(8,128)(2,1)S(1)} %get-tuple-element.15.refs_3_, ...), custom_call_target="tpu_custom_call" | custom-call | flops 1 | bytes 1 | tf_op jit(solution)/shard_map/layer/pallas_call | solution.py:224
  11.0 0.0 collective-permute-done.2.pooled_ref
  11.0 0.3 %join.1 = f32[128,1024]{1,0:T(8,128)S(1)} custom-call(f32[128,1024]{1,0:T(8,128)S(1)} %get-tuple-element.17.partial_ref, bf16[128,512]{1,0:T(8,128)(2,1)S(1)} %collective-permute-done.2.pooled_ref, bf16[512,1024]{1,0:T(8,128)(2,1)S(1)} %collective-permute-done.1.w_ref), custom_call_target="tpu_custom_call" | custom-call | flops 1 | bytes 1 | tf_op jit(solution)/shard_map/join/pallas_call | solution.py:240
  11.3 2.8 %collective-permute-done.3 = bf16[128,1024]{1,0:T(8,128)(2,1)S(1)} collective-permute-done((bf16[128,1024]{1,0:T(8,128)(2,1)S(1)}, bf16[128,1024]{1,0:T(8,128)(2,1)S(1)}, u32[]{:S(2)}, u32[]{:S(2)}) %collective-permute-start.3) | collective-permute-done | bytes 262176 | tf_op jit(solution)/shard_map/ppermute | solution.py:299
  14.1 0.0 copy-done
  14.1 0.3 %convolution_convert_fusion = bf16[128,512]{1,0:T(8,128)(2,1)S(1)} fusion(bf16[1,1024,512]{2,1,0:T(8,128)(2,1)S(1)} %copy-done, f32[128,1024]{1,0:T(8,128)S(1)} %join.1, bf16[128,1024]{1,0:T(8,128)(2,1)S(1)} %collective-permute-done.3), kind=kOutput, calls=%fused_computation.2 | convolution fusion | flops 134807552 | bytes 1966080 | tf_op jit(solution)/shard_map/dot_general | solution.py:58
  14.4 0.0 copy-start.1
  14.4 13.2 %all_to_all.4 = bf16[1,8,16,512]{3,2,0,1:T(8,128)(2,1)S(1)} all-to-all(bf16[1,8,16,512]{3,2,0,1:T(8,128)(2,1)S(1)} %bitcast.20), channel_id=1, replica_groups=mesh['tower'=8,'dev'=4] {'tower'}, dimensions={1} | all-to-all | bytes 262144 | tf_op jit(solution)/shard_map/all_to_all | solution.py:315
  27.6 0.0 copy-done.1
  27.6 0.9 %score.1 = f32[16,128]{1,0:T(8,128)} custom-call(bf16[8,16,512]{2,1,0:T(8,128)(2,1)S(1)} %bitcast.16, bf16[4096,128]{1,0:T(8,128)(2,1)S(1)} %get-tuple-element.18.head_ref, f32[64,128]{1,0:T(8,128)S(1)} %copy-done.1), custom_call_target="tpu_custom_call" | custom-call | tf_op jit(solution)/shard_map/score/pallas_call | solution.py:269
Async XLA Ops:
  0.0 14.1 %copy-start = (bf16[1,1024,512]{2,1,0:T(8,128)(2,1)S(1)}, bf16[1,1024,512]{2,1,0:T(8,128)(2,1)}, u32[]{:S(2)}) copy-start(bf16[1,1024,512]{2,1,0:T(8,128)(2,1)} %param.11) | copy-start | bytes 3145732
  0.0 4.2 %collective-permute-start.1 = (bf16[512,1024]{1,0:T(8,128)(2,1)}, bf16[512,1024]{1,0:T(8,128)(2,1)S(1)}, u32[]{:S(2)}, u32[]{:S(2)}) collective-permute-start(bf16[512,1024]{1,0:T(8,128)(2,1)} %bitcast.17), channel_id=1, source_target_pairs={{0,1},{1,0},{2,3},{3,2},{4,5},{5,4},{6,7},{7,6},{8,9},{9,8},{10,11... | collective-permute-start | bytes 3145736 | tf_op jit(solution)/shard_map/ppermute | solution.py:288
  2.6 1.6 %collective-permute-start = (bf16[128,512]{1,0:T(8,128)(2,1)S(1)}, bf16[128,512]{1,0:T(8,128)(2,1)S(1)}, u32[]{:S(2)}, u32[]{:S(2)}) collective-permute-start(bf16[128,512]{1,0:T(8,128)(2,1)S(1)} %get-tuple-element.16), channel_id=1, source_target_pairs={{0,1},{1,0},{2,3},{3,2},{4,5},{5,4},{6,7},{7,6},{8,9},{9,8},{10,11... | collective-permute-start | bytes 393224 | tf_op jit(solution)/shard_map/ppermute | solution.py:288
  4.6 9.5 %collective-permute-start.3 = (bf16[128,1024]{1,0:T(8,128)(2,1)S(1)}, bf16[128,1024]{1,0:T(8,128)(2,1)S(1)}, u32[]{:S(2)}, u32[]{:S(2)}) collective-permute-start(bf16[128,1024]{1,0:T(8,128)(2,1)S(1)} %fusion.refs_5_.refs_3_), channel_id=1, source_target_pairs={{0,2},{1,3},{2,0},{3,1},{4,6},{5,7},{6,4},{7,5},{8,10},{9,11},{10,... | collective-permute-start | bytes 786440 | tf_op jit(solution)/shard_map/ppermute | solution.py:299
  8.7 2.3 %collective-permute-start.2 = (bf16[128,512]{1,0:T(8,128)(2,1)S(1)}, bf16[128,512]{1,0:T(8,128)(2,1)S(1)}, u32[]{:S(2)}, u32[]{:S(2)}) collective-permute-start(bf16[128,512]{1,0:T(8,128)(2,1)S(1)} %pool.1), channel_id=1, source_target_pairs={{0,1},{1,0},{2,3},{3,2},{4,5},{5,4},{6,7},{7,6},{8,9},{9,8},{10,11... | collective-permute-start | bytes 393224 | tf_op jit(solution)/shard_map/ppermute | solution.py:288
  14.4 13.2 %copy-start.1 = (f32[64,128]{1,0:T(8,128)S(1)}, f32[64,128]{1,0:T(8,128)}, u32[]{:S(2)}) copy-start(f32[64,128]{1,0:T(8,128)} %interact_ref.1) | copy-start | bytes 98308

commit v3 on v2

v3 whole, which is shorter than its diff:
```python
import math

import jax
import jax.numpy as jnp
from jax import lax
from jax.experimental import pallas as pl
from jax.experimental.pallas import tpu as pltpu
from jax.sharding import PartitionSpec as P

WORD_BITS = 32


def multiply(left, right):
    return jnp.dot(left, right, preferred_element_type=jnp.float32)


def one_hot(order_row, samples):
    rows = order_row.shape[1]
    pick = lax.broadcasted_iota(jnp.int32, (samples, rows), 0) == order_row
    return jnp.where(pick, 1.0, 0.0).astype(jnp.bfloat16)


def select_ids(ids, picks, residues):
    feats, bag, samples = ids.shape
    shift = residues.bit_length() - 1
    flat = ids.reshape(feats * bag, samples)
    low = (flat & (residues - 1)).astype(jnp.float32).astype(jnp.bfloat16)
    high = (flat >> shift).astype(jnp.float32).astype(jnp.bfloat16)
    both = multiply(jnp.concatenate([low, high], axis=0), picks).astype(jnp.int32)
    return both[: feats * bag, :], jnp.left_shift(1, both[feats * bag :, :])


def bit_planes(hits):
    waiting = []

    def push(level, bits):
        if level == len(waiting):
            waiting.append([])
        queue = waiting[level]
        queue.append(bits)
        if len(queue) == 3:
            first, second, third = queue
            both = first ^ second
            waiting[level] = [both ^ third]
            push(level + 1, (first & second) | (both & third))

    for bits in hits:
        push(0, bits)
    level = 0
    while level < len(waiting):
        if len(waiting[level]) == 2:
            first, second = waiting[level]
            waiting[level] = [first ^ second]
            push(level + 1, first & second)
        level += 1
    return [queue[0] for queue in waiting]


def merge(low, high, width, mask, second):
    shift = width if second else 0
    low = (low >> shift) & mask if low is not None else None
    if high is None:
        return low
    high = ((high >> shift) & mask) << width
    return high if low is None else low | high


def byte_fields(planes):
    planes = planes + [None] * (8 - len(planes))
    pairs = [
        [merge(planes[p], planes[p + 1], 1, 0x55555555, odd) for odd in (0, 1)]
        for p in range(0, 8, 2)
    ]
    fours = [
        [[merge(pairs[p][a], pairs[p + 1][a], 2, 0x33333333, odd) for odd in (0, 1)] for a in (0, 1)]
        for p in (0, 2)
    ]
    return [
        merge(fours[0][i & 1][(i >> 1) & 1], fours[1][i & 1][(i >> 1) & 1], 4, 0x0F0F0F0F, i >> 2)
        for i in range(8)
    ]


def count_ids(residue_ref, weight_ref, base, bag, active):
    residues = active // WORD_BITS
    spots = lax.broadcasted_iota(jnp.int32, (residues, residue_ref.shape[1]), 0)
    hits = (
        jnp.where(residue_ref[pl.ds(at, 1), :] == spots, weight_ref[pl.ds(at, 1), :], 0)
        for at in range(base, base + bag)
    )
    words = jnp.concatenate(byte_fields(bit_planes(hits)), axis=0).T
    return jnp.concatenate(
        [
            ((words >> (8 * place)) & 255).astype(jnp.float32).astype(jnp.bfloat16)
            for place in range(4)
        ],
        axis=1,
    )


def pool_feature(residue_ref, weight_ref, base, bag, table):
    counts = count_ids(residue_ref, weight_ref, base, bag, table.shape[0])
    return multiply(counts, table).astype(jnp.bfloat16)


def pick_ids(targets, ids, order_ref, active):
    picks = [one_hot(order_ref[pl.ds(target, 1), :], ids.shape[2]) for target in targets]
    return select_ids(ids, jnp.concatenate(picks, axis=1), active // WORD_BITS)


def block_of(chips_on, core_flip, devices):
    return lax.rem((lax.axis_index("dev") ^ core_flip) + 2 * chips_on, devices)


def start_copies(source, target, sem, parts):
    size = source.shape[0] // parts
    for part in range(parts):
        here = pl.ds(part * size, size)
        pltpu.make_async_copy(source.at[here], target.at[here], sem).start()
    return pltpu.make_async_copy(source, target, sem)


def first_kernel(
    blocks, order_hbm, ids_hbm, tables_hbm, w_hbm,
    out_ref, order_ref, ids_ref, tables_ref, w_ref, residues_ref, weights_ref,
    residue_ref, weight_ref, sems,
):
    devices, rows = order_hbm.shape
    feats, bag, samples = ids_hbm.shape
    active, emb = tables_hbm.shape[1:]
    order_here = start_copies(order_hbm, order_ref, sems.at[0], 1)
    ids_here = start_copies(ids_hbm, ids_ref, sems.at[1], feats)
    tables_here = start_copies(tables_hbm, tables_ref, sems.at[2], feats)
    w_here = start_copies(w_hbm, w_ref, sems.at[3], 2 * feats)
    order_here.wait()
    ids_here.wait()
    for block, chips_on in enumerate(blocks):
        residue, weight = pick_ids(
            (block_of(chips_on, 1, devices), block_of(chips_on, 0, devices)),
            ids_ref[...], order_ref, active,
        )
        residue_ref[...], weight_ref[...] = residue[:, :rows], weight[:, :rows]
        residues_ref[block], weights_ref[block] = residue[:, rows:], weight[:, rows:]
        if block == 0:
            tables_here.wait()
        for feature in range(feats):
            out_ref[block * rows : (block + 1) * rows, feature * emb : (feature + 1) * emb] = (
                pool_feature(residue_ref, weight_ref, feature * bag, bag, tables_ref[feature])
            )
    w_here.wait()


def pool_kernel(order_ref, ids_ref, tables_ref, after_hbm, out_ref, residue_ref, weight_ref):
    feats, bag, samples = ids_ref.shape
    active, emb = tables_ref.shape[1:]
    residue_ref[...], weight_ref[...] = pick_ids(
        (block_of(0, 1, order_ref.shape[0]),), ids_ref[...], order_ref, active
    )
    for feature in range(feats):
        out_ref[:, feature * emb : (feature + 1) * emb] = pool_feature(
            residue_ref, weight_ref, feature * bag, bag, tables_ref[feature]
        )


def layer_block(residue_ref, weight_ref, bag, tables_ref, w_ref):
    feats, active, emb = tables_ref.shape
    total = None
    for first in range(0, feats, 2):
        some = range(first, min(first + 2, feats))
        pooled = [
            pool_feature(residue_ref, weight_ref, feature * bag, bag, tables_ref[feature])
            for feature in some
        ]
        part = multiply(
            jnp.concatenate(pooled, axis=1), w_ref[first * emb : (first + len(some)) * emb, :]
        )
        total = part if total is None else total + part
    return total


def away_kernel(residues_ref, weights_ref, tables_ref, w_ref, out_ref):
    count, picked, rows = residues_ref.shape
    bag = picked // tables_ref.shape[0]
    for block in range(count):
        out_ref[block * rows : (block + 1) * rows, :] = layer_block(
            residues_ref.at[block], weights_ref.at[block], bag, tables_ref, w_ref
        )


def home_kernel(
    order_ref, ids_ref, tables_ref, w_ref, after_hbm, out_ref, residue_ref, weight_ref
):
    feats, bag, samples = ids_ref.shape
    residue_ref[...], weight_ref[...] = pick_ids(
        (block_of(0, 0, order_ref.shape[0]),), ids_ref[...], order_ref, tables_ref.shape[1]
    )
    out_ref[...] = layer_block(residue_ref, weight_ref, bag, tables_ref, w_ref)


IN_HBM = pl.BlockSpec(memory_space=pltpu.HBM)
ON_CHIP = pl.BlockSpec(memory_space=pltpu.VMEM)
ANYWHERE = pl.BlockSpec(memory_space=pl.ANY)
VMEM_LIMIT = 16 * 1024 * 1024


def in_hbm(*arrays):
    return [pltpu.with_memory_space_constraint(array, pltpu.HBM) for array in arrays]


def like(array):
    return jax.ShapeDtypeStruct(array.shape, array.dtype)


def picked(ids, rows):
    return [pltpu.VMEM((ids.shape[0] * ids.shape[1], rows), jnp.int32)] * 2


def options():
    return {
        "compiler_params": pltpu.CompilerParams(vmem_limit_bytes=VMEM_LIMIT),
        "cost_estimate": pl.CostEstimate(flops=1, bytes_accessed=1, transcendentals=0),
    }


def first_pool(blocks, order, ids, tables, w):
    rows = order.shape[1]
    feats, bag = ids.shape[:2]
    chosen = jax.ShapeDtypeStruct((len(blocks), feats * bag, rows), jnp.int32)
    return pl.pallas_call(
        lambda *refs: first_kernel(blocks, *refs),
        out_shape=(
            jax.ShapeDtypeStruct((len(blocks) * rows, feats * tables.shape[2]), jnp.bfloat16),
            like(order), like(ids), like(tables), like(w), chosen, chosen,
        ),
        in_specs=[IN_HBM] * 4,
        out_specs=(ON_CHIP,) * 7,
        scratch_shapes=picked(ids, rows) + [pltpu.SemaphoreType.DMA((4,))],
        name="first_pool",
        **options(),
    )(*in_hbm(order, ids, tables, w))


def away_layer(residues, weights, tables, w):
    return pl.pallas_call(
        away_kernel,
        out_shape=jax.ShapeDtypeStruct((residues.shape[0] * residues.shape[2], w.shape[1]), jnp.float32),
        in_specs=[ON_CHIP] * 4,
        out_specs=ON_CHIP,
        name="away_layer",
        **options(),
    )(residues, weights, tables, w)


def home_pool(order, ids, tables, after):
    rows = order.shape[1]
    return pl.pallas_call(
        pool_kernel,
        out_shape=jax.ShapeDtypeStruct((rows, ids.shape[0] * tables.shape[2]), jnp.bfloat16),
        in_specs=[ON_CHIP] * 3 + [ANYWHERE],
        out_specs=ON_CHIP,
        scratch_shapes=picked(ids, rows),
        name="home_pool",
        **options(),
    )(order, ids, tables, after)


def home_layer(order, ids, tables, w, after):
    rows = order.shape[1]
    return pl.pallas_call(
        home_kernel,
        out_shape=jax.ShapeDtypeStruct((rows, w.shape[1]), jnp.float32),
        in_specs=[ON_CHIP] * 4 + [ANYWHERE],
        out_specs=ON_CHIP,
        scratch_shapes=picked(ids, rows),
        name="home_layer",
        **options(),
    )(order, ids, tables, w, after)


def fetch_kernel(head_hbm, interact_hbm, after_hbm, head_ref, interact_ref, sems):
    copies = (
        start_copies(head_hbm, head_ref, sems.at[0], 8),
        start_copies(interact_hbm, interact_ref, sems.at[1], 1),
    )
    for copy in copies:
        copy.wait()


def fetch_head(head, interact, after):
    return pl.pallas_call(
        fetch_kernel,
        out_shape=(like(head), like(interact)),
        in_specs=[IN_HBM] * 2 + [ANYWHERE],
        out_specs=(ON_CHIP,) * 2,
        scratch_shapes=[pltpu.SemaphoreType.DMA((2,))],
        name="fetch_head",
        **options(),
    )(*in_hbm(head, interact), after)


def join_kernel(partial_ref, pooled_ref, w_ref, out_ref):
    out_ref[...] = (partial_ref[...] + multiply(pooled_ref[...], w_ref[...])).astype(out_ref.dtype)


def join(partial, pooled, w, kind):
    return pl.pallas_call(
        join_kernel,
        out_shape=jax.ShapeDtypeStruct(partial.shape, kind),
        in_specs=[ON_CHIP] * 3,
        out_specs=ON_CHIP,
        name="join",
        **options(),
    )(partial, pooled, w)


def second_kernel(w_ref, preact_ref, *refs):
    *received_refs, out_ref = refs
    preact = preact_ref[...]
    for received_ref in received_refs:
        preact = preact + received_ref[...].astype(jnp.float32)
    hidden = jnp.maximum(preact, 0.0).astype(jnp.bfloat16)
    out_ref[...] = multiply(hidden, w_ref[...]).astype(out_ref.dtype)


def second_layer(w, preact, received):
    return pl.pallas_call(
        second_kernel,
        out_shape=jax.ShapeDtypeStruct((preact.shape[0], w.shape[1]), jnp.bfloat16),
        in_specs=[ON_CHIP] * (2 + len(received)),
        out_specs=ON_CHIP,
        name="second_layer",
        **options(),
    )(w, preact, *received)


def score_kernel(outputs_ref, head_ref, interact_ref, scores_ref):
    towers, rows, width = outputs_ref.shape
    me = lax.axis_index("tower")
    outputs = [outputs_ref[me ^ t] for t in range(towers)]
    wide = jnp.concatenate(outputs, axis=1)
    scores = multiply(wide, head_ref[...])
    interact = interact_ref[...] * (1.0 / math.sqrt(width))
    for t in range(towers):
        mine = outputs[t].astype(jnp.float32)
        for s in range(t, towers):
            gram = jnp.sum(mine * outputs[s].astype(jnp.float32), axis=1, keepdims=True)
            weights = interact[t * towers + s : t * towers + s + 1, :]
            if s != t:
                weights = weights + interact[s * towers + t : s * towers + t + 1, :]
            scores = scores + gram * weights
    scores_ref[...] = scores


def score(outputs, head, interact):
    towers, rows, width = outputs.shape
    return pl.pallas_call(
        score_kernel,
        out_shape=jax.ShapeDtypeStruct((rows, head.shape[1]), jnp.float32),
        in_specs=[ON_CHIP] * 3,
        out_specs=ON_CHIP,
        compiler_params=pltpu.CompilerParams(vmem_limit_bytes=VMEM_LIMIT),
        name="score",
    )(outputs, head, interact)


def exchange(blocks):
    towers, rows, width = blocks.shape
    me = lax.axis_index("tower")
    if towers & (towers - 1):
        gathered = lax.all_to_all(blocks, "tower", split_axis=0, concat_axis=0, tiled=True)
        return jnp.take(gathered, me ^ jnp.arange(towers), axis=0)
    held = blocks
    low = 1
    while low < towers:
        group = min(4, towers // low)
        split = held.reshape(held.shape[0] // group, group, *held.shape[1:])
        place = lax.rem(me // low, group)
        parts = [lax.dynamic_index_in_dim(split, place, 1, keepdims=False)]
        for k in range(1, group):
            part = lax.dynamic_index_in_dim(split, place ^ k, 1, keepdims=False)
            parts.append(lax.ppermute(part, "tower", [(i, i ^ (k * low)) for i in range(towers)]))
        held = jnp.stack(parts, axis=1).reshape(split.shape[0], group * held.shape[1], width)
        low *= group
    return held.reshape(towers, rows, width)


def on_device(ids, tables, order, w_first, w_second, w_head, w_interact):
    towers = lax.axis_size("tower")
    devices = lax.axis_size("dev")
    samples = ids.shape[2]
    my_rows = samples // devices
    order = order.reshape(devices, my_rows)
    ids, tables, w_first = jnp.swapaxes(ids[0], 1, 2), tables[0], w_first[0]

    def swap_cores(array):
        return lax.ppermute(array, "dev", [(i, i ^ 1) for i in range(devices)])

    w_other = swap_cores(w_first)
    away = tuple(range(1, devices // 2))
    pooled, order, ids, tables, w_first, residues, weights = first_pool(
        away, order, ids, tables, w_first
    )
    pooled = swap_cores(pooled)
    partial = away_layer(residues, weights, tables, w_first)
    partial = join(partial, pooled, w_other, jnp.bfloat16)
    received = []
    for k in away:
        received.append(
            lax.ppermute(
                partial[(k - 1) * my_rows : k * my_rows],
                "dev",
                [(i, (i + 2 * k) % devices) for i in range(devices)],
            )
        )
    pooled = swap_cores(home_pool(order, ids, tables, partial))
    preact = home_layer(order, ids, tables, w_first, partial)
    preact = join(preact, pooled, w_other, jnp.float32)
    w_head, w_interact = fetch_head(w_head, w_interact, preact)
    outputs = second_layer(w_second[0], preact, received)
    gathered = exchange(outputs.reshape(towers, my_rows // towers, outputs.shape[1]))
    return score(gathered, w_head, w_interact)[None]


def solution(mesh):
    return jax.shard_map(
        on_device,
        mesh=mesh,
        in_specs=(
            P("tower", "dev", None, None),
            P("tower", "dev", None, None),
            P(),
            P("tower", "dev", None),
            P("tower", None, None),
            P(),
            P(),
        ),
        out_specs=P("dev", "tower", None),
        check_vma=False,
    )
```

time: 28.7 us -> 27.5 us (0.958)
  blocking collectives: 13.2 us -> 0 us
  waiting for transfers between devices: 2.79 us -> 9.1 us
  starting transfers between devices: 3.67 us -> 9.6 us
  matrix products: 0.63 us -> 0 us
  Pallas kernels: 8.11 us -> 8.48 us
    all_to_all x1 -> x0, blocking collectives: 13.2 us -> none  [on_device(): lax.all_to_all(outputs.reshape(1, towers, share, width), 'tower', split_a...]
    ppermute x0 -> x4, starting transfers between devices: none -> 6.21 us  [exchange(): lax.ppermute(part, 'tower', [(i, i ^ k * low) for i in range(towers)])]
    ppermute x0 -> x4, waiting for transfers between devices: none -> 4.87 us  [exchange(): lax.ppermute(part, 'tower', [(i, i ^ k * low) for i in range(towers)])]
    ppermute x3, waiting for transfers between devices: 0.01 us -> 0.79 us  [swap_cores(): return lax.ppermute(array, 'dev', [(i, i ^ 1) for i in range(devices)])]
    ppermute x1, waiting for transfers between devices: 2.78 us -> 3.45 us  [on_device(): lax.ppermute(partial[(k - 1) * my_rows:k * my_rows], 'dev', [(i, (i + 2 *...]
    dot_general x2 -> x0, matrix products: 0.63 us -> none  [multiply(): return jnp.dot(left, right, preferred_element_type=jnp.float32)]
    pallas_call x4 -> x7, Pallas kernels: 5.07 us -> 5.69 us  [the longest x1 1.49 us: home_pool(): pl.pallas_call(pool_kernel, out_shape=jax.ShapeDtypeStruct((rows, ids.sha...]
  transfers between devices with their start and end apart: 4 -> 8, of which waited for: 1 -> 7; matrix products, arithmetic and copies ran while one was open for 0% -> 0% of each run, Pallas kernels for 25% -> 25%
where the time goes in v3:
time: 27.5 us; the launch traced here: 27.4 us
  starting transfers between devices  9.6 us (35%)
  waiting for transfers between devices  9.1 us (33%)
  Pallas kernels  8.48 us (31%)
    ppermute x4, starting transfers between devices, exchange(): lax.ppermute(part, 'tower', [(i, i ^ k * low) for i in range(towers)])  6.21 us
    ppermute x4, waiting for transfers between devices, exchange(): lax.ppermute(part, 'tower', [(i, i ^ k * low) for i in range(towers)])  4.87 us
    ppermute x1, waiting for transfers between devices, on_device(): lax.ppermute(partial[(k - 1) * my_rows:k * my_rows], 'dev', [(i, (i + 2 *...  3.45 us
    ppermute x1, starting transfers between devices, on_device(): lax.ppermute(partial[(k - 1) * my_rows:k * my_rows], 'dev', [(i, (i + 2 *...  2.74 us
    pallas_call x1, Pallas kernels, first_pool(): pl.pallas_call(lambda *refs: first_kernel(blocks, *refs), out_shape=(jax....  1.9 us
    pallas_call x1, Pallas kernels, home_pool(): pl.pallas_call(pool_kernel, out_shape=jax.ShapeDtypeStruct((rows, ids.sha...  1.49 us
    pallas_call x1, Pallas kernels, fetch_head(): pl.pallas_call(fetch_kernel, out_shape=(like(head), like(interact)), in_s...  1.3 us
    pallas_call x1, Pallas kernels, home_layer(): pl.pallas_call(home_kernel, out_shape=jax.ShapeDtypeStruct((rows, w.shape...  1.09 us
  transfers between devices with their start and end apart: 8, of which 7 were waited for; matrix products, arithmetic and copies ran while one was open for 0% of the time, Pallas kernels for 25%

profile of v3, /device:TPU:0, one launch (start us, length us, event | category | flops | bytes accessed | tf_op | source)
XLA Modules:
  0.0 27.4 jit_solution(18431950120343664853)
XLA Ops:
  0.0 0.5 %collective-permute-start.1 = (bf16[512,1024]{1,0:T(8,128)(2,1)}, bf16[512,1024]{1,0:T(8,128)(2,1)S(1)}, u32[]{:S(2)}, u32[]{:S(2)}) collective-permute-start(bf16[512,1024]{1,0:T(8,128)(2,1)} %bitcast.26), channel_id=1, source_target_pairs={{0,1},{1,0},{2,3},{3,2},{4,5},{5,4},{6,7},{7,6},{8,9},{9,8},{10,11... | collective-permute-start | bytes 3145736 | tf_op jit(solution)/shard_map/ppermute | solution.py:396
  0.5 1.9 %first_pool.1 = (bf16[128,512]{1,0:T(8,128)(2,1)S(1)}, s32[4,128]{1,0:T(4,128)S(1)}, s32[4,32,512]{2,1,0:T(8,128)S(1)}, bf16[4,512,128]{2,1,0:T(8,128)(2,1)S(1)}...) custom-call(s32[4,128]{1,0:T(4,128)} %bitcast.35, s32[4,32,512]{2,1,0:T(8,128)} %bitcast.30, ...), custom_call_target="tpu_custom_call" | custom-call | flops 1 | bytes 1 | tf_op jit(solution)/shard_map/first_pool/pallas_call | solution.py:229
  2.4 0.1 collective-permute-start
  2.5 0.9 %away_layer.1.partial_ref = f32[128,1024]{1,0:T(8,128)S(1)} custom-call(s32[1,128,128]{2,1,0:T(8,128)S(1)} %get-tuple-element.18.residues_ref, s32[1,128,128]{2,1,0:T(8,128)S(1)} %get-tuple-element.19.weights_ref, bf16[4,512,128]{2,1,0:T(8,128)(2,1)S(1)} %get-tuple-element.16.tables_ref, bf16[512,1024]{1,0:T(8,128)(2,1)S(1)} %get-tuple-element.17.w_ref), custom_call_target="tpu_custom_call" | custom-call | flops 1 | bytes 1 | tf_op jit(solution)/shard_map/away_layer/pallas_call | solution.py:244
  3.4 0.4 %collective-permute-done.pooled_ref = bf16[128,512]{1,0:T(8,128)(2,1)S(1)} collective-permute-done((bf16[128,512]{1,0:T(8,128)(2,1)S(1)}, bf16[128,512]{1,0:T(8,128)(2,1)S(1)}, u32[]{:S(2)}, u32[]{:S(2)}) %collective-permute-start) | collective-permute-done | bytes 131104 | tf_op jit(solution)/shard_map/ppermute | solution.py:396
  3.8 0.0 collective-permute-done.1.w_ref
  3.8 0.3 %join.2.after_hbm = bf16[128,1024]{1,0:T(8,128)(2,1)S(1)} custom-call(f32[128,1024]{1,0:T(8,128)S(1)} %away_layer.1.partial_ref, bf16[128,512]{1,0:T(8,128)(2,1)S(1)} %collective-permute-done.pooled_ref, bf16[512,1024]{1,0:T(8,128)(2,1)S(1)} %collective-permute-done.1.w_ref), custom_call_target="tpu_custom_call" | custom-call | flops 1 | bytes 1 | tf_op jit(solution)/shard_map/join/pallas_call | solution.py:306
  4.1 2.7 %collective-permute-start.3 = (bf16[128,1024]{1,0:T(8,128)(2,1)S(1)}, bf16[128,1024]{1,0:T(8,128)(2,1)S(1)}, u32[]{:S(2)}, u32[]{:S(2)}) collective-permute-start(bf16[128,1024]{1,0:T(8,128)(2,1)S(1)} %join.2.after_hbm), channel_id=1, source_target_pairs={{0,2},{1,3},{2,0},{3,1},{4,6},{5,7},{6,4},{7,5},{8,10},{9,11},{10,... | collective-permute-start | bytes 786440 | tf_op jit(solution)/shard_map/ppermute | solution.py:409
  6.8 1.5 %home_pool.1 = bf16[128,512]{1,0:T(8,128)(2,1)} custom-call(s32[4,128]{1,0:T(4,128)S(1)} %get-tuple-element.14.order_ref, s32[4,32,512]{2,1,0:T(8,128)S(1)} %get-tuple-element.15.ids_ref, bf16[4,512,128]{2,1,0:T(8,128)(2,1)S(1)} %get-tuple-element.16.tables_ref, bf16[128,1024]{1,0:T(8,128)(2,1)S(1)} %join.2.after_hbm), custom_call_target="tpu_custom_call" | custom-call | flops 1 | bytes 1 | tf_op jit(solution)/shard_map/home_pool/pallas_call | solution.py:256
  8.3 0.1 collective-permute-start.2
  8.4 1.1 %home_layer.1.partial_ref = f32[128,1024]{1,0:T(8,128)S(1)} custom-call(s32[4,128]{1,0:T(4,128)S(1)} %get-tuple-element.14.order_ref, s32[4,32,512]{2,1,0:T(8,128)S(1)} %get-tuple-element.15.ids_ref, bf16[4,512,128]{2,1,0:T(8,128)(2,1)S(1)} %get-tuple-element.16.tables_ref, bf16[512,1024]{1,0:T(8,128)(2,1)S(1)} %get-tuple-element.17.w_ref, ...), custom_call_target="tpu_custom_call" | custom-call | flops 1 | bytes 1 | tf_op jit(solution)/shard_map/home_layer/pallas_call | solution.py:269
  9.5 0.0 copy-start
  9.5 0.4 %collective-permute-done.2.pooled_ref = bf16[128,512]{1,0:T(8,128)(2,1)S(1)} collective-permute-done((bf16[128,512]{1,0:T(8,128)(2,1)}, bf16[128,512]{1,0:T(8,128)(2,1)S(1)}, u32[]{:S(2)}, u32[]{:S(2)}) %collective-permute-start.2) | collective-permute-done | bytes 131104 | tf_op jit(solution)/shard_map/ppermute | solution.py:396
  9.9 0.3 %join.3.preact_ref.after_hbm = f32[128,1024]{1,0:T(8,128)S(1)} custom-call(f32[128,1024]{1,0:T(8,128)S(1)} %home_layer.1.partial_ref, bf16[128,512]{1,0:T(8,128)(2,1)S(1)} %collective-permute-done.2.pooled_ref, bf16[512,1024]{1,0:T(8,128)(2,1)S(1)} %collective-permute-done.1.w_ref), custom_call_target="tpu_custom_call" | custom-call | flops 1 | bytes 1 | tf_op jit(solution)/shard_map/join/pallas_call | solution.py:306
  10.2 3.4 %collective-permute-done.3.refs_0_ = bf16[128,1024]{1,0:T(8,128)(2,1)S(1)} collective-permute-done((bf16[128,1024]{1,0:T(8,128)(2,1)S(1)}, bf16[128,1024]{1,0:T(8,128)(2,1)S(1)}, u32[]{:S(2)}, u32[]{:S(2)}) %collective-permute-start.3) | collective-permute-done | bytes 262176 | tf_op jit(solution)/shard_map/ppermute | solution.py:409
  13.7 0.0 copy-done
  13.7 0.3 %second_layer.1 = bf16[128,512]{1,0:T(8,128)(2,1)S(1)} custom-call(bf16[1024,512]{1,0:T(8,128)(2,1)S(1)} %bitcast.23, f32[128,1024]{1,0:T(8,128)S(1)} %join.3.preact_ref.after_hbm, bf16[128,1024]{1,0:T(8,128)(2,1)S(1)} %collective-permute-done.3.refs_0_), custom_call_target="tpu_custom_call" | custom-call | flops 1 | bytes 1 | tf_op jit(solution)/shard_map/second_layer/pallas_call | solution.py:326
  14.0 2.8 %collective-permute-start.6 = (bf16[2,16,512]{2,1,0:T(8,128)(2,1)S(1)}, bf16[2,16,512]{2,1,0:T(8,128)(2,1)S(1)}, u32[]{:S(2)}, u32[]{:S(2)}) collective-permute-start(bf16[2,16,512]{2,1,0:T(8,128)(2,1)S(1)} %get-tuple-element.26), channel_id=1, source_target_pairs={{0,12},{4,8},{8,4},{12,0},{16,28},{20,24},{24,20},{28,16},{1,13},{... | collective-permute-start | bytes 98312 | tf_op jit(solution)/shard_map/ppermute | solution.py:381
  16.8 0.4 %collective-permute-start.5 = (bf16[2,16,512]{2,1,0:T(8,128)(2,1)S(1)}, bf16[2,16,512]{2,1,0:T(8,128)(2,1)S(1)}, u32[]{:S(2)}, u32[]{:S(2)}) collective-permute-start(bf16[2,16,512]{2,1,0:T(8,128)(2,1)S(1)} %get-tuple-element.27), channel_id=1, source_target_pairs={{0,8},{4,12},{8,0},{12,4},{16,24},{20,28},{24,16},{28,20},{1,9},{5... | collective-permute-start | bytes 98312 | tf_op jit(solution)/shard_map/ppermute | solution.py:381
  17.2 0.3 %collective-permute-start.4 = (bf16[2,16,512]{2,1,0:T(8,128)(2,1)S(1)}, bf16[2,16,512]{2,1,0:T(8,128)(2,1)S(1)}, u32[]{:S(2)}, u32[]{:S(2)}) collective-permute-start(bf16[2,16,512]{2,1,0:T(8,128)(2,1)S(1)} %get-tuple-element.28), channel_id=1, source_target_pairs={{0,4},{4,0},{8,12},{12,8},{16,20},{20,16},{24,28},{28,24},{1,5},{5... | collective-permute-start | bytes 98312 | tf_op jit(solution)/shard_map/ppermute | solution.py:381
  17.6 1.6 %collective-permute-done.6 = bf16[2,16,512]{2,1,0:T(8,128)(2,1)S(1)} collective-permute-done((bf16[2,16,512]{2,1,0:T(8,128)(2,1)S(1)}, bf16[2,16,512]{2,1,0:T(8,128)(2,1)S(1)}, u32[]{:S(2)}, u32[]{:S(2)}) %collective-permute-start.6) | collective-permute-done | bytes 32800 | tf_op jit(solution)/shard_map/ppermute | solution.py:381
  19.1 1.6 %collective-permute-done.5 = bf16[2,16,512]{2,1,0:T(8,128)(2,1)S(1)} collective-permute-done((bf16[2,16,512]{2,1,0:T(8,128)(2,1)S(1)}, bf16[2,16,512]{2,1,0:T(8,128)(2,1)S(1)}, u32[]{:S(2)}, u32[]{:S(2)}) %collective-permute-start.5) | collective-permute-done | bytes 32800 | tf_op jit(solution)/shard_map/ppermute | solution.py:381
  20.7 0.4 %collective-permute-done.4 = bf16[2,16,512]{2,1,0:T(8,128)(2,1)S(1)} collective-permute-done((bf16[2,16,512]{2,1,0:T(8,128)(2,1)S(1)}, bf16[2,16,512]{2,1,0:T(8,128)(2,1)S(1)}, u32[]{:S(2)}, u32[]{:S(2)}) %collective-permute-start.4) | collective-permute-done | bytes 32800 | tf_op jit(solution)/shard_map/ppermute | solution.py:381
  21.2 2.7 %collective-permute-start.7 = (bf16[1,64,512]{2,1,0:T(8,128)(2,1)S(1)}, bf16[1,64,512]{2,1,0:T(8,128)(2,1)S(1)}, u32[]{:S(2)}, u32[]{:S(2)}) collective-permute-start(bf16[1,64,512]{2,1,0:T(8,128)(2,1)S(1)} %get-tuple-element.24), channel_id=1, source_target_pairs={{0,16},{4,20},{8,24},{12,28},{16,0},{20,4},{24,8},{28,12},{1,17},{... | collective-permute-start | bytes 196616 | tf_op jit(solution)/shard_map/ppermute | solution.py:381
  23.9 1.3 %fetch_head.1 = (bf16[4096,128]{1,0:T(8,128)(2,1)S(1)}, f32[64,128]{1,0:T(8,128)S(1)}) custom-call(bf16[4096,128]{1,0:T(8,128)(2,1)} %head_hbm.1, f32[64,128]{1,0:T(8,128)} %interact_hbm.1, f32[128,1024]{1,0:T(8,128)S(1)} %join.3.preact_ref.after_hbm), custom_call_target="tpu_custom_call" | custom-call | flops 1 | bytes 1 | tf_op jit(solution)/shard_map/fetch_head/pallas_call | solution.py:290
  25.2 1.3 %collective-permute-done.7 = bf16[1,64,512]{2,1,0:T(8,128)(2,1)S(1)} collective-permute-done((bf16[1,64,512]{2,1,0:T(8,128)(2,1)S(1)}, bf16[1,64,512]{2,1,0:T(8,128)(2,1)S(1)}, u32[]{:S(2)}, u32[]{:S(2)}) %collective-permute-start.7) | collective-permute-done | bytes 65568 | tf_op jit(solution)/shard_map/ppermute | solution.py:381
  26.5 0.9 %score.1 = f32[16,128]{1,0:T(8,128)} custom-call(bf16[8,16,512]{2,1,0:T(8,128)(2,1)S(1)} %bitcast.24, bf16[4096,128]{1,0:T(8,128)(2,1)S(1)} %get-tuple-element.21.head_ref, f32[64,128]{1,0:T(8,128)S(1)} %get-tuple-element.22.interact_ref), custom_call_target="tpu_custom_call" | custom-call | tf_op jit(solution)/shard_map/score/pallas_call | solution.py:356
  (4 shorter events, 0.1 us)
Async XLA Ops:
  0.0 3.8 %collective-permute-start.1 = (bf16[512,1024]{1,0:T(8,128)(2,1)}, bf16[512,1024]{1,0:T(8,128)(2,1)S(1)}, u32[]{:S(2)}, u32[]{:S(2)}) collective-permute-start(bf16[512,1024]{1,0:T(8,128)(2,1)} %bitcast.26), channel_id=1, source_target_pairs={{0,1},{1,0},{2,3},{3,2},{4,5},{5,4},{6,7},{7,6},{8,9},{9,8},{10,11... | collective-permute-start | bytes 3145736 | tf_op jit(solution)/shard_map/ppermute | solution.py:396
  2.4 1.4 %collective-permute-start = (bf16[128,512]{1,0:T(8,128)(2,1)S(1)}, bf16[128,512]{1,0:T(8,128)(2,1)S(1)}, u32[]{:S(2)}, u32[]{:S(2)}) collective-permute-start(bf16[128,512]{1,0:T(8,128)(2,1)S(1)} %get-tuple-element.20), channel_id=1, source_target_pairs={{0,1},{1,0},{2,3},{3,2},{4,5},{5,4},{6,7},{7,6},{8,9},{9,8},{10,11... | collective-permute-start | bytes 393224 | tf_op jit(solution)/shard_map/ppermute | solution.py:396
  4.1 9.6 %collective-permute-start.3 = (bf16[128,1024]{1,0:T(8,128)(2,1)S(1)}, bf16[128,1024]{1,0:T(8,128)(2,1)S(1)}, u32[]{:S(2)}, u32[]{:S(2)}) collective-permute-start(bf16[128,1024]{1,0:T(8,128)(2,1)S(1)} %join.2.after_hbm), channel_id=1, source_target_pairs={{0,2},{1,3},{2,0},{3,1},{4,6},{5,7},{6,4},{7,5},{8,10},{9,11},{10,... | collective-permute-start | bytes 786440 | tf_op jit(solution)/shard_map/ppermute | solution.py:409
  8.3 1.6 %collective-permute-start.2 = (bf16[128,512]{1,0:T(8,128)(2,1)}, bf16[128,512]{1,0:T(8,128)(2,1)S(1)}, u32[]{:S(2)}, u32[]{:S(2)}) collective-permute-start(bf16[128,512]{1,0:T(8,128)(2,1)} %home_pool.1), channel_id=1, source_target_pairs={{0,1},{1,0},{2,3},{3,2},{4,5},{5,4},{6,7},{7,6},{8,9},{9,8},{10,11... | collective-permute-start | bytes 393224 | tf_op jit(solution)/shard_map/ppermute | solution.py:396
  9.5 4.2 %copy-start = (bf16[1,1024,512]{2,1,0:T(8,128)(2,1)S(1)}, bf16[1,1024,512]{2,1,0:T(8,128)(2,1)}, u32[]{:S(2)}) copy-start(bf16[1,1024,512]{2,1,0:T(8,128)(2,1)} %param.11) | copy-start | bytes 3145732
  14.0 5.1 %collective-permute-start.6 = (bf16[2,16,512]{2,1,0:T(8,128)(2,1)S(1)}, bf16[2,16,512]{2,1,0:T(8,128)(2,1)S(1)}, u32[]{:S(2)}, u32[]{:S(2)}) collective-permute-start(bf16[2,16,512]{2,1,0:T(8,128)(2,1)S(1)} %get-tuple-element.26), channel_id=1, source_target_pairs={{0,12},{4,8},{8,4},{12,0},{16,28},{20,24},{24,20},{28,16},{1,13},{... | collective-permute-start | bytes 98312 | tf_op jit(solution)/shard_map/ppermute | solution.py:381
  16.8 3.9 %collective-permute-start.5 = (bf16[2,16,512]{2,1,0:T(8,128)(2,1)S(1)}, bf16[2,16,512]{2,1,0:T(8,128)(2,1)S(1)}, u32[]{:S(2)}, u32[]{:S(2)}) collective-permute-start(bf16[2,16,512]{2,1,0:T(8,128)(2,1)S(1)} %get-tuple-element.27), channel_id=1, source_target_pairs={{0,8},{4,12},{8,0},{12,4},{16,24},{20,28},{24,16},{28,20},{1,9},{5... | collective-permute-start | bytes 98312 | tf_op jit(solution)/shard_map/ppermute | solution.py:381
  17.2 3.9 %collective-permute-start.4 = (bf16[2,16,512]{2,1,0:T(8,128)(2,1)S(1)}, bf16[2,16,512]{2,1,0:T(8,128)(2,1)S(1)}, u32[]{:S(2)}, u32[]{:S(2)}) collective-permute-start(bf16[2,16,512]{2,1,0:T(8,128)(2,1)S(1)} %get-tuple-element.28), channel_id=1, source_target_pairs={{0,4},{4,0},{8,12},{12,8},{16,20},{20,16},{24,28},{28,24},{1,5},{5... | collective-permute-start | bytes 98312 | tf_op jit(solution)/shard_map/ppermute | solution.py:381
  21.2 5.2 %collective-permute-start.7 = (bf16[1,64,512]{2,1,0:T(8,128)(2,1)S(1)}, bf16[1,64,512]{2,1,0:T(8,128)(2,1)S(1)}, u32[]{:S(2)}, u32[]{:S(2)}) collective-permute-start(bf16[1,64,512]{2,1,0:T(8,128)(2,1)S(1)} %get-tuple-element.24), channel_id=1, source_target_pairs={{0,16},{4,20},{8,24},{12,28},{16,0},{20,4},{24,8},{28,12},{1,17},{... | collective-permute-start | bytes 196616 | tf_op jit(solution)/shard_map/ppermute | solution.py:381

commit v4 on v3

--- a/solution.py
+++ b/solution.py
@@ -103,9 +103,13 @@
     return multiply(counts, table).astype(jnp.bfloat16)
 
 
+def pick_rows(targets, order_ref, samples):
+    picks = [one_hot(order_ref[pl.ds(target, 1), :], samples) for target in targets]
+    return jnp.concatenate(picks, axis=1)
+
+
 def pick_ids(targets, ids, order_ref, active):
-    picks = [one_hot(order_ref[pl.ds(target, 1), :], ids.shape[2]) for target in targets]
-    return select_ids(ids, jnp.concatenate(picks, axis=1), active // WORD_BITS)
+    return select_ids(ids, pick_rows(targets, order_ref, ids.shape[2]), active // WORD_BITS)
 
 
 def block_of(chips_on, core_flip, devices):
@@ -123,22 +127,25 @@
 def first_kernel(
     blocks, order_hbm, ids_hbm, tables_hbm, w_hbm,
     out_ref, order_ref, ids_ref, tables_ref, w_ref, residues_ref, weights_ref,
-    residue_ref, weight_ref, sems,
+    residue_ref, weight_ref, picks_ref, sems,
 ):
     devices, rows = order_hbm.shape
     feats, bag, samples = ids_hbm.shape
     active, emb = tables_hbm.shape[1:]
     order_here = start_copies(order_hbm, order_ref, sems.at[0], 1)
-    ids_here = start_copies(ids_hbm, ids_ref, sems.at[1], feats)
-    tables_here = start_copies(tables_hbm, tables_ref, sems.at[2], feats)
-    w_here = start_copies(w_hbm, w_ref, sems.at[3], 2 * feats)
+    ids_here = start_copies(ids_hbm, ids_ref, sems.at[1], 1)
+    tables_here = start_copies(tables_hbm, tables_ref, sems.at[2], 1)
+    w_here = start_copies(w_hbm, w_ref, sems.at[3], 2)
     order_here.wait()
-    ids_here.wait()
     for block, chips_on in enumerate(blocks):
-        residue, weight = pick_ids(
-            (block_of(chips_on, 1, devices), block_of(chips_on, 0, devices)),
-            ids_ref[...], order_ref, active,
-        )
+        picks = pick_rows(
+            (block_of(chips_on, 1, devices), block_of(chips_on, 0, devices)), order_ref, samples
+        )
+        if block == 0:
+            picks_ref[...] = picks
+            ids_here.wait()
+            picks = picks_ref[...]
+        residue, weight = select_ids(ids_ref[...], picks, active // WORD_BITS)
         residue_ref[...], weight_ref[...] = residue[:, :rows], weight[:, :rows]
         residues_ref[block], weights_ref[block] = residue[:, rows:], weight[:, rows:]
         if block == 0:
@@ -148,18 +155,6 @@
                 pool_feature(residue_ref, weight_ref, feature * bag, bag, tables_ref[feature])
             )
     w_here.wait()
-
-
-def pool_kernel(order_ref, ids_ref, tables_ref, after_hbm, out_ref, residue_ref, weight_ref):
-    feats, bag, samples = ids_ref.shape
-    active, emb = tables_ref.shape[1:]
-    residue_ref[...], weight_ref[...] = pick_ids(
-        (block_of(0, 1, order_ref.shape[0]),), ids_ref[...], order_ref, active
-    )
-    for feature in range(feats):
-        out_ref[:, feature * emb : (feature + 1) * emb] = pool_feature(
-            residue_ref, weight_ref, feature * bag, bag, tables_ref[feature]
-        )
 
 
 def layer_block(residue_ref, weight_ref, bag, tables_ref, w_ref):
@@ -187,14 +182,53 @@
         )
 
 
-def home_kernel(
-    order_ref, ids_ref, tables_ref, w_ref, after_hbm, out_ref, residue_ref, weight_ref
+def home_rows(order_ref, ids_ref, tables_ref, w_ref, pooled_ref, out_ref, residue_ref, weight_ref):
+    devices, rows = order_ref.shape
+    feats, bag, samples = ids_ref.shape
+    active, emb = tables_ref.shape[1:]
+    residue, weight = pick_ids(
+        (block_of(0, 1, devices), block_of(0, 0, devices)), ids_ref[...], order_ref, active
+    )
+    residue_ref[...], weight_ref[...] = residue, weight
+    other, mine = slice(0, rows), slice(rows, 2 * rows)
+    for feature in range(feats):
+        pooled_ref[:, feature * emb : (feature + 1) * emb] = pool_feature(
+            residue_ref.at[:, other], weight_ref.at[:, other], feature * bag, bag, tables_ref[feature]
+        )
+    out_ref[...] = layer_block(
+        residue_ref.at[:, mine], weight_ref.at[:, mine], bag, tables_ref, w_ref
+    )
+
+
+def early_kernel(
+    order_ref, ids_ref, tables_ref, w_ref, partial_ref,
+    pooled_ref, out_ref, again_ref, residue_ref, weight_ref,
 ):
-    feats, bag, samples = ids_ref.shape
-    residue_ref[...], weight_ref[...] = pick_ids(
-        (block_of(0, 0, order_ref.shape[0]),), ids_ref[...], order_ref, tables_ref.shape[1]
-    )
-    out_ref[...] = layer_block(residue_ref, weight_ref, bag, tables_ref, w_ref)
+    @pl.when(lax.axis_index("dev") % 2 == 1)
+    def _():
+        home_rows(
+            order_ref, ids_ref, tables_ref, w_ref, pooled_ref, out_ref, residue_ref, weight_ref
+        )
+
+    again_ref[...] = partial_ref[...]
+
+
+def late_kernel(
+    order_ref, ids_ref, tables_ref, w_ref, pooled_in_ref, in_ref, after_hbm,
+    pooled_ref, out_ref, residue_ref, weight_ref,
+):
+    second = lax.axis_index("dev") % 2 == 1
+
+    @pl.when(second)
+    def _():
+        pooled_ref[...] = pooled_in_ref[...]
+        out_ref[...] = in_ref[...]
+
+    @pl.when(jnp.logical_not(second))
+    def _():
+        home_rows(
+            order_ref, ids_ref, tables_ref, w_ref, pooled_ref, out_ref, residue_ref, weight_ref
+        )
 
 
 IN_HBM = pl.BlockSpec(memory_space=pltpu.HBM)
@@ -234,7 +268,8 @@
         ),
         in_specs=[IN_HBM] * 4,
         out_specs=(ON_CHIP,) * 7,
-        scratch_shapes=picked(ids, rows) + [pltpu.SemaphoreType.DMA((4,))],
+        scratch_shapes=picked(ids, rows)
+        + [pltpu.VMEM((ids.shape[2], 2 * rows), jnp.bfloat16), pltpu.SemaphoreType.DMA((4,))],
         name="first_pool",
         **options(),
     )(*in_hbm(order, ids, tables, w))
@@ -251,30 +286,36 @@
     )(residues, weights, tables, w)
 
 
-def home_pool(order, ids, tables, after):
+def home_shapes(order, ids, tables, w):
     rows = order.shape[1]
-    return pl.pallas_call(
-        pool_kernel,
-        out_shape=jax.ShapeDtypeStruct((rows, ids.shape[0] * tables.shape[2]), jnp.bfloat16),
-        in_specs=[ON_CHIP] * 3 + [ANYWHERE],
-        out_specs=ON_CHIP,
-        scratch_shapes=picked(ids, rows),
-        name="home_pool",
-        **options(),
-    )(order, ids, tables, after)
-
-
-def home_layer(order, ids, tables, w, after):
-    rows = order.shape[1]
-    return pl.pallas_call(
-        home_kernel,
-        out_shape=jax.ShapeDtypeStruct((rows, w.shape[1]), jnp.float32),
-        in_specs=[ON_CHIP] * 4 + [ANYWHERE],
-        out_specs=ON_CHIP,
-        scratch_shapes=picked(ids, rows),
-        name="home_layer",
-        **options(),
-    )(order, ids, tables, w, after)
+    return (
+        jax.ShapeDtypeStruct((rows, ids.shape[0] * tables.shape[2]), jnp.bfloat16),
+        jax.ShapeDtypeStruct((rows, w.shape[1]), jnp.float32),
+    )
+
+
+def home_early(order, ids, tables, w, partial):
+    return pl.pallas_call(
+        early_kernel,
+        out_shape=home_shapes(order, ids, tables, w) + (like(partial),),
+        in_specs=[ON_CHIP] * 5,
+        out_specs=(ON_CHIP,) * 3,
+        scratch_shapes=picked(ids, 2 * order.shape[1]),
+        name="home_early",
+        **options(),
+    )(order, ids, tables, w, partial)
+
+
+def home_late(order, ids, tables, w, pooled, preact, after):
+    return pl.pallas_call(
+        late_kernel,
+        out_shape=home_shapes(order, ids, tables, w),
+        in_specs=[ON_CHIP] * 6 + [ANYWHERE],
+        out_specs=(ON_CHIP,) * 2,
+        scratch_shapes=picked(ids, 2 * order.shape[1]),
+        name="home_late",
+        **options(),
+    )(order, ids, tables, w, pooled, preact, after)
 
 
 def fetch_kernel(head_hbm, interact_hbm, after_hbm, head_ref, interact_ref, sems):
@@ -333,55 +374,108 @@
     )(w, preact, *received)
 
 
-def score_kernel(outputs_ref, head_ref, interact_ref, scores_ref):
-    towers, rows, width = outputs_ref.shape
+def score_terms(blocks, pairs, head_ref, interact_ref, towers):
+    width = head_ref.shape[0] // towers
+    total = None
+    for block, tower in blocks:
+        rows_of_head = pl.ds(pl.multiple_of(tower * width, width), width)
+        part = multiply(block, head_ref[rows_of_head, :])
+        total = part if total is None else total + part
+    for (one, t), (two, s) in pairs:
+        gram = jnp.sum(one.astype(jnp.float32) * two.astype(jnp.float32), axis=1, keepdims=True)
+        weights = interact_ref[pl.ds(t * towers + s, 1), :]
+        if one is not two:
+            weights = weights + interact_ref[pl.ds(s * towers + t, 1), :]
+        total = total + gram * (weights * (1.0 / math.sqrt(width)))
+    return total
+
+
+def pairs_among(blocks):
+    return [(blocks[i], blocks[j]) for i in range(len(blocks)) for j in range(i, len(blocks))]
+
+
+def blocks_in(ref, masks):
+    rows = ref.shape[0] // len(masks)
     me = lax.axis_index("tower")
-    outputs = [outputs_ref[me ^ t] for t in range(towers)]
-    wide = jnp.concatenate(outputs, axis=1)
-    scores = multiply(wide, head_ref[...])
-    interact = interact_ref[...] * (1.0 / math.sqrt(width))
-    for t in range(towers):
-        mine = outputs[t].astype(jnp.float32)
-        for s in range(t, towers):
-            gram = jnp.sum(mine * outputs[s].astype(jnp.float32), axis=1, keepdims=True)
-            weights = interact[t * towers + s : t * towers + s + 1, :]
-            if s != t:
-                weights = weights + interact[s * towers + t : s * towers + t + 1, :]
-            scores = scores + gram * weights
-    scores_ref[...] = scores
-
-
-def score(outputs, head, interact):
-    towers, rows, width = outputs.shape
-    return pl.pallas_call(
-        score_kernel,
+    return [(ref[i * rows : (i + 1) * rows, :], me ^ mask) for i, mask in enumerate(masks)]
+
+
+def score_kernel(masks, towers, *refs):
+    *held_refs, head_ref, interact_ref, scores_ref = refs
+    first = len(masks) == len(held_refs)
+    if first:
+        blocks = [b for ref, some in zip(held_refs, masks) for b in blocks_in(ref, some)]
+        scores_ref[...] = score_terms(
+            blocks, pairs_among(blocks), head_ref, interact_ref, towers
+        )
+    else:
+        so_far_ref, *held_refs = held_refs
+        kept = blocks_in(held_refs[0], masks[0])
+        new = [b for ref, some in zip(held_refs[1:], masks[1:]) for b in blocks_in(ref, some)]
+        pairs = [(one, two) for one in kept for two in new] + pairs_among(new)
+        scores_ref[...] = so_far_ref[...] + score_terms(
+            new, pairs, head_ref, interact_ref, towers
+        )
+
+
+def score(held, masks, head, interact, towers, so_far=None):
+    operands = ([] if so_far is None else [so_far]) + list(held) + [head, interact]
+    rows = held[0].shape[0] // len(masks[0])
+    return pl.pallas_call(
+        lambda *refs: score_kernel(masks, towers, *refs),
         out_shape=jax.ShapeDtypeStruct((rows, head.shape[1]), jnp.float32),
-        in_specs=[ON_CHIP] * 3,
+        in_specs=[ON_CHIP] * len(operands),
         out_specs=ON_CHIP,
-        compiler_params=pltpu.CompilerParams(vmem_limit_bytes=VMEM_LIMIT),
         name="score",
-    )(outputs, head, interact)
+        **options(),
+    )(*operands)
+
+
+def piece_kernel(low, ks, held_ref, after_hbm, *out_refs):
+    group = held_ref.shape[1]
+    place = lax.rem(lax.axis_index("tower") // low, group)
+    for k, out_ref in zip(ks, out_refs):
+        out_ref[...] = held_ref[:, place ^ k]
+
+
+def pieces(held, low, ks, after):
+    shape = jax.ShapeDtypeStruct((held.shape[0], *held.shape[2:]), held.dtype)
+    return pl.pallas_call(
+        lambda *refs: piece_kernel(low, ks, *refs),
+        out_shape=(shape,) * len(ks),
+        in_specs=[ON_CHIP, ANYWHERE],
+        out_specs=(ON_CHIP,) * len(ks),
+        name="pieces",
+        **options(),
+    )(held, after)
 
 
 def exchange(blocks):
     towers, rows, width = blocks.shape
-    me = lax.axis_index("tower")
-    if towers & (towers - 1):
-        gathered = lax.all_to_all(blocks, "tower", split_axis=0, concat_axis=0, tiled=True)
-        return jnp.take(gathered, me ^ jnp.arange(towers), axis=0)
-    held = blocks
+    assert towers & (towers - 1) == 0
+    held, masks = blocks, (0,)
     low = 1
-    while low < towers:
+    while True:
         group = min(4, towers // low)
         split = held.reshape(held.shape[0] // group, group, *held.shape[1:])
-        place = lax.rem(me // low, group)
-        parts = [lax.dynamic_index_in_dim(split, place, 1, keepdims=False)]
-        for k in range(1, group):
-            part = lax.dynamic_index_in_dim(split, place ^ k, 1, keepdims=False)
-            parts.append(lax.ppermute(part, "tower", [(i, i ^ (k * low)) for i in range(towers)]))
-        held = jnp.stack(parts, axis=1).reshape(split.shape[0], group * held.shape[1], width)
+        parts = [None] * group
+        after = split
+        for k in range(group - 1, 0, -1):
+            if k > 1:
+                (after,) = pieces(split, low, (k,), after)
+                part = after
+            else:
+                part, parts[0] = pieces(split, low, (1, 0), after)
+            parts[k] = lax.ppermute(part, "tower", [(i, i ^ (k * low)) for i in range(towers)])
+        groups = tuple(tuple(k * low + mask for mask in masks) for k in range(group))
+        if low * group == towers:
+            return [part[0] for part in parts], groups
+        joined = jnp.zeros_like(split)
+        for k in range(group - 1, -1, -1):
+            joined = lax.dynamic_update_index_in_dim(joined, parts[k], k, 1)
+        held = joined.reshape(split.shape[0], group * held.shape[1], width)
+        masks = sum(groups, ())
         low *= group
-    return held.reshape(towers, rows, width)
 
 
 def on_device(ids, tables, order, w_first, w_second, w_head, w_interact):
@@ -403,6 +497,7 @@
     pooled = swap_cores(pooled)
     partial = away_layer(residues, weights, tables, w_first)
     partial = join(partial, pooled, w_other, jnp.bfloat16)
+    pooled, preact, partial = home_early(order, ids, tables, w_first, partial)
     received = []
     for k in away:
         received.append(
@@ -412,13 +507,13 @@
                 [(i, (i + 2 * k) % devices) for i in range(devices)],
             )
         )
-    pooled = swap_cores(home_pool(order, ids, tables, partial))
-    preact = home_layer(order, ids, tables, w_first, partial)
-    preact = join(preact, pooled, w_other, jnp.float32)
+    pooled, preact = home_late(order, ids, tables, w_first, pooled, preact, partial)
+    preact = join(preact, swap_cores(pooled), w_other, jnp.float32)
     w_head, w_interact = fetch_head(w_head, w_interact, preact)
     outputs = second_layer(w_second[0], preact, received)
-    gathered = exchange(outputs.reshape(towers, my_rows // towers, outputs.shape[1]))
-    return score(gathered, w_head, w_interact)[None]
+    held, masks = exchange(outputs.reshape(towers, my_rows // towers, outputs.shape[1]))
+    so_far = score(held[:1], masks[:1], w_head, w_interact, towers)
+    return score(held, masks, w_head, w_interact, towers, so_far)[None]
 
 
 def solution(mesh):

time: 27.5 us -> 27.1 us (0.985)
  Pallas kernels: 8.48 us -> 7.77 us
  starting transfers between devices: 9.6 us -> 10.2 us
  waiting for transfers between devices: 9.1 us -> 8.81 us
    ppermute x1, waiting for transfers between devices: 3.45 us -> 2.43 us  [on_device(): lax.ppermute(partial[(k - 1) * my_rows:k * my_rows], 'dev', [(i, (i + 2 *...]
    ppermute x3, waiting for transfers between devices: 0.79 us -> 1.63 us  [swap_cores(): return lax.ppermute(array, 'dev', [(i, i ^ 1) for i in range(devices)])]
    pallas_call x3 -> x8, Pallas kernels: 3.47 us -> 2.74 us  [the longest x1 1.63 us: home_late(): pl.pallas_call(late_kernel, out_shape=home_shapes(order, ids, tables, w),...]
    ppermute x4, starting transfers between devices: 6.21 us -> 6.7 us  [exchange(): lax.ppermute(part, 'tower', [(i, i ^ k * low) for i in range(towers)])]
  transfers between devices with their start and end apart: 8 -> 8, of which waited for: 7 -> 7; matrix products, arithmetic and copies ran while one was open for 0% -> 0% of each run, Pallas kernels for 25% -> 23%
where the time goes in v4:
time: 27.1 us; the launch traced here: 26.9 us
  starting transfers between devices  10.2 us (38%)
  waiting for transfers between devices  8.81 us (33%)
  Pallas kernels  7.77 us (29%)
    ppermute x4, starting transfers between devices, exchange(): lax.ppermute(part, 'tower', [(i, i ^ k * low) for i in range(towers)])  6.7 us
    ppermute x4, waiting for transfers between devices, exchange(): lax.ppermute(part, 'tower', [(i, i ^ k * low) for i in range(towers)])  4.75 us
    ppermute x1, starting transfers between devices, on_device(): lax.ppermute(partial[(k - 1) * my_rows:k * my_rows], 'dev', [(i, (i + 2 *...  2.73 us
    ppermute x1, waiting for transfers between devices, on_device(): lax.ppermute(partial[(k - 1) * my_rows:k * my_rows], 'dev', [(i, (i + 2 *...  2.43 us
    pallas_call x1, Pallas kernels, first_pool(): pl.pallas_call(lambda *refs: first_kernel(blocks, *refs), out_shape=(jax....  1.9 us
    ppermute x3, waiting for transfers between devices, swap_cores(): return lax.ppermute(array, 'dev', [(i, i ^ 1) for i in range(devices)])  1.63 us
    pallas_call x1, Pallas kernels, home_late(): pl.pallas_call(late_kernel, out_shape=home_shapes(order, ids, tables, w),...  1.63 us
    pallas_call x1, Pallas kernels, fetch_head(): pl.pallas_call(fetch_kernel, out_shape=(like(head), like(interact)), in_s...  1.3 us
  transfers between devices with their start and end apart: 8, of which 7 were waited for; matrix products, arithmetic and copies ran while one was open for 0% of the time, Pallas kernels for 23%

profile of v4, /device:TPU:0, one launch (start us, length us, event | category | flops | bytes accessed | tf_op | source)
XLA Modules:
  0.0 26.9 jit_solution(6823237775222389598)
XLA Ops:
  0.0 0.5 %collective-permute-start.1 = (bf16[512,1024]{1,0:T(8,128)(2,1)}, bf16[512,1024]{1,0:T(8,128)(2,1)S(1)}, u32[]{:S(2)}, u32[]{:S(2)}) collective-permute-start(bf16[512,1024]{1,0:T(8,128)(2,1)} %bitcast.29), channel_id=1, source_target_pairs={{0,1},{1,0},{2,3},{3,2},{4,5},{5,4},{6,7},{7,6},{8,9},{9,8},{10,11... | collective-permute-start | bytes 3145736 | tf_op jit(solution)/shard_map/ppermute | solution.py:490
  0.5 1.9 %first_pool.1 = (bf16[128,512]{1,0:T(8,128)(2,1)S(1)}, s32[4,128]{1,0:T(4,128)S(1)}, s32[4,32,512]{2,1,0:T(8,128)S(1)}, bf16[4,512,128]{2,1,0:T(8,128)(2,1)S(1)}...) custom-call(s32[4,128]{1,0:T(4,128)} %bitcast.34, s32[4,32,512]{2,1,0:T(8,128)} %bitcast.32, ...), custom_call_target="tpu_custom_call" | custom-call | flops 1 | bytes 1 | tf_op jit(solution)/shard_map/first_pool/pallas_call | solution.py:263
  2.4 0.1 collective-permute-start
  2.5 0.9 %away_layer.1.partial_ref = f32[128,1024]{1,0:T(8,128)S(1)} custom-call(s32[1,128,128]{2,1,0:T(8,128)S(1)} %get-tuple-element.27.residues_ref, s32[1,128,128]{2,1,0:T(8,128)S(1)} %get-tuple-element.28.weights_ref, bf16[4,512,128]{2,1,0:T(8,128)(2,1)S(1)} %get-tuple-element.25.tables_ref, bf16[512,1024]{1,0:T(8,128)(2,1)S(1)} %get-tuple-element.26.w_ref), custom_call_target="tpu_custom_call" | custom-call | flops 1 | bytes 1 | tf_op jit(solution)/shard_map/away_layer/pallas_call | solution.py:279
  3.4 0.4 %collective-permute-done.pooled_ref = bf16[128,512]{1,0:T(8,128)(2,1)S(1)} collective-permute-done((bf16[128,512]{1,0:T(8,128)(2,1)S(1)}, bf16[128,512]{1,0:T(8,128)(2,1)S(1)}, u32[]{:S(2)}, u32[]{:S(2)}) %collective-permute-start) | collective-permute-done | bytes 131104 | tf_op jit(solution)/shard_map/ppermute | solution.py:490
  3.8 0.0 collective-permute-done.1.w_ref
  3.8 0.3 %join.2.partial_ref = bf16[128,1024]{1,0:T(8,128)(2,1)S(1)} custom-call(f32[128,1024]{1,0:T(8,128)S(1)} %away_layer.1.partial_ref, bf16[128,512]{1,0:T(8,128)(2,1)S(1)} %collective-permute-done.pooled_ref, bf16[512,1024]{1,0:T(8,128)(2,1)S(1)} %collective-permute-done.1.w_ref), custom_call_target="tpu_custom_call" | custom-call | flops 1 | bytes 1 | tf_op jit(solution)/shard_map/join/pallas_call | solution.py:347
  4.1 2.7 %collective-permute-start.3 = (bf16[128,1024]{1,0:T(8,128)(2,1)S(1)}, bf16[128,1024]{1,0:T(8,128)(2,1)S(1)}, u32[]{:S(2)}, u32[]{:S(2)}) collective-permute-start(bf16[128,1024]{1,0:T(8,128)(2,1)S(1)} %get-tuple-element.32.after_hbm), channel_id=1, source_target_pairs={{0,2},{1,3},{2,0},{3,1},{4,6},{5,7},{6,4},{7,5},{8,10},{9,11},{10,... | collective-permute-start | bytes 786440 | tf_op jit(solution)/shard_map/ppermute | solution.py:504
  6.9 1.6 %home_late.1 = (bf16[128,512]{1,0:T(8,128)(2,1)S(1)}, f32[128,1024]{1,0:T(8,128)S(1)}) custom-call(s32[4,128]{1,0:T(4,128)S(1)} %get-tuple-element.23.order_ref, s32[4,32,512]{2,1,0:T(8,128)S(1)} %get-tuple-element.24.ids_ref, bf16[4,512,128]{2,1,0:T(8,128)(2,1)S(1)} %get-tuple-element.25.tables_ref, bf16[512,1024]{1,0:T(8,128)(2,1)S(1)} %get-tuple-element.26.w_ref, ...), custom_call_target="tpu_custom_call" | custom-call | flops 1 | bytes 1 | tf_op jit(solution)/shard_map/home_late/pallas_call | solution.py:310
  8.5 0.2 collective-permute-start.2
  8.7 1.2 %collective-permute-done.2.pooled_ref = bf16[128,512]{1,0:T(8,128)(2,1)S(1)} collective-permute-done((bf16[128,512]{1,0:T(8,128)(2,1)S(1)}, bf16[128,512]{1,0:T(8,128)(2,1)S(1)}, u32[]{:S(2)}, u32[]{:S(2)}) %collective-permute-start.2) | collective-permute-done | bytes 131104 | tf_op jit(solution)/shard_map/ppermute | solution.py:490
  9.9 0.0 copy-start
  9.9 0.3 %join.3.preact_ref.after_hbm = f32[128,1024]{1,0:T(8,128)S(1)} custom-call(f32[128,1024]{1,0:T(8,128)S(1)} %get-tuple-element.33.partial_ref, bf16[128,512]{1,0:T(8,128)(2,1)S(1)} %collective-permute-done.2.pooled_ref, bf16[512,1024]{1,0:T(8,128)(2,1)S(1)} %collective-permute-done.1.w_ref), custom_call_target="tpu_custom_call" | custom-call | flops 1 | bytes 1 | tf_op jit(solution)/shard_map/join/pallas_call | solution.py:347
  10.3 2.4 %collective-permute-done.3.refs_0_ = bf16[128,1024]{1,0:T(8,128)(2,1)S(1)} collective-permute-done((bf16[128,1024]{1,0:T(8,128)(2,1)S(1)}, bf16[128,1024]{1,0:T(8,128)(2,1)S(1)}, u32[]{:S(2)}, u32[]{:S(2)}) %collective-permute-start.3) | collective-permute-done | bytes 262176 | tf_op jit(solution)/shard_map/ppermute | solution.py:504
  12.7 0.0 copy-done
  12.7 0.3 %second_layer.1 = bf16[128,512]{1,0:T(8,128)(2,1)S(1)} custom-call(bf16[1024,512]{1,0:T(8,128)(2,1)S(1)} %bitcast.25, f32[128,1024]{1,0:T(8,128)S(1)} %join.3.preact_ref.after_hbm, bf16[128,1024]{1,0:T(8,128)(2,1)S(1)} %collective-permute-done.3.refs_0_), custom_call_target="tpu_custom_call" | custom-call | flops 1 | bytes 1 | tf_op jit(solution)/shard_map/second_layer/pallas_call | solution.py:367
  13.0 3.4 %collective-permute-start.4 = (bf16[2,16,512]{2,1,0:T(8,128)(2,1)S(1)}, bf16[2,16,512]{2,1,0:T(8,128)(2,1)S(1)}, u32[]{:S(2)}, u32[]{:S(2)}) collective-permute-start(bf16[2,16,512]{2,1,0:T(8,128)(2,1)S(1)} %pieces.4.refs_1_), channel_id=1, source_target_pairs={{0,12},{4,8},{8,4},{12,0},{16,28},{20,24},{24,20},{28,16},{1,13},{... | collective-permute-start | bytes 98312 | tf_op jit(solution)/shard_map/ppermute | solution.py:469
  16.4 0.5 %collective-permute-start.5 = (bf16[2,16,512]{2,1,0:T(8,128)(2,1)S(1)}, bf16[2,16,512]{2,1,0:T(8,128)(2,1)S(1)}, u32[]{:S(2)}, u32[]{:S(2)}) collective-permute-start(bf16[2,16,512]{2,1,0:T(8,128)(2,1)S(1)} %pieces.5.refs_1_), channel_id=1, source_target_pairs={{0,8},{4,12},{8,0},{12,4},{16,24},{20,28},{24,16},{28,20},{1,9},{5... | collective-permute-start | bytes 98312 | tf_op jit(solution)/shard_map/ppermute | solution.py:469
  16.9 0.2 collective-permute-start.6
  17.1 1.4 %collective-permute-done.4 = bf16[2,16,512]{2,1,0:T(8,128)(2,1)S(1)} collective-permute-done((bf16[2,16,512]{2,1,0:T(8,128)(2,1)S(1)}, bf16[2,16,512]{2,1,0:T(8,128)(2,1)S(1)}, u32[]{:S(2)}, u32[]{:S(2)}) %collective-permute-start.4) | collective-permute-done | bytes 32800 | tf_op jit(solution)/shard_map/ppermute | solution.py:469
  18.5 1.8 %collective-permute-done.5 = bf16[2,16,512]{2,1,0:T(8,128)(2,1)S(1)} collective-permute-done((bf16[2,16,512]{2,1,0:T(8,128)(2,1)S(1)}, bf16[2,16,512]{2,1,0:T(8,128)(2,1)S(1)}, u32[]{:S(2)}, u32[]{:S(2)}) %collective-permute-start.5) | collective-permute-done | bytes 32800 | tf_op jit(solution)/shard_map/ppermute | solution.py:469
  20.3 0.5 %collective-permute-done.6 = bf16[2,16,512]{2,1,0:T(8,128)(2,1)S(1)} collective-permute-done((bf16[2,16,512]{2,1,0:T(8,128)(2,1)S(1)}, bf16[2,16,512]{2,1,0:T(8,128)(2,1)S(1)}, u32[]{:S(2)}, u32[]{:S(2)}) %collective-permute-start.6) | collective-permute-done | bytes 32800 | tf_op jit(solution)/shard_map/ppermute | solution.py:469
  20.9 2.7 %collective-permute-start.7 = (bf16[1,64,512]{2,1,0:T(8,128)(2,1)S(1)}, bf16[1,64,512]{2,1,0:T(8,128)(2,1)S(1)}, u32[]{:S(2)}, u32[]{:S(2)}) collective-permute-start(bf16[1,64,512]{2,1,0:T(8,128)(2,1)S(1)} %get-tuple-element.40), channel_id=1, source_target_pairs={{0,16},{4,20},{8,24},{12,28},{16,0},{20,4},{24,8},{28,12},{1,17},{... | collective-permute-start | bytes 196616 | tf_op jit(solution)/shard_map/ppermute | solution.py:469
  23.5 1.3 %fetch_head.1 = (bf16[4096,128]{1,0:T(8,128)(2,1)S(1)}, f32[64,128]{1,0:T(8,128)S(1)}) custom-call(bf16[4096,128]{1,0:T(8,128)(2,1)} %head_hbm.1, f32[64,128]{1,0:T(8,128)} %interact_hbm.1, f32[128,1024]{1,0:T(8,128)S(1)} %join.3.preact_ref.after_hbm), custom_call_target="tpu_custom_call" | custom-call | flops 1 | bytes 1 | tf_op jit(solution)/shard_map/fetch_head/pallas_call | solution.py:331
  24.8 0.2 score.2.refs_0_
  25.0 1.1 %collective-permute-done.7 = bf16[1,64,512]{2,1,0:T(8,128)(2,1)S(1)} collective-permute-done((bf16[1,64,512]{2,1,0:T(8,128)(2,1)S(1)}, bf16[1,64,512]{2,1,0:T(8,128)(2,1)S(1)}, u32[]{:S(2)}, u32[]{:S(2)}) %collective-permute-start.7) | collective-permute-done | bytes 65568 | tf_op jit(solution)/shard_map/ppermute | solution.py:469
  26.1 0.8 %score.3 = f32[16,128]{1,0:T(8,128)} custom-call(f32[16,128]{1,0:T(8,128)S(1)} %score.2.refs_0_, bf16[64,512]{1,0:T(8,128)(2,1)S(1)} %bitcast.27, bf16[64,512]{1,0:T(8,128)(2,1)S(1)} %bitcast.28, bf16[4096,128]{1,0:T(8,128)(2,1)S(1)} %get-tuple-element.38.refs_1_.refs_3_, f32[64,128]{1,0:T(8,128)S(1)} %get-tuple-element.39.refs_2_.refs_4_), custom_call_target="tpu_custom_call" | custom-call | flops 1 | bytes 1 | tf_op jit(solution)/shard_map/score/pallas_call | solution.py:424
  (10 shorter events, 0.1 us)
Async XLA Ops:
  0.0 3.8 %collective-permute-start.1 = (bf16[512,1024]{1,0:T(8,128)(2,1)}, bf16[512,1024]{1,0:T(8,128)(2,1)S(1)}, u32[]{:S(2)}, u32[]{:S(2)}) collective-permute-start(bf16[512,1024]{1,0:T(8,128)(2,1)} %bitcast.29), channel_id=1, source_target_pairs={{0,1},{1,0},{2,3},{3,2},{4,5},{5,4},{6,7},{7,6},{8,9},{9,8},{10,11... | collective-permute-start | bytes 3145736 | tf_op jit(solution)/shard_map/ppermute | solution.py:490
  2.4 1.4 %collective-permute-start = (bf16[128,512]{1,0:T(8,128)(2,1)S(1)}, bf16[128,512]{1,0:T(8,128)(2,1)S(1)}, u32[]{:S(2)}, u32[]{:S(2)}) collective-permute-start(bf16[128,512]{1,0:T(8,128)(2,1)S(1)} %get-tuple-element.29), channel_id=1, source_target_pairs={{0,1},{1,0},{2,3},{3,2},{4,5},{5,4},{6,7},{7,6},{8,9},{9,8},{10,11... | collective-permute-start | bytes 393224 | tf_op jit(solution)/shard_map/ppermute | solution.py:490
  4.1 8.5 %collective-permute-start.3 = (bf16[128,1024]{1,0:T(8,128)(2,1)S(1)}, bf16[128,1024]{1,0:T(8,128)(2,1)S(1)}, u32[]{:S(2)}, u32[]{:S(2)}) collective-permute-start(bf16[128,1024]{1,0:T(8,128)(2,1)S(1)} %get-tuple-element.32.after_hbm), channel_id=1, source_target_pairs={{0,2},{1,3},{2,0},{3,1},{4,6},{5,7},{6,4},{7,5},{8,10},{9,11},{10,... | collective-permute-start | bytes 786440 | tf_op jit(solution)/shard_map/ppermute | solution.py:504
  8.5 1.4 %collective-permute-start.2 = (bf16[128,512]{1,0:T(8,128)(2,1)S(1)}, bf16[128,512]{1,0:T(8,128)(2,1)S(1)}, u32[]{:S(2)}, u32[]{:S(2)}) collective-permute-start(bf16[128,512]{1,0:T(8,128)(2,1)S(1)} %get-tuple-element.34), channel_id=1, source_target_pairs={{0,1},{1,0},{2,3},{3,2},{4,5},{5,4},{6,7},{7,6},{8,9},{9,8},{10,11... | collective-permute-start | bytes 393224 | tf_op jit(solution)/shard_map/ppermute | solution.py:490
  9.9 2.8 %copy-start = (bf16[1,1024,512]{2,1,0:T(8,128)(2,1)S(1)}, bf16[1,1024,512]{2,1,0:T(8,128)(2,1)}, u32[]{:S(2)}) copy-start(bf16[1,1024,512]{2,1,0:T(8,128)(2,1)} %param.11) | copy-start | bytes 3145732
  13.0 5.5 %collective-permute-start.4 = (bf16[2,16,512]{2,1,0:T(8,128)(2,1)S(1)}, bf16[2,16,512]{2,1,0:T(8,128)(2,1)S(1)}, u32[]{:S(2)}, u32[]{:S(2)}) collective-permute-start(bf16[2,16,512]{2,1,0:T(8,128)(2,1)S(1)} %pieces.4.refs_1_), channel_id=1, source_target_pairs={{0,12},{4,8},{8,4},{12,0},{16,28},{20,24},{24,20},{28,16},{1,13},{... | collective-permute-start | bytes 98312 | tf_op jit(solution)/shard_map/ppermute | solution.py:469
  16.4 3.9 %collective-permute-start.5 = (bf16[2,16,512]{2,1,0:T(8,128)(2,1)S(1)}, bf16[2,16,512]{2,1,0:T(8,128)(2,1)S(1)}, u32[]{:S(2)}, u32[]{:S(2)}) collective-permute-start(bf16[2,16,512]{2,1,0:T(8,128)(2,1)S(1)} %pieces.5.refs_1_), channel_id=1, source_target_pairs={{0,8},{4,12},{8,0},{12,4},{16,24},{20,28},{24,16},{28,20},{1,9},{5... | collective-permute-start | bytes 98312 | tf_op jit(solution)/shard_map/ppermute | solution.py:469
  16.9 3.9 %collective-permute-start.6 = (bf16[2,16,512]{2,1,0:T(8,128)(2,1)S(1)}, bf16[2,16,512]{2,1,0:T(8,128)(2,1)S(1)}, u32[]{:S(2)}, u32[]{:S(2)}) collective-permute-start(bf16[2,16,512]{2,1,0:T(8,128)(2,1)S(1)} %get-tuple-element.35), channel_id=1, source_target_pairs={{0,4},{4,0},{8,12},{12,8},{16,20},{20,16},{24,28},{28,24},{1,5},{5... | collective-permute-start | bytes 98312 | tf_op jit(solution)/shard_map/ppermute | solution.py:469
  20.9 5.2 %collective-permute-start.7 = (bf16[1,64,512]{2,1,0:T(8,128)(2,1)S(1)}, bf16[1,64,512]{2,1,0:T(8,128)(2,1)S(1)}, u32[]{:S(2)}, u32[]{:S(2)}) collective-permute-start(bf16[1,64,512]{2,1,0:T(8,128)(2,1)S(1)} %get-tuple-element.40), channel_id=1, source_target_pairs={{0,16},{4,20},{8,24},{12,28},{16,0},{20,4},{24,8},{28,12},{1,17},{... | collective-permute-start | bytes 196616 | tf_op jit(solution)/shard_map/ppermute | solution.py:469

commit v5 on v4

--- a/solution.py
+++ b/solution.py
@@ -8,6 +8,7 @@
 from jax.sharding import PartitionSpec as P
 
 WORD_BITS = 32
+CODE_TOP = 32767.0
 
 
 def multiply(left, right):
@@ -201,8 +202,8 @@
 
 
 def early_kernel(
-    order_ref, ids_ref, tables_ref, w_ref, partial_ref,
-    pooled_ref, out_ref, again_ref, residue_ref, weight_ref,
+    order_ref, ids_ref, tables_ref, w_ref, partial_ref, step_ref,
+    pooled_ref, out_ref, again_ref, step_again_ref, residue_ref, weight_ref,
 ):
     @pl.when(lax.axis_index("dev") % 2 == 1)
     def _():
@@ -211,6 +212,7 @@
         )
 
     again_ref[...] = partial_ref[...]
+    step_again_ref[...] = step_ref[...]
 
 
 def late_kernel(
@@ -294,16 +296,16 @@
     )
 
 
-def home_early(order, ids, tables, w, partial):
+def home_early(order, ids, tables, w, partial, step):
     return pl.pallas_call(
         early_kernel,
-        out_shape=home_shapes(order, ids, tables, w) + (like(partial),),
-        in_specs=[ON_CHIP] * 5,
-        out_specs=(ON_CHIP,) * 3,
+        out_shape=home_shapes(order, ids, tables, w) + (like(partial), like(step)),
+        in_specs=[ON_CHIP] * 6,
+        out_specs=(ON_CHIP,) * 4,
         scratch_shapes=picked(ids, 2 * order.shape[1]),
         name="home_early",
         **options(),
-    )(order, ids, tables, w, partial)
+    )(order, ids, tables, w, partial, step)
 
 
 def home_late(order, ids, tables, w, pooled, preact, after):
@@ -340,13 +342,13 @@
 
 
 def join_kernel(partial_ref, pooled_ref, w_ref, out_ref):
-    out_ref[...] = (partial_ref[...] + multiply(pooled_ref[...], w_ref[...])).astype(out_ref.dtype)
-
-
-def join(partial, pooled, w, kind):
+    out_ref[...] = partial_ref[...] + multiply(pooled_ref[...], w_ref[...])
+
+
+def join(partial, pooled, w):
     return pl.pallas_call(
         join_kernel,
-        out_shape=jax.ShapeDtypeStruct(partial.shape, kind),
+        out_shape=like(partial),
         in_specs=[ON_CHIP] * 3,
         out_specs=ON_CHIP,
         name="join",
@@ -354,11 +356,34 @@
     )(partial, pooled, w)
 
 
+def join_coded_kernel(partial_ref, pooled_ref, w_ref, coded_ref, step_ref):
+    total = partial_ref[...] + multiply(pooled_ref[...], w_ref[...])
+    top = jnp.maximum(jnp.max(jnp.abs(total)), 1e-30)
+    coded = jnp.round(total * (CODE_TOP / top))
+    coded_ref[...] = coded.astype(jnp.int32).astype(coded_ref.dtype)
+    step_ref[...] = jnp.full(step_ref.shape, top * (1.0 / CODE_TOP), step_ref.dtype)
+
+
+def join_coded(partial, pooled, w):
+    return pl.pallas_call(
+        join_coded_kernel,
+        out_shape=(
+            jax.ShapeDtypeStruct(partial.shape, jnp.int16),
+            jax.ShapeDtypeStruct((8, 128), jnp.float32),
+        ),
+        in_specs=[ON_CHIP] * 3,
+        out_specs=(ON_CHIP,) * 2,
+        name="join_coded",
+        **options(),
+    )(partial, pooled, w)
+
+
 def second_kernel(w_ref, preact_ref, *refs):
     *received_refs, out_ref = refs
     preact = preact_ref[...]
-    for received_ref in received_refs:
-        preact = preact + received_ref[...].astype(jnp.float32)
+    for coded_ref, step_ref in zip(received_refs[::2], received_refs[1::2]):
+        coded = coded_ref[...].astype(jnp.int32).astype(jnp.float32)
+        preact = preact + coded * step_ref[0:1, 0:1]
     hidden = jnp.maximum(preact, 0.0).astype(jnp.bfloat16)
     out_ref[...] = multiply(hidden, w_ref[...]).astype(out_ref.dtype)
 
@@ -496,19 +521,15 @@
     )
     pooled = swap_cores(pooled)
     partial = away_layer(residues, weights, tables, w_first)
-    partial = join(partial, pooled, w_other, jnp.bfloat16)
-    pooled, preact, partial = home_early(order, ids, tables, w_first, partial)
+    partial, step = join_coded(partial, pooled, w_other)
+    pooled, preact, partial, step = home_early(order, ids, tables, w_first, partial, step)
     received = []
-    for k in away:
-        received.append(
-            lax.ppermute(
-                partial[(k - 1) * my_rows : k * my_rows],
-                "dev",
-                [(i, (i + 2 * k) % devices) for i in range(devices)],
-            )
-        )
+    for place, chips_on in enumerate(away):
+        onward = [(i, (i + 2 * chips_on) % devices) for i in range(devices)]
+        block = partial[place * my_rows : (place + 1) * my_rows]
+        received += [lax.ppermute(block, "dev", onward), lax.ppermute(step, "dev", onward)]
     pooled, preact = home_late(order, ids, tables, w_first, pooled, preact, partial)
-    preact = join(preact, swap_cores(pooled), w_other, jnp.float32)
+    preact = join(preact, swap_cores(pooled), w_other)
     w_head, w_interact = fetch_head(w_head, w_interact, preact)
     outputs = second_layer(w_second[0], preact, received)
     held, masks = exchange(outputs.reshape(towers, my_rows // towers, outputs.shape[1]))

time: 27.1 us -> 27.4 us (1.011)
  starting transfers between devices: 10.2 us -> 10.5 us
    ppermute x1 -> x2, starting transfers between devices: 2.73 us -> 3.04 us  [the longest x1 2.73 us: on_device(): lax.ppermute(block, 'dev', onward)]
    ppermute x3, waiting for transfers between devices: 1.63 us -> 1.32 us  [swap_cores(): return lax.ppermute(array, 'dev', [(i, i ^ 1) for i in range(devices)])]
    ppermute x1 -> x2, waiting for transfers between devices: 2.43 us -> 2.52 us  [the longest x1 2.52 us: on_device(): lax.ppermute(step, 'dev', onward)]
  transfers between devices with their start and end apart: 8 -> 9, of which waited for: 7 -> 7; matrix products, arithmetic and copies ran while one was open for 0% -> 0% of each run, Pallas kernels for 23% -> 23%
where the time goes in v5:
time: 27.4 us; the launch traced here: 27.3 us
  starting transfers between devices  10.5 us (38%)
  waiting for transfers between devices  8.6 us (31%)
  Pallas kernels  8.03 us (29%)
    ppermute x4, starting transfers between devices, exchange(): lax.ppermute(part, 'tower', [(i, i ^ k * low) for i in range(towers)])  6.7 us
    ppermute x4, waiting for transfers between devices, exchange(): lax.ppermute(part, 'tower', [(i, i ^ k * low) for i in range(towers)])  4.75 us
    ppermute x1, starting transfers between devices, on_device(): lax.ppermute(block, 'dev', onward)  2.73 us
    ppermute x1, waiting for transfers between devices, on_device(): lax.ppermute(step, 'dev', onward)  2.52 us
    pallas_call x1, Pallas kernels, first_pool(): pl.pallas_call(lambda *refs: first_kernel(blocks, *refs), out_shape=(jax....  1.9 us
    pallas_call x1, Pallas kernels, home_late(): pl.pallas_call(late_kernel, out_shape=home_shapes(order, ids, tables, w),...  1.63 us
    ppermute x3, waiting for transfers between devices, swap_cores(): return lax.ppermute(array, 'dev', [(i, i ^ 1) for i in range(devices)])  1.32 us
    pallas_call x1, Pallas kernels, fetch_head(): pl.pallas_call(fetch_kernel, out_shape=(like(head), like(interact)), in_s...  1.3 us
  transfers between devices with their start and end apart: 9, of which 7 were waited for; matrix products, arithmetic and copies ran while one was open for 0% of the time, Pallas kernels for 23%

profile of v5, /device:TPU:0, one launch (start us, length us, event | category | flops | bytes accessed | tf_op | source)
XLA Modules:
  0.0 27.3 jit_solution(9914726990940537225)
XLA Ops:
  0.0 0.5 %collective-permute-start.1 = (bf16[512,1024]{1,0:T(8,128)(2,1)}, bf16[512,1024]{1,0:T(8,128)(2,1)S(1)}, u32[]{:S(2)}, u32[]{:S(2)}) collective-permute-start(bf16[512,1024]{1,0:T(8,128)(2,1)} %bitcast.29), channel_id=1, source_target_pairs={{0,1},{1,0},{2,3},{3,2},{4,5},{5,4},{6,7},{7,6},{8,9},{9,8},{10,11... | collective-permute-start | bytes 3145736 | tf_op jit(solution)/shard_map/ppermute | solution.py:515
  0.5 1.9 %first_pool.1 = (bf16[128,512]{1,0:T(8,128)(2,1)S(1)}, s32[4,128]{1,0:T(4,128)S(1)}, s32[4,32,512]{2,1,0:T(8,128)S(1)}, bf16[4,512,128]{2,1,0:T(8,128)(2,1)S(1)}...) custom-call(s32[4,128]{1,0:T(4,128)} %bitcast.34, s32[4,32,512]{2,1,0:T(8,128)} %bitcast.32, ...), custom_call_target="tpu_custom_call" | custom-call | flops 1 | bytes 1 | tf_op jit(solution)/shard_map/first_pool/pallas_call | solution.py:265
  2.4 0.1 collective-permute-start
  2.5 0.9 %away_layer.1.partial_ref = f32[128,1024]{1,0:T(8,128)S(1)} custom-call(s32[1,128,128]{2,1,0:T(8,128)S(1)} %get-tuple-element.30.residues_ref, s32[1,128,128]{2,1,0:T(8,128)S(1)} %get-tuple-element.31.weights_ref, bf16[4,512,128]{2,1,0:T(8,128)(2,1)S(1)} %get-tuple-element.28.tables_ref, bf16[512,1024]{1,0:T(8,128)(2,1)S(1)} %get-tuple-element.29.w_ref), custom_call_target="tpu_custom_call" | custom-call | flops 1 | bytes 1 | tf_op jit(solution)/shard_map/away_layer/pallas_call | solution.py:281
  3.4 0.4 %collective-permute-done.pooled_ref = bf16[128,512]{1,0:T(8,128)(2,1)S(1)} collective-permute-done((bf16[128,512]{1,0:T(8,128)(2,1)S(1)}, bf16[128,512]{1,0:T(8,128)(2,1)S(1)}, u32[]{:S(2)}, u32[]{:S(2)}) %collective-permute-start) | collective-permute-done | bytes 131104 | tf_op jit(solution)/shard_map/ppermute | solution.py:515
  3.8 0.0 collective-permute-done.1.w_ref
  3.8 0.6 %join_coded.1 = (s16[128,1024]{1,0:T(8,128)(2,1)S(1)}, f32[8,128]{1,0:T(8,128)S(1)}) custom-call(f32[128,1024]{1,0:T(8,128)S(1)} %away_layer.1.partial_ref, bf16[128,512]{1,0:T(8,128)(2,1)S(1)} %collective-permute-done.pooled_ref, bf16[512,1024]{1,0:T(8,128)(2,1)S(1)} %collective-permute-done.1.w_ref), custom_call_target="tpu_custom_call" | custom-call | flops 1 | bytes 1 | tf_op jit(solution)/shard_map/join_coded/pallas_call | solution.py:368
  4.4 2.7 %collective-permute-start.3 = (s16[128,1024]{1,0:T(8,128)(2,1)S(1)}, s16[128,1024]{1,0:T(8,128)(2,1)S(1)}, u32[]{:S(2)}, u32[]{:S(2)}) collective-permute-start(s16[128,1024]{1,0:T(8,128)(2,1)S(1)} %get-tuple-element.37.after_hbm), channel_id=1, source_target_pairs={{0,2},{1,3},{2,0},{3,1},{4,6},{5,7},{6,4},{7,5},{8,10},{9,11},{10,... | collective-permute-start | bytes 786440 | tf_op jit(solution)/shard_map/ppermute | solution.py:530
  7.1 1.6 %home_late.1 = (bf16[128,512]{1,0:T(8,128)(2,1)S(1)}, f32[128,1024]{1,0:T(8,128)S(1)}) custom-call(s32[4,128]{1,0:T(4,128)S(1)} %get-tuple-element.26.order_ref, s32[4,32,512]{2,1,0:T(8,128)S(1)} %get-tuple-element.27.ids_ref, bf16[4,512,128]{2,1,0:T(8,128)(2,1)S(1)} %get-tuple-element.28.tables_ref, bf16[512,1024]{1,0:T(8,128)(2,1)S(1)} %get-tuple-element.29.w_ref, ...), custom_call_target="tpu_custom_call" | custom-call | flops 1 | bytes 1 | tf_op jit(solution)/shard_map/home_late/pallas_call | solution.py:312
  8.7 0.2 collective-permute-start.2
  8.9 0.3 %collective-permute-start.4 = (f32[8,128]{1,0:T(8,128)S(1)}, f32[8,128]{1,0:T(8,128)S(1)}, u32[]{:S(2)}, u32[]{:S(2)}) collective-permute-start(f32[8,128]{1,0:T(8,128)S(1)} %get-tuple-element.40), channel_id=1, source_target_pairs={{0,2},{1,3},{2,0},{3,1},{4,6},{5,7},{6,4},{7,5},{8,10},{9,11},{10,... | collective-permute-start | bytes 12296 | tf_op jit(solution)/shard_map/ppermute | solution.py:530
  9.3 0.9 %collective-permute-done.2.pooled_ref = bf16[128,512]{1,0:T(8,128)(2,1)S(1)} collective-permute-done((bf16[128,512]{1,0:T(8,128)(2,1)S(1)}, bf16[128,512]{1,0:T(8,128)(2,1)S(1)}, u32[]{:S(2)}, u32[]{:S(2)}) %collective-permute-start.2) | collective-permute-done | bytes 131104 | tf_op jit(solution)/shard_map/ppermute | solution.py:515
  10.2 0.0 copy-start
  10.2 0.3 %join.1.preact_ref.after_hbm = f32[128,1024]{1,0:T(8,128)S(1)} custom-call(f32[128,1024]{1,0:T(8,128)S(1)} %get-tuple-element.38.partial_ref, bf16[128,512]{1,0:T(8,128)(2,1)S(1)} %collective-permute-done.2.pooled_ref, bf16[512,1024]{1,0:T(8,128)(2,1)S(1)} %collective-permute-done.1.w_ref), custom_call_target="tpu_custom_call" | custom-call | flops 1 | bytes 1 | tf_op jit(solution)/shard_map/join/pallas_call | solution.py:349
  10.5 2.5 %collective-permute-done.4.refs_1_ = f32[8,128]{1,0:T(8,128)S(1)} collective-permute-done((f32[8,128]{1,0:T(8,128)S(1)}, f32[8,128]{1,0:T(8,128)S(1)}, u32[]{:S(2)}, u32[]{:S(2)}) %collective-permute-start.4) | collective-permute-done | bytes 4128 | tf_op jit(solution)/shard_map/ppermute | solution.py:530
  13.0 0.0 collective-permute-done.3.refs_0_
  13.0 0.0 copy-done
  13.0 0.3 %second_layer.1 = bf16[128,512]{1,0:T(8,128)(2,1)S(1)} custom-call(bf16[1024,512]{1,0:T(8,128)(2,1)S(1)} %bitcast.25, f32[128,1024]{1,0:T(8,128)S(1)} %join.1.preact_ref.after_hbm, s16[128,1024]{1,0:T(8,128)(2,1)S(1)} %collective-permute-done.3.refs_0_, f32[8,128]{1,0:T(8,128)S(1)} %collective-permute-done.4.refs_1_), custom_call_target="tpu_custom_call" | custom-call | flops 1 | bytes 1 | tf_op jit(solution)/shard_map/second_layer/pallas_call | solution.py:392
  13.4 3.4 %collective-permute-start.5 = (bf16[2,16,512]{2,1,0:T(8,128)(2,1)S(1)}, bf16[2,16,512]{2,1,0:T(8,128)(2,1)S(1)}, u32[]{:S(2)}, u32[]{:S(2)}) collective-permute-start(bf16[2,16,512]{2,1,0:T(8,128)(2,1)S(1)} %pieces.4.refs_1_), channel_id=1, source_target_pairs={{0,12},{4,8},{8,4},{12,0},{16,28},{20,24},{24,20},{28,16},{1,13},{... | collective-permute-start | bytes 98312 | tf_op jit(solution)/shard_map/ppermute | solution.py:494
  16.8 0.5 %collective-permute-start.6 = (bf16[2,16,512]{2,1,0:T(8,128)(2,1)S(1)}, bf16[2,16,512]{2,1,0:T(8,128)(2,1)S(1)}, u32[]{:S(2)}, u32[]{:S(2)}) collective-permute-start(bf16[2,16,512]{2,1,0:T(8,128)(2,1)S(1)} %pieces.5.refs_1_), channel_id=1, source_target_pairs={{0,8},{4,12},{8,0},{12,4},{16,24},{20,28},{24,16},{28,20},{1,9},{5... | collective-permute-start | bytes 98312 | tf_op jit(solution)/shard_map/ppermute | solution.py:494
  17.2 0.2 collective-permute-start.7
  17.5 1.4 %collective-permute-done.5 = bf16[2,16,512]{2,1,0:T(8,128)(2,1)S(1)} collective-permute-done((bf16[2,16,512]{2,1,0:T(8,128)(2,1)S(1)}, bf16[2,16,512]{2,1,0:T(8,128)(2,1)S(1)}, u32[]{:S(2)}, u32[]{:S(2)}) %collective-permute-start.5) | collective-permute-done | bytes 32800 | tf_op jit(solution)/shard_map/ppermute | solution.py:494
  18.9 1.8 %collective-permute-done.6 = bf16[2,16,512]{2,1,0:T(8,128)(2,1)S(1)} collective-permute-done((bf16[2,16,512]{2,1,0:T(8,128)(2,1)S(1)}, bf16[2,16,512]{2,1,0:T(8,128)(2,1)S(1)}, u32[]{:S(2)}, u32[]{:S(2)}) %collective-permute-start.6) | collective-permute-done | bytes 32800 | tf_op jit(solution)/shard_map/ppermute | solution.py:494
  20.7 0.5 %collective-permute-done.7 = bf16[2,16,512]{2,1,0:T(8,128)(2,1)S(1)} collective-permute-done((bf16[2,16,512]{2,1,0:T(8,128)(2,1)S(1)}, bf16[2,16,512]{2,1,0:T(8,128)(2,1)S(1)}, u32[]{:S(2)}, u32[]{:S(2)}) %collective-permute-start.7) | collective-permute-done | bytes 32800 | tf_op jit(solution)/shard_map/ppermute | solution.py:494
  21.2 2.6 %collective-permute-start.8 = (bf16[1,64,512]{2,1,0:T(8,128)(2,1)S(1)}, bf16[1,64,512]{2,1,0:T(8,128)(2,1)S(1)}, u32[]{:S(2)}, u32[]{:S(2)}) collective-permute-start(bf16[1,64,512]{2,1,0:T(8,128)(2,1)S(1)} %get-tuple-element.46), channel_id=1, source_target_pairs={{0,16},{4,20},{8,24},{12,28},{16,0},{20,4},{24,8},{28,12},{1,17},{... | collective-permute-start | bytes 196616 | tf_op jit(solution)/shard_map/ppermute | solution.py:494
  23.9 1.3 %fetch_head.1 = (bf16[4096,128]{1,0:T(8,128)(2,1)S(1)}, f32[64,128]{1,0:T(8,128)S(1)}) custom-call(bf16[4096,128]{1,0:T(8,128)(2,1)} %head_hbm.1, f32[64,128]{1,0:T(8,128)} %interact_hbm.1, f32[128,1024]{1,0:T(8,128)S(1)} %join.1.preact_ref.after_hbm), custom_call_target="tpu_custom_call" | custom-call | flops 1 | bytes 1 | tf_op jit(solution)/shard_map/fetch_head/pallas_call | solution.py:333
  25.2 0.2 score.2.refs_0_
  25.4 1.1 %collective-permute-done.8 = bf16[1,64,512]{2,1,0:T(8,128)(2,1)S(1)} collective-permute-done((bf16[1,64,512]{2,1,0:T(8,128)(2,1)S(1)}, bf16[1,64,512]{2,1,0:T(8,128)(2,1)S(1)}, u32[]{:S(2)}, u32[]{:S(2)}) %collective-permute-start.8) | collective-permute-done | bytes 65568 | tf_op jit(solution)/shard_map/ppermute | solution.py:494
  26.4 0.8 %score.3 = f32[16,128]{1,0:T(8,128)} custom-call(f32[16,128]{1,0:T(8,128)S(1)} %score.2.refs_0_, bf16[64,512]{1,0:T(8,128)(2,1)S(1)} %bitcast.27, bf16[64,512]{1,0:T(8,128)(2,1)S(1)} %bitcast.28, bf16[4096,128]{1,0:T(8,128)(2,1)S(1)} %get-tuple-element.44.refs_1_.refs_3_, f32[64,128]{1,0:T(8,128)S(1)} %get-tuple-element.45.refs_2_.refs_4_), custom_call_target="tpu_custom_call" | custom-call | flops 1 | bytes 1 | tf_op jit(solution)/shard_map/score/pallas_call | solution.py:449
  (10 shorter events, 0.1 us)
Async XLA Ops:
  0.0 3.8 %collective-permute-start.1 = (bf16[512,1024]{1,0:T(8,128)(2,1)}, bf16[512,1024]{1,0:T(8,128)(2,1)S(1)}, u32[]{:S(2)}, u32[]{:S(2)}) collective-permute-start(bf16[512,1024]{1,0:T(8,128)(2,1)} %bitcast.29), channel_id=1, source_target_pairs={{0,1},{1,0},{2,3},{3,2},{4,5},{5,4},{6,7},{7,6},{8,9},{9,8},{10,11... | collective-permute-start | bytes 3145736 | tf_op jit(solution)/shard_map/ppermute | solution.py:515
  2.4 1.4 %collective-permute-start = (bf16[128,512]{1,0:T(8,128)(2,1)S(1)}, bf16[128,512]{1,0:T(8,128)(2,1)S(1)}, u32[]{:S(2)}, u32[]{:S(2)}) collective-permute-start(bf16[128,512]{1,0:T(8,128)(2,1)S(1)} %get-tuple-element.32), channel_id=1, source_target_pairs={{0,1},{1,0},{2,3},{3,2},{4,5},{5,4},{6,7},{7,6},{8,9},{9,8},{10,11... | collective-permute-start | bytes 393224 | tf_op jit(solution)/shard_map/ppermute | solution.py:515
  4.4 8.6 %collective-permute-start.3 = (s16[128,1024]{1,0:T(8,128)(2,1)S(1)}, s16[128,1024]{1,0:T(8,128)(2,1)S(1)}, u32[]{:S(2)}, u32[]{:S(2)}) collective-permute-start(s16[128,1024]{1,0:T(8,128)(2,1)S(1)} %get-tuple-element.37.after_hbm), channel_id=1, source_target_pairs={{0,2},{1,3},{2,0},{3,1},{4,6},{5,7},{6,4},{7,5},{8,10},{9,11},{10,... | collective-permute-start | bytes 786440 | tf_op jit(solution)/shard_map/ppermute | solution.py:530
  8.7 1.4 %collective-permute-start.2 = (bf16[128,512]{1,0:T(8,128)(2,1)S(1)}, bf16[128,512]{1,0:T(8,128)(2,1)S(1)}, u32[]{:S(2)}, u32[]{:S(2)}) collective-permute-start(bf16[128,512]{1,0:T(8,128)(2,1)S(1)} %get-tuple-element.39), channel_id=1, source_target_pairs={{0,1},{1,0},{2,3},{3,2},{4,5},{5,4},{6,7},{7,6},{8,9},{9,8},{10,11... | collective-permute-start | bytes 393224 | tf_op jit(solution)/shard_map/ppermute | solution.py:515
  8.9 4.1 %collective-permute-start.4 = (f32[8,128]{1,0:T(8,128)S(1)}, f32[8,128]{1,0:T(8,128)S(1)}, u32[]{:S(2)}, u32[]{:S(2)}) collective-permute-start(f32[8,128]{1,0:T(8,128)S(1)} %get-tuple-element.40), channel_id=1, source_target_pairs={{0,2},{1,3},{2,0},{3,1},{4,6},{5,7},{6,4},{7,5},{8,10},{9,11},{10,... | collective-permute-start | bytes 12296 | tf_op jit(solution)/shard_map/ppermute | solution.py:530
  10.2 2.9 %copy-start = (bf16[1,1024,512]{2,1,0:T(8,128)(2,1)S(1)}, bf16[1,1024,512]{2,1,0:T(8,128)(2,1)}, u32[]{:S(2)}) copy-start(bf16[1,1024,512]{2,1,0:T(8,128)(2,1)} %param.11) | copy-start | bytes 3145732
  13.4 5.5 %collective-permute-start.5 = (bf16[2,16,512]{2,1,0:T(8,128)(2,1)S(1)}, bf16[2,16,512]{2,1,0:T(8,128)(2,1)S(1)}, u32[]{:S(2)}, u32[]{:S(2)}) collective-permute-start(bf16[2,16,512]{2,1,0:T(8,128)(2,1)S(1)} %pieces.4.refs_1_), channel_id=1, source_target_pairs={{0,12},{4,8},{8,4},{12,0},{16,28},{20,24},{24,20},{28,16},{1,13},{... | collective-permute-start | bytes 98312 | tf_op jit(solution)/shard_map/ppermute | solution.py:494
  16.8 3.9 %collective-permute-start.6 = (bf16[2,16,512]{2,1,0:T(8,128)(2,1)S(1)}, bf16[2,16,512]{2,1,0:T(8,128)(2,1)S(1)}, u32[]{:S(2)}, u32[]{:S(2)}) collective-permute-start(bf16[2,16,512]{2,1,0:T(8,128)(2,1)S(1)} %pieces.5.refs_1_), channel_id=1, source_target_pairs={{0,8},{4,12},{8,0},{12,4},{16,24},{20,28},{24,16},{28,20},{1,9},{5... | collective-permute-start | bytes 98312 | tf_op jit(solution)/shard_map/ppermute | solution.py:494
  17.2 3.9 %collective-permute-start.7 = (bf16[2,16,512]{2,1,0:T(8,128)(2,1)S(1)}, bf16[2,16,512]{2,1,0:T(8,128)(2,1)S(1)}, u32[]{:S(2)}, u32[]{:S(2)}) collective-permute-start(bf16[2,16,512]{2,1,0:T(8,128)(2,1)S(1)} %get-tuple-element.41), channel_id=1, source_target_pairs={{0,4},{4,0},{8,12},{12,8},{16,20},{20,16},{24,28},{28,24},{1,5},{5... | collective-permute-start | bytes 98312 | tf_op jit(solution)/shard_map/ppermute | solution.py:494
  21.2 5.2 %collective-permute-start.8 = (bf16[1,64,512]{2,1,0:T(8,128)(2,1)S(1)}, bf16[1,64,512]{2,1,0:T(8,128)(2,1)S(1)}, u32[]{:S(2)}, u32[]{:S(2)}) collective-permute-start(bf16[1,64,512]{2,1,0:T(8,128)(2,1)S(1)} %get-tuple-element.46), channel_id=1, source_target_pairs={{0,16},{4,20},{8,24},{12,28},{16,0},{20,4},{24,8},{28,12},{1,17},{... | collective-permute-start | bytes 196616 | tf_op jit(solution)/shard_map/ppermute | solution.py:494

commit v6 on v5

--- a/solution.py
+++ b/solution.py
@@ -356,12 +356,21 @@
     )(partial, pooled, w)
 
 
+def code_chunks(width):
+    count = max(1, min(8, width // 256))
+    return [slice(i * width // count, (i + 1) * width // count) for i in range(count)]
+
+
 def join_coded_kernel(partial_ref, pooled_ref, w_ref, coded_ref, step_ref):
-    total = partial_ref[...] + multiply(pooled_ref[...], w_ref[...])
-    top = jnp.maximum(jnp.max(jnp.abs(total)), 1e-30)
-    coded = jnp.round(total * (CODE_TOP / top))
-    coded_ref[...] = coded.astype(jnp.int32).astype(coded_ref.dtype)
-    step_ref[...] = jnp.full(step_ref.shape, top * (1.0 / CODE_TOP), step_ref.dtype)
+    step_ref[...] = jnp.zeros_like(step_ref)
+    for place, here in enumerate(code_chunks(partial_ref.shape[1])):
+        total = partial_ref[:, here] + multiply(pooled_ref[...], w_ref[:, here])
+        top = jnp.maximum(jnp.max(jnp.abs(total), keepdims=True), 1e-30)
+        coded = jnp.round(total * (CODE_TOP / top))
+        coded_ref[:, here] = coded.astype(jnp.int32).astype(coded_ref.dtype)
+        step_ref[place : place + 1, :] = jnp.broadcast_to(
+            top * (1.0 / CODE_TOP), (1, step_ref.shape[1])
+        )
 
 
 def join_coded(partial, pooled, w):
@@ -380,12 +389,16 @@
 
 def second_kernel(w_ref, preact_ref, *refs):
     *received_refs, out_ref = refs
-    preact = preact_ref[...]
-    for coded_ref, step_ref in zip(received_refs[::2], received_refs[1::2]):
-        coded = coded_ref[...].astype(jnp.int32).astype(jnp.float32)
-        preact = preact + coded * step_ref[0:1, 0:1]
-    hidden = jnp.maximum(preact, 0.0).astype(jnp.bfloat16)
-    out_ref[...] = multiply(hidden, w_ref[...]).astype(out_ref.dtype)
+    outputs = None
+    for place, here in enumerate(code_chunks(preact_ref.shape[1])):
+        preact = preact_ref[:, here]
+        for coded_ref, step_ref in zip(received_refs[::2], received_refs[1::2]):
+            coded = coded_ref[:, here].astype(jnp.int32).astype(jnp.float32)
+            preact = preact + coded * step_ref[place : place + 1, 0:1]
+        hidden = jnp.maximum(preact, 0.0).astype(jnp.bfloat16)
+        part = multiply(hidden, w_ref[here, :])
+        outputs = part if outputs is None else outputs + part
+    out_ref[...] = outputs.astype(out_ref.dtype)
 
 
 def second_layer(w, preact, received):

time: 27.4 us -> 27.4 us (level)
  no operation moved by 1% of the time
where the time goes in v6:
time: 27.4 us; the launch traced here: 27.2 us
  starting transfers between devices  10.5 us (38%)
  waiting for transfers between devices  8.59 us (31%)
  Pallas kernels  7.97 us (29%)
    ppermute x4, starting transfers between devices, exchange(): lax.ppermute(part, 'tower', [(i, i ^ k * low) for i in range(towers)])  6.7 us
    ppermute x4, waiting for transfers between devices, exchange(): lax.ppermute(part, 'tower', [(i, i ^ k * low) for i in range(towers)])  4.74 us
    ppermute x1, starting transfers between devices, on_device(): lax.ppermute(block, 'dev', onward)  2.73 us
    ppermute x1, waiting for transfers between devices, on_device(): lax.ppermute(step, 'dev', onward)  2.52 us
    pallas_call x1, Pallas kernels, first_pool(): pl.pallas_call(lambda *refs: first_kernel(blocks, *refs), out_shape=(jax....  1.9 us
    pallas_call x1, Pallas kernels, home_late(): pl.pallas_call(late_kernel, out_shape=home_shapes(order, ids, tables, w),...  1.63 us
    ppermute x3, waiting for transfers between devices, swap_cores(): return lax.ppermute(array, 'dev', [(i, i ^ 1) for i in range(devices)])  1.32 us
    pallas_call x1, Pallas kernels, fetch_head(): pl.pallas_call(fetch_kernel, out_shape=(like(head), like(interact)), in_s...  1.3 us
  transfers between devices with their start and end apart: 9, of which 7 were waited for; matrix products, arithmetic and copies ran while one was open for 0% of the time, Pallas kernels for 23%

profile of v6, /device:TPU:0, one launch (start us, length us, event | category | flops | bytes accessed | tf_op | source)
XLA Modules:
  0.0 27.2 jit_solution(9011574107444787488)
XLA Ops:
  0.0 0.5 %collective-permute-start.1 = (bf16[512,1024]{1,0:T(8,128)(2,1)}, bf16[512,1024]{1,0:T(8,128)(2,1)S(1)}, u32[]{:S(2)}, u32[]{:S(2)}) collective-permute-start(bf16[512,1024]{1,0:T(8,128)(2,1)} %bitcast.29), channel_id=1, source_target_pairs={{0,1},{1,0},{2,3},{3,2},{4,5},{5,4},{6,7},{7,6},{8,9},{9,8},{10,11... | collective-permute-start | bytes 3145736 | tf_op jit(solution)/shard_map/ppermute | solution.py:528
  0.5 1.9 %first_pool.1 = (bf16[128,512]{1,0:T(8,128)(2,1)S(1)}, s32[4,128]{1,0:T(4,128)S(1)}, s32[4,32,512]{2,1,0:T(8,128)S(1)}, bf16[4,512,128]{2,1,0:T(8,128)(2,1)S(1)}...) custom-call(s32[4,128]{1,0:T(4,128)} %bitcast.34, s32[4,32,512]{2,1,0:T(8,128)} %bitcast.32, ...), custom_call_target="tpu_custom_call" | custom-call | flops 1 | bytes 1 | tf_op jit(solution)/shard_map/first_pool/pallas_call | solution.py:265
  2.4 0.1 collective-permute-start
  2.5 0.9 %away_layer.1.partial_ref = f32[128,1024]{1,0:T(8,128)S(1)} custom-call(s32[1,128,128]{2,1,0:T(8,128)S(1)} %get-tuple-element.30.residues_ref, s32[1,128,128]{2,1,0:T(8,128)S(1)} %get-tuple-element.31.weights_ref, bf16[4,512,128]{2,1,0:T(8,128)(2,1)S(1)} %get-tuple-element.28.tables_ref, bf16[512,1024]{1,0:T(8,128)(2,1)S(1)} %get-tuple-element.29.w_ref), custom_call_target="tpu_custom_call" | custom-call | flops 1 | bytes 1 | tf_op jit(solution)/shard_map/away_layer/pallas_call | solution.py:281
  3.4 0.4 %collective-permute-done.pooled_ref = bf16[128,512]{1,0:T(8,128)(2,1)S(1)} collective-permute-done((bf16[128,512]{1,0:T(8,128)(2,1)S(1)}, bf16[128,512]{1,0:T(8,128)(2,1)S(1)}, u32[]{:S(2)}, u32[]{:S(2)}) %collective-permute-start) | collective-permute-done | bytes 131104 | tf_op jit(solution)/shard_map/ppermute | solution.py:528
  3.8 0.0 collective-permute-done.1.w_ref
  3.8 0.5 %join_coded.1 = (s16[128,1024]{1,0:T(8,128)(2,1)S(1)}, f32[8,128]{1,0:T(8,128)S(1)}) custom-call(f32[128,1024]{1,0:T(8,128)S(1)} %away_layer.1.partial_ref, bf16[128,512]{1,0:T(8,128)(2,1)S(1)} %collective-permute-done.pooled_ref, bf16[512,1024]{1,0:T(8,128)(2,1)S(1)} %collective-permute-done.1.w_ref), custom_call_target="tpu_custom_call" | custom-call | flops 1 | bytes 1 | tf_op jit(solution)/shard_map/join_coded/pallas_call | solution.py:377
  4.3 2.7 %collective-permute-start.3 = (s16[128,1024]{1,0:T(8,128)(2,1)S(1)}, s16[128,1024]{1,0:T(8,128)(2,1)S(1)}, u32[]{:S(2)}, u32[]{:S(2)}) collective-permute-start(s16[128,1024]{1,0:T(8,128)(2,1)S(1)} %get-tuple-element.37.after_hbm), channel_id=1, source_target_pairs={{0,2},{1,3},{2,0},{3,1},{4,6},{5,7},{6,4},{7,5},{8,10},{9,11},{10,... | collective-permute-start | bytes 786440 | tf_op jit(solution)/shard_map/ppermute | solution.py:543
  7.0 1.6 %home_late.1 = (bf16[128,512]{1,0:T(8,128)(2,1)S(1)}, f32[128,1024]{1,0:T(8,128)S(1)}) custom-call(s32[4,128]{1,0:T(4,128)S(1)} %get-tuple-element.26.order_ref, s32[4,32,512]{2,1,0:T(8,128)S(1)} %get-tuple-element.27.ids_ref, bf16[4,512,128]{2,1,0:T(8,128)(2,1)S(1)} %get-tuple-element.28.tables_ref, bf16[512,1024]{1,0:T(8,128)(2,1)S(1)} %get-tuple-element.29.w_ref, ...), custom_call_target="tpu_custom_call" | custom-call | flops 1 | bytes 1 | tf_op jit(solution)/shard_map/home_late/pallas_call | solution.py:312
  8.7 0.2 collective-permute-start.2
  8.9 0.3 %collective-permute-start.4 = (f32[8,128]{1,0:T(8,128)S(1)}, f32[8,128]{1,0:T(8,128)S(1)}, u32[]{:S(2)}, u32[]{:S(2)}) collective-permute-start(f32[8,128]{1,0:T(8,128)S(1)} %get-tuple-element.40), channel_id=1, source_target_pairs={{0,2},{1,3},{2,0},{3,1},{4,6},{5,7},{6,4},{7,5},{8,10},{9,11},{10,... | collective-permute-start | bytes 12296 | tf_op jit(solution)/shard_map/ppermute | solution.py:543
  9.2 0.9 %collective-permute-done.2.pooled_ref = bf16[128,512]{1,0:T(8,128)(2,1)S(1)} collective-permute-done((bf16[128,512]{1,0:T(8,128)(2,1)S(1)}, bf16[128,512]{1,0:T(8,128)(2,1)S(1)}, u32[]{:S(2)}, u32[]{:S(2)}) %collective-permute-start.2) | collective-permute-done | bytes 131104 | tf_op jit(solution)/shard_map/ppermute | solution.py:528
  10.1 0.0 copy-start
  10.1 0.3 %join.1.preact_ref.after_hbm = f32[128,1024]{1,0:T(8,128)S(1)} custom-call(f32[128,1024]{1,0:T(8,128)S(1)} %get-tuple-element.38.partial_ref, bf16[128,512]{1,0:T(8,128)(2,1)S(1)} %collective-permute-done.2.pooled_ref, bf16[512,1024]{1,0:T(8,128)(2,1)S(1)} %collective-permute-done.1.w_ref), custom_call_target="tpu_custom_call" | custom-call | flops 1 | bytes 1 | tf_op jit(solution)/shard_map/join/pallas_call | solution.py:349
  10.4 2.5 %collective-permute-done.4.refs_1_ = f32[8,128]{1,0:T(8,128)S(1)} collective-permute-done((f32[8,128]{1,0:T(8,128)S(1)}, f32[8,128]{1,0:T(8,128)S(1)}, u32[]{:S(2)}, u32[]{:S(2)}) %collective-permute-start.4) | collective-permute-done | bytes 4128 | tf_op jit(solution)/shard_map/ppermute | solution.py:543
  13.0 0.0 collective-permute-done.3.refs_0_
  13.0 0.0 copy-done
  13.0 0.3 %second_layer.1 = bf16[128,512]{1,0:T(8,128)(2,1)S(1)} custom-call(bf16[1024,512]{1,0:T(8,128)(2,1)S(1)} %bitcast.25, f32[128,1024]{1,0:T(8,128)S(1)} %join.1.preact_ref.after_hbm, s16[128,1024]{1,0:T(8,128)(2,1)S(1)} %collective-permute-done.3.refs_0_, f32[8,128]{1,0:T(8,128)S(1)} %collective-permute-done.4.refs_1_), custom_call_target="tpu_custom_call" | custom-call | flops 1 | bytes 1 | tf_op jit(solution)/shard_map/second_layer/pallas_call | solution.py:405
  13.3 3.4 %collective-permute-start.5 = (bf16[2,16,512]{2,1,0:T(8,128)(2,1)S(1)}, bf16[2,16,512]{2,1,0:T(8,128)(2,1)S(1)}, u32[]{:S(2)}, u32[]{:S(2)}) collective-permute-start(bf16[2,16,512]{2,1,0:T(8,128)(2,1)S(1)} %pieces.4.refs_1_), channel_id=1, source_target_pairs={{0,12},{4,8},{8,4},{12,0},{16,28},{20,24},{24,20},{28,16},{1,13},{... | collective-permute-start | bytes 98312 | tf_op jit(solution)/shard_map/ppermute | solution.py:507
  16.7 0.4 %collective-permute-start.6 = (bf16[2,16,512]{2,1,0:T(8,128)(2,1)S(1)}, bf16[2,16,512]{2,1,0:T(8,128)(2,1)S(1)}, u32[]{:S(2)}, u32[]{:S(2)}) collective-permute-start(bf16[2,16,512]{2,1,0:T(8,128)(2,1)S(1)} %pieces.5.refs_1_), channel_id=1, source_target_pairs={{0,8},{4,12},{8,0},{12,4},{16,24},{20,28},{24,16},{28,20},{1,9},{5... | collective-permute-start | bytes 98312 | tf_op jit(solution)/shard_map/ppermute | solution.py:507
  17.2 0.2 collective-permute-start.7
  17.4 1.4 %collective-permute-done.5 = bf16[2,16,512]{2,1,0:T(8,128)(2,1)S(1)} collective-permute-done((bf16[2,16,512]{2,1,0:T(8,128)(2,1)S(1)}, bf16[2,16,512]{2,1,0:T(8,128)(2,1)S(1)}, u32[]{:S(2)}, u32[]{:S(2)}) %collective-permute-start.5) | collective-permute-done | bytes 32800 | tf_op jit(solution)/shard_map/ppermute | solution.py:507
  18.8 1.8 %collective-permute-done.6 = bf16[2,16,512]{2,1,0:T(8,128)(2,1)S(1)} collective-permute-done((bf16[2,16,512]{2,1,0:T(8,128)(2,1)S(1)}, bf16[2,16,512]{2,1,0:T(8,128)(2,1)S(1)}, u32[]{:S(2)}, u32[]{:S(2)}) %collective-permute-start.6) | collective-permute-done | bytes 32800 | tf_op jit(solution)/shard_map/ppermute | solution.py:507
  20.6 0.5 %collective-permute-done.7 = bf16[2,16,512]{2,1,0:T(8,128)(2,1)S(1)} collective-permute-done((bf16[2,16,512]{2,1,0:T(8,128)(2,1)S(1)}, bf16[2,16,512]{2,1,0:T(8,128)(2,1)S(1)}, u32[]{:S(2)}, u32[]{:S(2)}) %collective-permute-start.7) | collective-permute-done | bytes 32800 | tf_op jit(solution)/shard_map/ppermute | solution.py:507
  21.1 2.7 %collective-permute-start.8 = (bf16[1,64,512]{2,1,0:T(8,128)(2,1)S(1)}, bf16[1,64,512]{2,1,0:T(8,128)(2,1)S(1)}, u32[]{:S(2)}, u32[]{:S(2)}) collective-permute-start(bf16[1,64,512]{2,1,0:T(8,128)(2,1)S(1)} %get-tuple-element.46), channel_id=1, source_target_pairs={{0,16},{4,20},{8,24},{12,28},{16,0},{20,4},{24,8},{28,12},{1,17},{... | collective-permute-start | bytes 196616 | tf_op jit(solution)/shard_map/ppermute | solution.py:507
  23.8 1.3 %fetch_head.1 = (bf16[4096,128]{1,0:T(8,128)(2,1)S(1)}, f32[64,128]{1,0:T(8,128)S(1)}) custom-call(bf16[4096,128]{1,0:T(8,128)(2,1)} %head_hbm.1, f32[64,128]{1,0:T(8,128)} %interact_hbm.1, f32[128,1024]{1,0:T(8,128)S(1)} %join.1.preact_ref.after_hbm), custom_call_target="tpu_custom_call" | custom-call | flops 1 | bytes 1 | tf_op jit(solution)/shard_map/fetch_head/pallas_call | solution.py:333
  25.1 0.2 score.2.refs_0_
  25.3 1.1 %collective-permute-done.8 = bf16[1,64,512]{2,1,0:T(8,128)(2,1)S(1)} collective-permute-done((bf16[1,64,512]{2,1,0:T(8,128)(2,1)S(1)}, bf16[1,64,512]{2,1,0:T(8,128)(2,1)S(1)}, u32[]{:S(2)}, u32[]{:S(2)}) %collective-permute-start.8) | collective-permute-done | bytes 65568 | tf_op jit(solution)/shard_map/ppermute | solution.py:507
  26.4 0.8 %score.3 = f32[16,128]{1,0:T(8,128)} custom-call(f32[16,128]{1,0:T(8,128)S(1)} %score.2.refs_0_, bf16[64,512]{1,0:T(8,128)(2,1)S(1)} %bitcast.27, bf16[64,512]{1,0:T(8,128)(2,1)S(1)} %bitcast.28, bf16[4096,128]{1,0:T(8,128)(2,1)S(1)} %get-tuple-element.44.refs_1_.refs_3_, f32[64,128]{1,0:T(8,128)S(1)} %get-tuple-element.45.refs_2_.refs_4_), custom_call_target="tpu_custom_call" | custom-call | flops 1 | bytes 1 | tf_op jit(solution)/shard_map/score/pallas_call | solution.py:462
  (10 shorter events, 0.1 us)
Async XLA Ops:
  0.0 3.8 %collective-permute-start.1 = (bf16[512,1024]{1,0:T(8,128)(2,1)}, bf16[512,1024]{1,0:T(8,128)(2,1)S(1)}, u32[]{:S(2)}, u32[]{:S(2)}) collective-permute-start(bf16[512,1024]{1,0:T(8,128)(2,1)} %bitcast.29), channel_id=1, source_target_pairs={{0,1},{1,0},{2,3},{3,2},{4,5},{5,4},{6,7},{7,6},{8,9},{9,8},{10,11... | collective-permute-start | bytes 3145736 | tf_op jit(solution)/shard_map/ppermute | solution.py:528
  2.4 1.4 %collective-permute-start = (bf16[128,512]{1,0:T(8,128)(2,1)S(1)}, bf16[128,512]{1,0:T(8,128)(2,1)S(1)}, u32[]{:S(2)}, u32[]{:S(2)}) collective-permute-start(bf16[128,512]{1,0:T(8,128)(2,1)S(1)} %get-tuple-element.32), channel_id=1, source_target_pairs={{0,1},{1,0},{2,3},{3,2},{4,5},{5,4},{6,7},{7,6},{8,9},{9,8},{10,11... | collective-permute-start | bytes 393224 | tf_op jit(solution)/shard_map/ppermute | solution.py:528
  4.3 8.6 %collective-permute-start.3 = (s16[128,1024]{1,0:T(8,128)(2,1)S(1)}, s16[128,1024]{1,0:T(8,128)(2,1)S(1)}, u32[]{:S(2)}, u32[]{:S(2)}) collective-permute-start(s16[128,1024]{1,0:T(8,128)(2,1)S(1)} %get-tuple-element.37.after_hbm), channel_id=1, source_target_pairs={{0,2},{1,3},{2,0},{3,1},{4,6},{5,7},{6,4},{7,5},{8,10},{9,11},{10,... | collective-permute-start | bytes 786440 | tf_op jit(solution)/shard_map/ppermute | solution.py:543
  8.7 1.4 %collective-permute-start.2 = (bf16[128,512]{1,0:T(8,128)(2,1)S(1)}, bf16[128,512]{1,0:T(8,128)(2,1)S(1)}, u32[]{:S(2)}, u32[]{:S(2)}) collective-permute-start(bf16[128,512]{1,0:T(8,128)(2,1)S(1)} %get-tuple-element.39), channel_id=1, source_target_pairs={{0,1},{1,0},{2,3},{3,2},{4,5},{5,4},{6,7},{7,6},{8,9},{9,8},{10,11... | collective-permute-start | bytes 393224 | tf_op jit(solution)/shard_map/ppermute | solution.py:528
  8.9 4.1 %collective-permute-start.4 = (f32[8,128]{1,0:T(8,128)S(1)}, f32[8,128]{1,0:T(8,128)S(1)}, u32[]{:S(2)}, u32[]{:S(2)}) collective-permute-start(f32[8,128]{1,0:T(8,128)S(1)} %get-tuple-element.40), channel_id=1, source_target_pairs={{0,2},{1,3},{2,0},{3,1},{4,6},{5,7},{6,4},{7,5},{8,10},{9,11},{10,... | collective-permute-start | bytes 12296 | tf_op jit(solution)/shard_map/ppermute | solution.py:543
  10.1 2.9 %copy-start = (bf16[1,1024,512]{2,1,0:T(8,128)(2,1)S(1)}, bf16[1,1024,512]{2,1,0:T(8,128)(2,1)}, u32[]{:S(2)}) copy-start(bf16[1,1024,512]{2,1,0:T(8,128)(2,1)} %param.11) | copy-start | bytes 3145732
  13.3 5.5 %collective-permute-start.5 = (bf16[2,16,512]{2,1,0:T(8,128)(2,1)S(1)}, bf16[2,16,512]{2,1,0:T(8,128)(2,1)S(1)}, u32[]{:S(2)}, u32[]{:S(2)}) collective-permute-start(bf16[2,16,512]{2,1,0:T(8,128)(2,1)S(1)} %pieces.4.refs_1_), channel_id=1, source_target_pairs={{0,12},{4,8},{8,4},{12,0},{16,28},{20,24},{24,20},{28,16},{1,13},{... | collective-permute-start | bytes 98312 | tf_op jit(solution)/shard_map/ppermute | solution.py:507
  16.7 3.9 %collective-permute-start.6 = (bf16[2,16,512]{2,1,0:T(8,128)(2,1)S(1)}, bf16[2,16,512]{2,1,0:T(8,128)(2,1)S(1)}, u32[]{:S(2)}, u32[]{:S(2)}) collective-permute-start(bf16[2,16,512]{2,1,0:T(8,128)(2,1)S(1)} %pieces.5.refs_1_), channel_id=1, source_target_pairs={{0,8},{4,12},{8,0},{12,4},{16,24},{20,28},{24,16},{28,20},{1,9},{5... | collective-permute-start | bytes 98312 | tf_op jit(solution)/shard_map/ppermute | solution.py:507
  17.2 3.9 %collective-permute-start.7 = (bf16[2,16,512]{2,1,0:T(8,128)(2,1)S(1)}, bf16[2,16,512]{2,1,0:T(8,128)(2,1)S(1)}, u32[]{:S(2)}, u32[]{:S(2)}) collective-permute-start(bf16[2,16,512]{2,1,0:T(8,128)(2,1)S(1)} %get-tuple-element.41), channel_id=1, source_target_pairs={{0,4},{4,0},{8,12},{12,8},{16,20},{20,16},{24,28},{28,24},{1,5},{5... | collective-permute-start | bytes 98312 | tf_op jit(solution)/shard_map/ppermute | solution.py:507
  21.1 5.2 %collective-permute-start.8 = (bf16[1,64,512]{2,1,0:T(8,128)(2,1)S(1)}, bf16[1,64,512]{2,1,0:T(8,128)(2,1)S(1)}, u32[]{:S(2)}, u32[]{:S(2)}) collective-permute-start(bf16[1,64,512]{2,1,0:T(8,128)(2,1)S(1)} %get-tuple-element.46), channel_id=1, source_target_pairs={{0,16},{4,20},{8,24},{12,28},{16,0},{20,4},{24,8},{28,12},{1,17},{... | collective-permute-start | bytes 196616 | tf_op jit(solution)/shard_map/ppermute | solution.py:507

commit v7 on v6

--- a/solution.py
+++ b/solution.py
@@ -488,7 +488,7 @@
     )(held, after)
 
 
-def exchange(blocks):
+def exchange(blocks, after):
     towers, rows, width = blocks.shape
     assert towers & (towers - 1) == 0
     held, masks = blocks, (0,)
@@ -497,7 +497,6 @@
         group = min(4, towers // low)
         split = held.reshape(held.shape[0] // group, group, *held.shape[1:])
         parts = [None] * group
-        after = split
         for k in range(group - 1, 0, -1):
             if k > 1:
                 (after,) = pieces(split, low, (k,), after)
@@ -545,7 +544,7 @@
     preact = join(preact, swap_cores(pooled), w_other)
     w_head, w_interact = fetch_head(w_head, w_interact, preact)
     outputs = second_layer(w_second[0], preact, received)
-    held, masks = exchange(outputs.reshape(towers, my_rows // towers, outputs.shape[1]))
+    held, masks = exchange(outputs.reshape(towers, my_rows // towers, outputs.shape[1]), w_head)
     so_far = score(held[:1], masks[:1], w_head, w_interact, towers)
     return score(held, masks, w_head, w_interact, towers, so_far)[None]
 

time: 27.4 us -> 27.4 us (level)
    ppermute x1, waiting for transfers between devices: 2.52 us -> 1.13 us  [on_device(): lax.ppermute(step, 'dev', onward)]
    ppermute x4, waiting for transfers between devices: 4.74 us -> 6.05 us  [exchange(): lax.ppermute(part, 'tower', [(i, i ^ k * low) for i in range(towers)])]
where the time goes in v7:
time: 27.4 us; the launch traced here: 27.2 us
  starting transfers between devices  10.5 us (38%)
  waiting for transfers between devices  8.5 us (31%)
  Pallas kernels  8.03 us (29%)
    ppermute x4, starting transfers between devices, exchange(): lax.ppermute(part, 'tower', [(i, i ^ k * low) for i in range(towers)])  6.71 us
    ppermute x4, waiting for transfers between devices, exchange(): lax.ppermute(part, 'tower', [(i, i ^ k * low) for i in range(towers)])  6.05 us
    ppermute x1, starting transfers between devices, on_device(): lax.ppermute(block, 'dev', onward)  2.73 us
    pallas_call x1, Pallas kernels, first_pool(): pl.pallas_call(lambda *refs: first_kernel(blocks, *refs), out_shape=(jax....  1.9 us
    pallas_call x1, Pallas kernels, home_late(): pl.pallas_call(late_kernel, out_shape=home_shapes(order, ids, tables, w),...  1.63 us
    pallas_call x1, Pallas kernels, fetch_head(): pl.pallas_call(fetch_kernel, out_shape=(like(head), like(interact)), in_s...  1.38 us
    ppermute x3, waiting for transfers between devices, swap_cores(): return lax.ppermute(array, 'dev', [(i, i ^ 1) for i in range(devices)])  1.32 us
    ppermute x1, waiting for transfers between devices, on_device(): lax.ppermute(step, 'dev', onward)  1.13 us
  transfers between devices with their start and end apart: 9, of which 7 were waited for; matrix products, arithmetic and copies ran while one was open for 0% of the time, Pallas kernels for 23%

profile of v7, /device:TPU:0, one launch (start us, length us, event | category | flops | bytes accessed | tf_op | source)
XLA Modules:
  0.0 27.2 jit_solution(1658762062226003668)
XLA Ops:
  0.0 0.5 %collective-permute-start.1 = (bf16[512,1024]{1,0:T(8,128)(2,1)}, bf16[512,1024]{1,0:T(8,128)(2,1)S(1)}, u32[]{:S(2)}, u32[]{:S(2)}) collective-permute-start(bf16[512,1024]{1,0:T(8,128)(2,1)} %bitcast.27), channel_id=1, source_target_pairs={{0,1},{1,0},{2,3},{3,2},{4,5},{5,4},{6,7},{7,6},{8,9},{9,8},{10,11... | collective-permute-start | bytes 3145736 | tf_op jit(solution)/shard_map/ppermute | solution.py:527
  0.5 1.9 %first_pool.1 = (bf16[128,512]{1,0:T(8,128)(2,1)S(1)}, s32[4,128]{1,0:T(4,128)S(1)}, s32[4,32,512]{2,1,0:T(8,128)S(1)}, bf16[4,512,128]{2,1,0:T(8,128)(2,1)S(1)}...) custom-call(s32[4,128]{1,0:T(4,128)} %bitcast.32, s32[4,32,512]{2,1,0:T(8,128)} %bitcast.30, ...), custom_call_target="tpu_custom_call" | custom-call | flops 1 | bytes 1 | tf_op jit(solution)/shard_map/first_pool/pallas_call | solution.py:265
  2.4 0.1 collective-permute-start
  2.5 0.9 %away_layer.1.partial_ref = f32[128,1024]{1,0:T(8,128)S(1)} custom-call(s32[1,128,128]{2,1,0:T(8,128)S(1)} %get-tuple-element.30.residues_ref, s32[1,128,128]{2,1,0:T(8,128)S(1)} %get-tuple-element.31.weights_ref, bf16[4,512,128]{2,1,0:T(8,128)(2,1)S(1)} %get-tuple-element.28.tables_ref, bf16[512,1024]{1,0:T(8,128)(2,1)S(1)} %get-tuple-element.29.w_ref), custom_call_target="tpu_custom_call" | custom-call | flops 1 | bytes 1 | tf_op jit(solution)/shard_map/away_layer/pallas_call | solution.py:281
  3.4 0.4 %collective-permute-done.pooled_ref = bf16[128,512]{1,0:T(8,128)(2,1)S(1)} collective-permute-done((bf16[128,512]{1,0:T(8,128)(2,1)S(1)}, bf16[128,512]{1,0:T(8,128)(2,1)S(1)}, u32[]{:S(2)}, u32[]{:S(2)}) %collective-permute-start) | collective-permute-done | bytes 131104 | tf_op jit(solution)/shard_map/ppermute | solution.py:527
  3.8 0.0 collective-permute-done.1.w_ref
  3.8 0.5 %join_coded.1 = (s16[128,1024]{1,0:T(8,128)(2,1)S(1)}, f32[8,128]{1,0:T(8,128)S(1)}) custom-call(f32[128,1024]{1,0:T(8,128)S(1)} %away_layer.1.partial_ref, bf16[128,512]{1,0:T(8,128)(2,1)S(1)} %collective-permute-done.pooled_ref, bf16[512,1024]{1,0:T(8,128)(2,1)S(1)} %collective-permute-done.1.w_ref), custom_call_target="tpu_custom_call" | custom-call | flops 1 | bytes 1 | tf_op jit(solution)/shard_map/join_coded/pallas_call | solution.py:377
  4.3 2.7 %collective-permute-start.3 = (s16[128,1024]{1,0:T(8,128)(2,1)S(1)}, s16[128,1024]{1,0:T(8,128)(2,1)S(1)}, u32[]{:S(2)}, u32[]{:S(2)}) collective-permute-start(s16[128,1024]{1,0:T(8,128)(2,1)S(1)} %get-tuple-element.37.after_hbm), channel_id=1, source_target_pairs={{0,2},{1,3},{2,0},{3,1},{4,6},{5,7},{6,4},{7,5},{8,10},{9,11},{10,... | collective-permute-start | bytes 786440 | tf_op jit(solution)/shard_map/ppermute | solution.py:542
  7.0 1.6 %home_late.1 = (bf16[128,512]{1,0:T(8,128)(2,1)S(1)}, f32[128,1024]{1,0:T(8,128)S(1)}) custom-call(s32[4,128]{1,0:T(4,128)S(1)} %get-tuple-element.26.order_ref, s32[4,32,512]{2,1,0:T(8,128)S(1)} %get-tuple-element.27.ids_ref, bf16[4,512,128]{2,1,0:T(8,128)(2,1)S(1)} %get-tuple-element.28.tables_ref, bf16[512,1024]{1,0:T(8,128)(2,1)S(1)} %get-tuple-element.29.w_ref, ...), custom_call_target="tpu_custom_call" | custom-call | flops 1 | bytes 1 | tf_op jit(solution)/shard_map/home_late/pallas_call | solution.py:312
  8.7 0.2 collective-permute-start.2
  8.9 0.3 %collective-permute-start.4 = (f32[8,128]{1,0:T(8,128)S(1)}, f32[8,128]{1,0:T(8,128)S(1)}, u32[]{:S(2)}, u32[]{:S(2)}) collective-permute-start(f32[8,128]{1,0:T(8,128)S(1)} %get-tuple-element.40), channel_id=1, source_target_pairs={{0,2},{1,3},{2,0},{3,1},{4,6},{5,7},{6,4},{7,5},{8,10},{9,11},{10,... | collective-permute-start | bytes 12296 | tf_op jit(solution)/shard_map/ppermute | solution.py:542
  9.2 0.9 %collective-permute-done.2.pooled_ref = bf16[128,512]{1,0:T(8,128)(2,1)S(1)} collective-permute-done((bf16[128,512]{1,0:T(8,128)(2,1)S(1)}, bf16[128,512]{1,0:T(8,128)(2,1)S(1)}, u32[]{:S(2)}, u32[]{:S(2)}) %collective-permute-start.2) | collective-permute-done | bytes 131104 | tf_op jit(solution)/shard_map/ppermute | solution.py:527
  10.1 0.3 %join.1.preact_ref.after_hbm = f32[128,1024]{1,0:T(8,128)S(1)} custom-call(f32[128,1024]{1,0:T(8,128)S(1)} %get-tuple-element.38.partial_ref, bf16[128,512]{1,0:T(8,128)(2,1)S(1)} %collective-permute-done.2.pooled_ref, bf16[512,1024]{1,0:T(8,128)(2,1)S(1)} %collective-permute-done.1.w_ref), custom_call_target="tpu_custom_call" | custom-call | flops 1 | bytes 1 | tf_op jit(solution)/shard_map/join/pallas_call | solution.py:349
  10.4 0.0 copy-start
  10.4 1.4 %fetch_head.1 = (bf16[4096,128]{1,0:T(8,128)(2,1)S(1)}, f32[64,128]{1,0:T(8,128)S(1)}) custom-call(bf16[4096,128]{1,0:T(8,128)(2,1)} %head_hbm.1, f32[64,128]{1,0:T(8,128)} %interact_hbm.1, f32[128,1024]{1,0:T(8,128)S(1)} %join.1.preact_ref.after_hbm), custom_call_target="tpu_custom_call" | custom-call | flops 1 | bytes 1 | tf_op jit(solution)/shard_map/fetch_head/pallas_call | solution.py:333
  11.8 1.1 %collective-permute-done.4.refs_1_ = f32[8,128]{1,0:T(8,128)S(1)} collective-permute-done((f32[8,128]{1,0:T(8,128)S(1)}, f32[8,128]{1,0:T(8,128)S(1)}, u32[]{:S(2)}, u32[]{:S(2)}) %collective-permute-start.4) | collective-permute-done | bytes 4128 | tf_op jit(solution)/shard_map/ppermute | solution.py:542
  12.9 0.0 collective-permute-done.3.refs_0_
  13.0 0.0 copy-done
  13.0 0.3 %second_layer.1 = bf16[128,512]{1,0:T(8,128)(2,1)S(1)} custom-call(bf16[1024,512]{1,0:T(8,128)(2,1)S(1)} %bitcast.22, f32[128,1024]{1,0:T(8,128)S(1)} %join.1.preact_ref.after_hbm, s16[128,1024]{1,0:T(8,128)(2,1)S(1)} %collective-permute-done.3.refs_0_, f32[8,128]{1,0:T(8,128)S(1)} %collective-permute-done.4.refs_1_), custom_call_target="tpu_custom_call" | custom-call | flops 1 | bytes 1 | tf_op jit(solution)/shard_map/second_layer/pallas_call | solution.py:405
  13.3 3.4 %collective-permute-start.5 = (bf16[2,16,512]{2,1,0:T(8,128)(2,1)S(1)}, bf16[2,16,512]{2,1,0:T(8,128)(2,1)S(1)}, u32[]{:S(2)}, u32[]{:S(2)}) collective-permute-start(bf16[2,16,512]{2,1,0:T(8,128)(2,1)S(1)} %pieces.4.refs_1_), channel_id=1, source_target_pairs={{0,12},{4,8},{8,4},{12,0},{16,28},{20,24},{24,20},{28,16},{1,13},{... | collective-permute-start | bytes 98312 | tf_op jit(solution)/shard_map/ppermute | solution.py:506
  16.7 0.4 %collective-permute-start.6 = (bf16[2,16,512]{2,1,0:T(8,128)(2,1)S(1)}, bf16[2,16,512]{2,1,0:T(8,128)(2,1)S(1)}, u32[]{:S(2)}, u32[]{:S(2)}) collective-permute-start(bf16[2,16,512]{2,1,0:T(8,128)(2,1)S(1)} %pieces.5.refs_1_), channel_id=1, source_target_pairs={{0,8},{4,12},{8,0},{12,4},{16,24},{20,28},{24,16},{28,20},{1,9},{5... | collective-permute-start | bytes 98312 | tf_op jit(solution)/shard_map/ppermute | solution.py:506
  17.2 0.2 collective-permute-start.7
  17.4 1.4 %collective-permute-done.5 = bf16[2,16,512]{2,1,0:T(8,128)(2,1)S(1)} collective-permute-done((bf16[2,16,512]{2,1,0:T(8,128)(2,1)S(1)}, bf16[2,16,512]{2,1,0:T(8,128)(2,1)S(1)}, u32[]{:S(2)}, u32[]{:S(2)}) %collective-permute-start.5) | collective-permute-done | bytes 32800 | tf_op jit(solution)/shard_map/ppermute | solution.py:506
  18.8 1.8 %collective-permute-done.6 = bf16[2,16,512]{2,1,0:T(8,128)(2,1)S(1)} collective-permute-done((bf16[2,16,512]{2,1,0:T(8,128)(2,1)S(1)}, bf16[2,16,512]{2,1,0:T(8,128)(2,1)S(1)}, u32[]{:S(2)}, u32[]{:S(2)}) %collective-permute-start.6) | collective-permute-done | bytes 32800 | tf_op jit(solution)/shard_map/ppermute | solution.py:506
  20.6 0.4 %collective-permute-done.7 = bf16[2,16,512]{2,1,0:T(8,128)(2,1)S(1)} collective-permute-done((bf16[2,16,512]{2,1,0:T(8,128)(2,1)S(1)}, bf16[2,16,512]{2,1,0:T(8,128)(2,1)S(1)}, u32[]{:S(2)}, u32[]{:S(2)}) %collective-permute-start.7) | collective-permute-done | bytes 32800 | tf_op jit(solution)/shard_map/ppermute | solution.py:506
  21.1 2.7 %collective-permute-start.8 = (bf16[1,64,512]{2,1,0:T(8,128)(2,1)S(1)}, bf16[1,64,512]{2,1,0:T(8,128)(2,1)S(1)}, u32[]{:S(2)}, u32[]{:S(2)}) collective-permute-start(bf16[1,64,512]{2,1,0:T(8,128)(2,1)S(1)} %get-tuple-element.46), channel_id=1, source_target_pairs={{0,16},{4,20},{8,24},{12,28},{16,0},{20,4},{24,8},{28,12},{1,17},{... | collective-permute-start | bytes 196616 | tf_op jit(solution)/shard_map/ppermute | solution.py:506
  23.8 0.2 score.2.refs_0_
  24.0 2.4 %collective-permute-done.8 = bf16[1,64,512]{2,1,0:T(8,128)(2,1)S(1)} collective-permute-done((bf16[1,64,512]{2,1,0:T(8,128)(2,1)S(1)}, bf16[1,64,512]{2,1,0:T(8,128)(2,1)S(1)}, u32[]{:S(2)}, u32[]{:S(2)}) %collective-permute-start.8) | collective-permute-done | bytes 65568 | tf_op jit(solution)/shard_map/ppermute | solution.py:506
  26.4 0.8 %score.3 = f32[16,128]{1,0:T(8,128)} custom-call(f32[16,128]{1,0:T(8,128)S(1)} %score.2.refs_0_, bf16[64,512]{1,0:T(8,128)(2,1)S(1)} %bitcast.25, bf16[64,512]{1,0:T(8,128)(2,1)S(1)} %bitcast.26, bf16[4096,128]{1,0:T(8,128)(2,1)S(1)} %get-tuple-element.41.refs_1_.refs_3_, f32[64,128]{1,0:T(8,128)S(1)} %get-tuple-element.45.refs_2_.refs_4_), custom_call_target="tpu_custom_call" | custom-call | flops 1 | bytes 1 | tf_op jit(solution)/shard_map/score/pallas_call | solution.py:462
  (10 shorter events, 0.1 us)
Async XLA Ops:
  0.0 3.8 %collective-permute-start.1 = (bf16[512,1024]{1,0:T(8,128)(2,1)}, bf16[512,1024]{1,0:T(8,128)(2,1)S(1)}, u32[]{:S(2)}, u32[]{:S(2)}) collective-permute-start(bf16[512,1024]{1,0:T(8,128)(2,1)} %bitcast.27), channel_id=1, source_target_pairs={{0,1},{1,0},{2,3},{3,2},{4,5},{5,4},{6,7},{7,6},{8,9},{9,8},{10,11... | collective-permute-start | bytes 3145736 | tf_op jit(solution)/shard_map/ppermute | solution.py:527
  2.4 1.4 %collective-permute-start = (bf16[128,512]{1,0:T(8,128)(2,1)S(1)}, bf16[128,512]{1,0:T(8,128)(2,1)S(1)}, u32[]{:S(2)}, u32[]{:S(2)}) collective-permute-start(bf16[128,512]{1,0:T(8,128)(2,1)S(1)} %get-tuple-element.32), channel_id=1, source_target_pairs={{0,1},{1,0},{2,3},{3,2},{4,5},{5,4},{6,7},{7,6},{8,9},{9,8},{10,11... | collective-permute-start | bytes 393224 | tf_op jit(solution)/shard_map/ppermute | solution.py:527
  4.3 8.6 %collective-permute-start.3 = (s16[128,1024]{1,0:T(8,128)(2,1)S(1)}, s16[128,1024]{1,0:T(8,128)(2,1)S(1)}, u32[]{:S(2)}, u32[]{:S(2)}) collective-permute-start(s16[128,1024]{1,0:T(8,128)(2,1)S(1)} %get-tuple-element.37.after_hbm), channel_id=1, source_target_pairs={{0,2},{1,3},{2,0},{3,1},{4,6},{5,7},{6,4},{7,5},{8,10},{9,11},{10,... | collective-permute-start | bytes 786440 | tf_op jit(solution)/shard_map/ppermute | solution.py:542
  8.7 1.4 %collective-permute-start.2 = (bf16[128,512]{1,0:T(8,128)(2,1)S(1)}, bf16[128,512]{1,0:T(8,128)(2,1)S(1)}, u32[]{:S(2)}, u32[]{:S(2)}) collective-permute-start(bf16[128,512]{1,0:T(8,128)(2,1)S(1)} %get-tuple-element.39), channel_id=1, source_target_pairs={{0,1},{1,0},{2,3},{3,2},{4,5},{5,4},{6,7},{7,6},{8,9},{9,8},{10,11... | collective-permute-start | bytes 393224 | tf_op jit(solution)/shard_map/ppermute | solution.py:527
  8.9 4.1 %collective-permute-start.4 = (f32[8,128]{1,0:T(8,128)S(1)}, f32[8,128]{1,0:T(8,128)S(1)}, u32[]{:S(2)}, u32[]{:S(2)}) collective-permute-start(f32[8,128]{1,0:T(8,128)S(1)} %get-tuple-element.40), channel_id=1, source_target_pairs={{0,2},{1,3},{2,0},{3,1},{4,6},{5,7},{6,4},{7,5},{8,10},{9,11},{10,... | collective-permute-start | bytes 12296 | tf_op jit(solution)/shard_map/ppermute | solution.py:542
  10.4 2.5 %copy-start = (bf16[1,1024,512]{2,1,0:T(8,128)(2,1)S(1)}, bf16[1,1024,512]{2,1,0:T(8,128)(2,1)}, u32[]{:S(2)}) copy-start(bf16[1,1024,512]{2,1,0:T(8,128)(2,1)} %param.11) | copy-start | bytes 3145732
  13.3 5.5 %collective-permute-start.5 = (bf16[2,16,512]{2,1,0:T(8,128)(2,1)S(1)}, bf16[2,16,512]{2,1,0:T(8,128)(2,1)S(1)}, u32[]{:S(2)}, u32[]{:S(2)}) collective-permute-start(bf16[2,16,512]{2,1,0:T(8,128)(2,1)S(1)} %pieces.4.refs_1_), channel_id=1, source_target_pairs={{0,12},{4,8},{8,4},{12,0},{16,28},{20,24},{24,20},{28,16},{1,13},{... | collective-permute-start | bytes 98312 | tf_op jit(solution)/shard_map/ppermute | solution.py:506
  16.7 3.9 %collective-permute-start.6 = (bf16[2,16,512]{2,1,0:T(8,128)(2,1)S(1)}, bf16[2,16,512]{2,1,0:T(8,128)(2,1)S(1)}, u32[]{:S(2)}, u32[]{:S(2)}) collective-permute-start(bf16[2,16,512]{2,1,0:T(8,128)(2,1)S(1)} %pieces.5.refs_1_), channel_id=1, source_target_pairs={{0,8},{4,12},{8,0},{12,4},{16,24},{20,28},{24,16},{28,20},{1,9},{5... | collective-permute-start | bytes 98312 | tf_op jit(solution)/shard_map/ppermute | solution.py:506
  17.2 3.9 %collective-permute-start.7 = (bf16[2,16,512]{2,1,0:T(8,128)(2,1)S(1)}, bf16[2,16,512]{2,1,0:T(8,128)(2,1)S(1)}, u32[]{:S(2)}, u32[]{:S(2)}) collective-permute-start(bf16[2,16,512]{2,1,0:T(8,128)(2,1)S(1)} %get-tuple-element.42), channel_id=1, source_target_pairs={{0,4},{4,0},{8,12},{12,8},{16,20},{20,16},{24,28},{28,24},{1,5},{5... | collective-permute-start | bytes 98312 | tf_op jit(solution)/shard_map/ppermute | solution.py:506
  21.1 5.2 %collective-permute-start.8 = (bf16[1,64,512]{2,1,0:T(8,128)(2,1)S(1)}, bf16[1,64,512]{2,1,0:T(8,128)(2,1)S(1)}, u32[]{:S(2)}, u32[]{:S(2)}) collective-permute-start(bf16[1,64,512]{2,1,0:T(8,128)(2,1)S(1)} %get-tuple-element.46), channel_id=1, source_target_pairs={{0,16},{4,20},{8,24},{12,28},{16,0},{20,4},{24,8},{28,12},{1,17},{... | collective-permute-start | bytes 196616 | tf_op jit(solution)/shard_map/ppermute | solution.py:506
